TPU v7x, 32 devices: a whole 2x2x4 slice. The times are simulated.
32 devices in a mesh: rep: 16 (over z, y, core), grp: 2 (over x).
Axes of the slice: x: 2, y: 2, z: 4, core: 2. Of those that a mesh axis runs over, the one named last changes fastest.
Arguments:
- clips: bfloat16 [48, 1568, 1024], P('rep', 'grp'), may hold values from -6 to 6
- clip_count: int32 [16], P('rep'), may hold values from 2 to 3, as said below
- cotangent: bfloat16 [48, 1568, 1024], P('rep', 'grp'), may hold values from -6 to 6
- norm_gain: bfloat16 [2, 1024], P(None, 'grp'), may hold values from 0.099609375 to 1.8984375
- bias_d: bfloat16 [6, 1024], P(None, 'grp'), may hold values from -1.1953125 to 1.1953125
- bias_ff: bfloat16 [4096], P('grp'), may hold values from -1.796875 to 1.796875
- w_qkv: bfloat16 [1024, 3072], P('grp'), may hold values from -0.25 to 0.25
- w_o: bfloat16 [1024, 1024], P('grp'), may hold values from -0.5 to 0.5
- w_up: bfloat16 [1024, 4096], P('grp'), may hold values from -0.1875 to 0.1875
- w_down: bfloat16 [4096, 1024], P('grp'), may hold values from -0.09375 to 0.09375
Outputs:
- block_out: bfloat16 [48, 1568, 1024], P('rep', 'grp')
- input_grad: float32 [48, 1568, 1024], P('rep', 'grp')
- grad_gain: float32 [2, 1024], P(None, 'grp')
- grad_bias: float32 [6, 1024], P(None, 'grp')
- grad_bias_ff: float32 [4096], P('grp')
- grad_qkv: float32 [1024, 3072], P('grp', 'rep')
- grad_o: float32 [1024, 1024], P('grp', 'rep')
- grad_up: float32 [1024, 4096], P('grp', 'rep')
- grad_down: float32 [4096, 1024], P('grp', 'rep')
Inputs may be any that keep to these rules, and one draw needn't show every extreme that they name: Group g's live clips are its slots 0 to clip_count[g] - 1.
All inputs are finite; a program needn't handle non-finite values.
Results may differ from a plain program's by a relative error of at most 0.012.
The roundings to bfloat16 on the way count: a program that leaves them out, or rounds other values in their place, can miss the bound.
Values may be sent and summed in bfloat16 or wider, within the bound.
No kernel may reach another device: no remote copies, remote signals or barrier semaphores. Data moves between devices by JAX's collectives and lax.ppermute only.
A program may use at most 568 MiB of HBM per device.

v0:
```python
import jax
import jax.numpy as jnp
from jax import lax
from jax.sharding import PartitionSpec as P

H = 16
HD = 64


EPSILON = 1e-06


def matmul(left, right):
    return jnp.dot(left, right, preferred_element_type=jnp.float32)


def layer_norm(values, gain, shift):
    centred = values - jnp.mean(values, -1, keepdims=True)
    spread = jnp.mean(centred * centred, -1, keepdims=True)
    inverse = lax.rsqrt(spread + EPSILON)
    scaled = centred * inverse
    return (scaled, inverse, scaled * gain + shift)


def norm_back(scaled, inverse, gain, incoming):
    weighted = incoming * gain
    first = jnp.mean(weighted, -1, keepdims=True)
    second = jnp.mean(weighted * scaled, -1, keepdims=True)
    return inverse * (weighted - first - scaled * second)


def fetch_weights(shards):
    return (
        lax.all_gather(shards[0], "grp", axis=0, tiled=True),
        lax.all_gather(shards[1], "grp", axis=0, tiled=True),
        lax.all_gather(shards[2], "grp", axis=0, tiled=True),
        lax.all_gather(shards[3], "grp", axis=0, tiled=True),
        lax.all_gather(shards[4], "grp", axis=1, tiled=True),
        lax.all_gather(shards[5], "grp", axis=1, tiled=True),
        lax.all_gather(shards[6], "grp", axis=0, tiled=True),
    )


def shard_grads(weight_grads):
    return (
        lax.psum_scatter(weight_grads[0], "grp", scatter_dimension=1, tiled=True),
        lax.psum_scatter(weight_grads[1], "grp", scatter_dimension=1, tiled=True),
        lax.psum_scatter(weight_grads[2], "grp", scatter_dimension=0, tiled=True),
        lax.psum_scatter(weight_grads[3], "grp", scatter_dimension=0, tiled=True),
        lax.psum_scatter(weight_grads[4], "grp", scatter_dimension=0, tiled=True),
        lax.psum_scatter(weight_grads[5], "grp", scatter_dimension=0, tiled=True),
        lax.psum_scatter(weight_grads[6], "grp", scatter_dimension=0, tiled=True),
    )


def raw_scores(query, keys):
    rows = query.shape[0]
    length = keys.shape[0]
    return jnp.einsum(
        "qhd,khd->hqk",
        query.reshape(rows, H, HD),
        keys.reshape(length, H, HD),
        preferred_element_type=jnp.float32,
    ) * HD ** (-0.5)


def score_probs(query, keys):
    return jax.nn.softmax(raw_scores(query, keys), axis=-1)


def forward_pass(row_block, gathered):
    qkv_weight, out_weight, up_weight, down_weight, gains, biases, hidden_bias = gathered
    gain_f = gains.astype(jnp.float32)
    bias_f = biases.astype(jnp.float32)
    rows = row_block.shape[0]
    model_width = row_block.shape[1]
    inputs = row_block.astype(jnp.float32)
    scaled1, inverse1, normed = layer_norm(inputs, gain_f[0], bias_f[0])
    normed = normed.astype(jnp.bfloat16)
    shift = jnp.concatenate([bias_f[1], jnp.zeros_like(bias_f[1]), bias_f[2]])
    qkv = (matmul(normed, qkv_weight) + shift).astype(jnp.bfloat16)
    query = qkv[:, :model_width]
    key_part = qkv[:, model_width : 2 * model_width]
    value_part = qkv[:, 2 * model_width :]
    keys, values = (
        lax.all_gather(key_part, "grp", axis=0, tiled=True),
        lax.all_gather(value_part, "grp", axis=0, tiled=True),
    )
    length = keys.shape[0]
    probs = score_probs(query, keys)
    context = (
        jnp.einsum(
            "hqk,khd->qhd",
            probs.astype(jnp.bfloat16),
            values.reshape(length, H, HD),
            preferred_element_type=jnp.float32,
        )
        .reshape(rows, model_width)
        .astype(jnp.bfloat16)
    )
    hidden = inputs + matmul(context, out_weight) + bias_f[3]
    scaled2, inverse2, normed2 = layer_norm(hidden, gain_f[1], bias_f[4])
    normed2 = normed2.astype(jnp.bfloat16)
    pre = matmul(normed2, up_weight) + hidden_bias.astype(jnp.float32)
    active = jax.nn.gelu(pre, approximate=False).astype(jnp.bfloat16)
    result = hidden + matmul(active, down_weight) + bias_f[5]
    saved = (
        scaled1,
        inverse1,
        normed,
        query,
        keys,
        values,
        context,
        scaled2,
        inverse2,
        normed2,
        pre,
        active,
    )
    return (result, saved)


def backward_pass(incoming, weight, saved, gathered):
    qkv_weight, out_weight, up_weight, down_weight, gains, biases, hidden_bias = gathered
    gain_f = gains.astype(jnp.float32)
    (
        scaled1,
        inverse1,
        normed,
        query,
        keys,
        values,
        context,
        scaled2,
        inverse2,
        normed2,
        pre,
        active,
    ) = saved
    rows = query.shape[0]
    model_width = query.shape[1]
    length = keys.shape[0]
    d_out = incoming * weight.astype(jnp.bfloat16)
    d_out_f = d_out.astype(jnp.float32)
    grad_down = jnp.einsum("rf,rd->fd", active, d_out, preferred_element_type=jnp.float32)
    grad_b2 = jnp.sum(d_out_f, 0)
    d_act = jnp.einsum("rd,fd->rf", d_out, down_weight, preferred_element_type=jnp.float32)
    unused, gelu_pull = jax.vjp(lambda inputs: jax.nn.gelu(inputs, approximate=False), pre)
    d_pre = gelu_pull(d_act)[0].astype(jnp.bfloat16)
    grad_up = jnp.einsum("rd,rf->df", normed2, d_pre, preferred_element_type=jnp.float32)
    grad_hidden_bias = jnp.sum(d_pre.astype(jnp.float32), 0)
    d_norm2 = jnp.einsum("rf,df->rd", d_pre, up_weight, preferred_element_type=jnp.float32)
    d_hidden = d_out_f + norm_back(scaled2, inverse2, gain_f[1], d_norm2)
    grad_g2 = jnp.sum(d_norm2 * scaled2, 0)
    grad_beta2 = jnp.sum(d_norm2, 0)
    d_branch = d_hidden.astype(jnp.bfloat16)
    grad_out = jnp.einsum("rd,re->de", context, d_branch, preferred_element_type=jnp.float32)
    grad_bo = jnp.sum(d_branch.astype(jnp.float32), 0)
    d_context = jnp.einsum(
        "re,de->rd", d_branch, out_weight, preferred_element_type=jnp.float32
    ).astype(jnp.bfloat16)
    scores = raw_scores(query, keys)
    probs = jax.nn.softmax(scores, axis=-1)
    context_heads = d_context.reshape(rows, H, HD)
    d_probs = jnp.einsum(
        "qhd,khd->hqk",
        context_heads,
        values.reshape(length, H, HD),
        preferred_element_type=jnp.float32,
    )
    delta = jnp.sum(probs * d_probs, -1)
    d_scores = (probs * (d_probs - delta[..., None])).astype(jnp.bfloat16)
    d_query = (
        jnp.einsum(
            "hqk,khd->qhd",
            d_scores,
            keys.reshape(length, H, HD),
            preferred_element_type=jnp.float32,
        )
        * HD ** (-0.5)
    ).reshape(rows, model_width)
    d_value = jnp.einsum(
        "hqk,qhd->khd",
        probs.astype(jnp.bfloat16),
        context_heads,
        preferred_element_type=jnp.float32,
    ).reshape(length, model_width)
    d_key = (
        jnp.einsum(
            "hqk,qhd->khd", d_scores, query.reshape(rows, H, HD), preferred_element_type=jnp.float32
        )
        * HD ** (-0.5)
    ).reshape(length, model_width)
    d_key, d_value = (
        lax.psum_scatter(d_key, "grp", scatter_dimension=0, tiled=True),
        lax.psum_scatter(d_value, "grp", scatter_dimension=0, tiled=True),
    )
    d_qkv = jnp.concatenate(
        [d_query.astype(jnp.bfloat16), d_key.astype(jnp.bfloat16), d_value.astype(jnp.bfloat16)], 1
    )
    grad_qkv = jnp.einsum("rd,re->de", normed, d_qkv, preferred_element_type=jnp.float32)
    d_qkv_f = d_qkv.astype(jnp.float32)
    grad_bq = jnp.sum(d_qkv_f[:, :model_width], 0)
    grad_bv = jnp.sum(d_qkv_f[:, 2 * model_width :], 0)
    d_norm1 = jnp.einsum("re,de->rd", d_qkv, qkv_weight, preferred_element_type=jnp.float32)
    row_grad = d_hidden + norm_back(scaled1, inverse1, gain_f[0], d_norm1)
    grad_g1 = jnp.sum(d_norm1 * scaled1, 0)
    grad_beta1 = jnp.sum(d_norm1, 0)
    grad_gains = jnp.stack([grad_g1, grad_g2])
    grad_biases = jnp.stack([grad_beta1, grad_bq, grad_bv, grad_bo, grad_beta2, grad_b2])
    weight_grads = (
        grad_gains,
        grad_biases,
        grad_hidden_bias,
        grad_qkv,
        grad_out,
        grad_up,
        grad_down,
    )
    return (row_grad, weight_grads)


def body(clips, clip_count, cotangent, norm_gain, bias_d, bias_ff, w_qkv, w_o, w_up, w_down):
    shards = (w_qkv, w_o, w_up, w_down, norm_gain, bias_d, bias_ff)
    number = clips.shape[0]
    outputs = []
    records = []
    actives = []
    for slot_index in range(number):
        gathered = fetch_weights(shards)
        active = (clip_count[0] > slot_index).astype(jnp.float32)
        result, saved = forward_pass(clips[slot_index], gathered)
        outputs.append((result * active).astype(jnp.bfloat16))
        records.append(saved)
        actives.append(active)
    row_grads = [None] * number
    totals = None
    for slot_index in reversed(range(number)):
        gathered = fetch_weights(shards)
        row_grad, weight_grads = backward_pass(
            cotangent[slot_index], actives[slot_index], records[slot_index], gathered
        )
        row_grads[slot_index] = row_grad
        totals = (
            weight_grads
            if totals is None
            else jax.tree.map(lambda left, right: left + right, totals, weight_grads)
        )
    totals = shard_grads(totals)
    small_sums = lax.psum((totals[0], totals[1], totals[2]), "rep")
    matrix_sums = (
        lax.psum_scatter(totals[3], "rep", scatter_dimension=1, tiled=True),
        lax.psum_scatter(totals[4], "rep", scatter_dimension=1, tiled=True),
        lax.psum_scatter(totals[5], "rep", scatter_dimension=1, tiled=True),
        lax.psum_scatter(totals[6], "rep", scatter_dimension=1, tiled=True),
    )
    return (jnp.stack(outputs), jnp.stack(row_grads)) + tuple(small_sums) + tuple(matrix_sums)


def solution(mesh):
    in_specs = (
        P("rep", "grp", None),
        P("rep"),
        P("rep", "grp", None),
        P(None, "grp"),
        P(None, "grp"),
        P("grp"),
        P("grp", None),
        P("grp", None),
        P("grp", None),
        P("grp", None),
    )
    out_specs = (
        P("rep", "grp", None),
        P("rep", "grp", None),
        P(None, "grp"),
        P(None, "grp"),
        P("grp"),
        P("grp", "rep"),
        P("grp", "rep"),
        P("grp", "rep"),
        P("grp", "rep"),
    )
    return jax.shard_map(body, mesh=mesh, in_specs=in_specs, out_specs=out_specs, check_vma=False)
```

profile of v0, /device:TPU:9, one launch (start us, length us, event | category | flops | bytes accessed | tf_op | source)
XLA Modules:
  0.0 2439.0 jit_solution(3226198045179241031)
XLA Ops:
  21.0 70.1 %all-gather.11.cloned.1.call-done = bf16[1024,3072]{1,0:T(8,128)(2,1)} async-done(((bf16[512,3072]{1,0:T(8,128)(2,1)}), bf16[1024,3072]{1,0:T(8,128)(2,1)}) %all-gather.11.cloned.1.call-update) | async-done | bytes 6291472 | tf_op jit(solution)/shard_map/all_gather | solution.py:34
  151.5 36.7 %fusion.174 = (f32[16,784]{1,0:T(8,128)S(1)}, f32[16,784,1568]{2,1,0:T(8,128)}) fusion(bf16[784,16,64]{0,2,1:T(8,128)(2,1)} %bitcast.370, bf16[1568,16,64]{0,2,1:T(8,128)(2,1)S(1)} %bitcast.352), kind=kOutput, calls=%fused_computation.292 | convolution fusion | flops 2576639488 | bytes 83543040 | tf_op jit(solution)/shard_map/sub | solution.py:68
  198.8 31.8 %fusion.105 = bf16[16,64,784]{2,1,0:T(8,128)(2,1)} fusion(bf16[1568,16,64]{0,2,1:T(8,128)(2,1)S(1)} %bitcast.377, f32[16,784,1568]{2,1,0:T(8,128)} %get-tuple-element.132, f32[16,784]{1,0:T(8,128)S(1)} %get-tuple-element.131), kind=kOutput, calls=%fused_computation.210 | convolution fusion | flops 2557771776 | bytes 83543040 | tf_op jit(solution)/shard_map/hqk,khd->qhd/dot_general | solution.py:92
  238.1 38.5 %all-gather.29.cloned.1.call-done = bf16[1568,1024]{1,0:T(8,128)(2,1)} async-done(((bf16[784,1024]{1,0:T(8,128)(2,1)}), bf16[1568,1024]{1,0:T(8,128)(2,1)}) %all-gather.29.cloned.1.call-update) | async-done | bytes 3211280 | tf_op jit(solution)/shard_map/all_gather | solution.py:86
  280.9 36.7 %fusion.173 = (f32[16,784]{1,0:T(8,128)S(1)}, f32[16,784,1568]{2,1,0:T(8,128)}) fusion(bf16[784,16,64]{0,2,1:T(8,128)(2,1)} %bitcast.368, bf16[1568,16,64]{0,2,1:T(8,128)(2,1)S(1)} %bitcast.354), kind=kOutput, calls=%fused_computation.291 | convolution fusion | flops 2576639488 | bytes 83543040 | tf_op jit(solution)/shard_map/sub | solution.py:68
  328.1 32.5 %fusion.111 = bf16[16,64,784]{2,1,0:T(8,128)(2,1)} fusion(bf16[1568,16,64]{0,2,1:T(8,128)(2,1)S(1)} %bitcast.379, f32[16,784,1568]{2,1,0:T(8,128)} %get-tuple-element.130, f32[16,784]{1,0:T(8,128)S(1)} %get-tuple-element.129), kind=kOutput, calls=%fused_computation.212 | convolution fusion | flops 2557771776 | bytes 83543040 | tf_op jit(solution)/shard_map/hqk,khd->qhd/dot_general | solution.py:92
  375.3 36.8 %fusion.177 = (f32[16,784]{1,0:T(8,128)S(1)}, f32[16,784,1568]{2,1,0:T(8,128)}) fusion(bf16[784,16,64]{0,2,1:T(8,128)(2,1)} %bitcast.372, bf16[1568,16,64]{0,2,1:T(8,128)(2,1)S(1)} %bitcast.356), kind=kOutput, calls=%fused_computation.295 | convolution fusion | flops 2576639488 | bytes 83543040 | tf_op jit(solution)/shard_map/sub | solution.py:68
  422.6 34.2 %fusion.108 = bf16[16,64,784]{2,1,0:T(8,128)(2,1)} fusion(bf16[1568,16,64]{0,2,1:T(8,128)(2,1)S(1)} %bitcast.381, f32[16,784,1568]{2,1,0:T(8,128)} %get-tuple-element.138, f32[16,784]{1,0:T(8,128)S(1)} %get-tuple-element.137), kind=kOutput, calls=%fused_computation.211 | convolution fusion | flops 2557771776 | bytes 83543040 | tf_op jit(solution)/shard_map/hqk,khd->qhd/dot_general | solution.py:92
  464.0 59.9 %all-gather.19.cloned.1.call-done = bf16[1024,4096]{1,0:T(8,128)(2,1)} async-done(((bf16[512,4096]{1,0:T(8,128)(2,1)}), bf16[1024,4096]{1,0:T(8,128)(2,1)}) %all-gather.19.cloned.1.call-update) | async-done | bytes 8388624 | tf_op jit(solution)/shard_map/all_gather | solution.py:36
  549.9 99.4 %multiply_convert_fusion.5 = (bf16[784,4096]{1,0:T(8,128)(2,1)}, f32[784,4096]{1,0:T(8,128)}, bf16[784,4096]{1,0:T(8,128)(2,1)}, f32[784,4096]{1,0:T(8,128)}, bf...) fusion(f32[4096]{0:T(1024)S(1)} %copy-done.88, f32[784,4096]{1,0:T(8,128)} %fusion.164, ...), kind=kOutput, calls=%fused_computation.79 | convolution fusion | flops 7216513024 | bytes 107968640 | tf_op jit(solution)/shard_map/dot_general | solution.py:14
  833.4 31.9 %fusion.23 = f32[16,64,1568]{2,1,0:T(8,128)} fusion(bf16[784,16,64]{0,2,1:T(8,128)(2,1)S(1)} %bitcast.388, f32[16,784,1568]{2,1,0:T(8,128)} %get-tuple-element.132, f32[16,784]{1,0:T(8,128)S(1)} %copy-done.47), kind=kOutput, calls=%fused_computation.32 | convolution fusion | flops 2556968960 | bytes 86754304 | tf_op jit(solution)/shard_map/hqk,qhd->khd/dot_general | solution.py:183
  874.3 30.7 %fusion.19 = f32[16,64,1568]{2,1,0:T(8,128)} fusion(bf16[784,16,64]{0,2,1:T(8,128)(2,1)S(1)} %bitcast.391, f32[16,784,1568]{2,1,0:T(8,128)} %get-tuple-element.138, f32[16,784]{1,0:T(8,128)S(1)} %copy-done.53), kind=kOutput, calls=%fused_computation.28 | convolution fusion | flops 2556968960 | bytes 86754304 | tf_op jit(solution)/shard_map/hqk,qhd->khd/dot_general | solution.py:183
  912.7 56.6 %multiply_reduce_fusion.1 = (f32[16,784]{1,0:T(8,128)S(1)}, f32[16,784,1568]{2,1,0:T(8,128)}) fusion(f32[16,784,1568]{2,1,0:T(8,128)} %get-tuple-element.138, f32[16,784]{1,0:T(8,128)S(1)} %copy-done.53, bf16[784,16,64]{0,2,1:T(8,128)(2,1)} %bitcast.390, bf16[1568,16,64]{0,2,1:T(8,128)(2,1)S(1)} %bitcast.382), kind=kOutput, calls=%fused_computation.6 | convolution fusion | flops 2576625408 | bytes 162269184 | tf_op jit(solution)/shard_map/qhd,khd->hqk/dot_general | solution.py:166
  969.3 67.2 %multiply_convert_fusion.1 = bf16[16,784,1568]{2,1,0:T(8,128)(2,1)} fusion(f32[16,784,1568]{2,1,0:T(8,128)} %get-tuple-element.149, f32[16,784]{1,0:T(8,128)S(1)} %get-tuple-element.148, f32[16,784,1568]{2,1,0:T(8,128)} %get-tuple-element.138, f32[16,784]{1,0:T(8,128)S(1)} %copy-done.53), kind=kLoop, calls=%fused_computation.5 | loop fusion | flops 78675968 | bytes 196790272 | tf_op jit(solution)/shard_map/convert_element_type | solution.py:173
  1063.6 55.6 %multiply_reduce_fusion.2 = (f32[16,784]{1,0:T(8,128)S(1)}, f32[16,784,1568]{2,1,0:T(8,128)}) fusion(f32[16,784,1568]{2,1,0:T(8,128)} %get-tuple-element.132, f32[16,784]{1,0:T(8,128)S(1)} %copy-done.48, bf16[784,16,64]{0,2,1:T(8,128)(2,1)} %bitcast.389, bf16[1568,16,64]{0,2,1:T(8,128)(2,1)S(1)} %bitcast.378), kind=kOutput, calls=%fused_computation.8 | convolution fusion | flops 2576625408 | bytes 162269184 | tf_op jit(solution)/shard_map/qhd,khd->hqk/dot_general | solution.py:166
  1119.3 67.2 %multiply_convert_fusion.2 = bf16[16,784,1568]{2,1,0:T(8,128)(2,1)} fusion(f32[16,784,1568]{2,1,0:T(8,128)} %get-tuple-element.145, f32[16,784]{1,0:T(8,128)S(1)} %get-tuple-element.144, f32[16,784,1568]{2,1,0:T(8,128)} %get-tuple-element.132, f32[16,784]{1,0:T(8,128)S(1)} %copy-done.48), kind=kLoop, calls=%fused_computation.7 | loop fusion | flops 78675968 | bytes 196790272 | tf_op jit(solution)/shard_map/convert_element_type | solution.py:173
  1213.6 55.8 %multiply_reduce_fusion = (f32[16,784]{1,0:T(8,128)S(1)}, f32[16,784,1568]{2,1,0:T(8,128)}) fusion(f32[16,784,1568]{2,1,0:T(8,128)} %get-tuple-element.130, f32[16,784]{1,0:T(8,128)S(1)} %copy-done.51, bf16[784,16,64]{0,2,1:T(8,128)(2,1)} %bitcast.387, bf16[1568,16,64]{0,2,1:T(8,128)(2,1)S(1)} %bitcast.380), kind=kOutput, calls=%fused_computation.4 | convolution fusion | flops 2576625408 | bytes 162269184 | tf_op jit(solution)/shard_map/qhd,khd->hqk/dot_general | solution.py:166
  1269.5 67.2 %multiply_convert_fusion = bf16[16,784,1568]{2,1,0:T(8,128)(2,1)} fusion(f32[16,784,1568]{2,1,0:T(8,128)} %get-tuple-element.147, f32[16,784]{1,0:T(8,128)S(1)} %get-tuple-element.146, f32[16,784,1568]{2,1,0:T(8,128)} %get-tuple-element.130, f32[16,784]{1,0:T(8,128)S(1)} %copy-done.51), kind=kLoop, calls=%fused_computation.3 | loop fusion | flops 78675968 | bytes 196790272 | tf_op jit(solution)/shard_map/convert_element_type | solution.py:173
  1691.1 191.4 %reduce-scatter.47.cloned.1.call-done = f32[2048,1024]{1,0:T(8,128)} async-done(((f32[4096,1024]{1,0:T(8,128)}), f32[2048,1024]{1,0:T(8,128)}) %reduce-scatter.47.cloned.1.call-update) | async-done | bytes 8388624 | tf_op jit(solution)/shard_map/reduce_scatter | solution.py:52
  1899.9 129.7 %reduce-scatter.39.cloned.1.call-done = f32[512,3072]{1,0:T(8,128)} async-done(((f32[1024,3072]{1,0:T(8,128)}), f32[512,3072]{1,0:T(8,128)}) %reduce-scatter.39.cloned.1.call-update) | async-done | bytes 6291472 | tf_op jit(solution)/shard_map/reduce_scatter | solution.py:49
  2087.5 49.1 %all-reduce.1 = (f32[2,512]{1,0:T(2,128)}, f32[6,512]{1,0:T(8,128)}, f32[2048]{0:T(1024)}) all-reduce(f32[2,512]{1,0:T(2,128)S(1)} %copy.89, f32[6,512]{1,0:T(8,128)} %reduce-scatter.37.cloned.1.call-done, f32[2048]{0:T(1024)S(1)} %dynamic-slice-done), channel_id=1, replica_groups=mesh['rep'=16,'grp'=2] {'rep'}, use_global_device_ids=true, to_apply=%region_46.0 | all-reduce | flops 6144 | bytes 49152 | tf_op jit(solution)/shard_map/psum | solution.py:251
  2136.6 97.1 %reduce-scatter.45.cloned.1.call-done = f32[512,256]{1,0:T(8,128)} async-done(((f32[512,4096]{1,0:T(8,128)}), f32[512,256]{1,0:T(8,128)}) %reduce-scatter.45.cloned.1.call-update) | async-done | bytes 524304 | tf_op jit(solution)/shard_map/reduce_scatter | solution.py:255
  2233.7 109.6 %reduce-scatter.67.cloned.1.call-done = f32[64,2048]{1,0:T(8,128)} async-done(((f32[1024,2048]{1,0:T(8,128)}), f32[64,2048]{1,0:T(8,128)}) %reduce-scatter.67.cloned.1.call-update) | async-done | bytes 524304
  2343.3 88.9 %reduce-scatter.63.cloned.1.call-done = f32[192,512]{1,0:T(8,128)} async-done(((f32[3072,512]{1,0:T(8,128)}), f32[192,512]{1,0:T(8,128)}) %reduce-scatter.63.cloned.1.call-update) | async-done | bytes 393232
  (453 shorter events, 847.3 us)
Async XLA Ops:
  7.9 139.3 %all-gather.15.cloned.1.call-start = ((), (), s32[]{:S(2)}) async-start(), calls=%async_computation.18 | async-start | bytes 4816896 | tf_op jit(solution)/shard_map/all_gather | solution.py:86
  102.0 128.6 %all-gather.17.cloned.1.call-start = ((), (), s32[]{:S(2)}) async-start(), calls=%async_computation.19 | async-start | bytes 3145728 | tf_op jit(solution)/shard_map/all_gather | solution.py:35
  102.6 174.1 %all-gather.29.cloned.1.call-start = ((), (), s32[]{:S(2)}) async-start(), calls=%async_computation.25 | async-start | bytes 4816896 | tf_op jit(solution)/shard_map/all_gather | solution.py:86
  112.9 210.9 %all-gather.27.cloned.1.call-start = ((), (), s32[]{:S(2)}) async-start(), calls=%async_computation.24 | async-start | bytes 4816896 | tf_op jit(solution)/shard_map/all_gather | solution.py:87
  113.4 257.6 %all-gather.25.cloned.1.call-start = ((), (), s32[]{:S(2)}) async-start(), calls=%async_computation.23 | async-start | bytes 4816896 | tf_op jit(solution)/shard_map/all_gather | solution.py:86
  124.5 293.8 %all-gather.23.cloned.1.call-start = ((), (), s32[]{:S(2)}) async-start(), calls=%async_computation.22 | async-start | bytes 4816896 | tf_op jit(solution)/shard_map/all_gather | solution.py:87
  125.2 398.6 %all-gather.19.cloned.1.call-start = ((), (), s32[]{:S(2)}) async-start(), calls=%async_computation.20 | async-start | bytes 12582912 | tf_op jit(solution)/shard_map/all_gather | solution.py:36
  126.0 523.4 %all-gather.21.cloned.1.call-start = ((), (), s32[]{:S(2)}) async-start(), calls=%async_computation.21 | async-start | bytes 12582912 | tf_op jit(solution)/shard_map/all_gather | solution.py:37
  126.6 1417.0 %reduce-scatter.59.cloned.1.call-start = ((), (), s32[]{:S(2)}) async-start(), calls=%async_computation.37 | async-start | bytes 9633792
  816.3 731.4 %reduce-scatter.51.cloned.1.call-start = ((), (), s32[]{:S(2)}) async-start(), calls=%async_computation.33 | async-start | bytes 9633792
  872.8 679.2 %reduce-scatter.55.cloned.1.call-start = ((), (), s32[]{:S(2)}) async-start(), calls=%async_computation.35 | async-start | bytes 9633792
  969.3 587.1 %reduce-scatter.53.cloned.1.call-start = ((), (), s32[]{:S(2)}) async-start(), calls=%async_computation.34 | async-start | bytes 9633792
  1119.3 441.4 %reduce-scatter.49.cloned.1.call-start = ((), (), s32[]{:S(2)}) async-start(), calls=%async_computation.32 | async-start | bytes 9633792
  1269.4 295.4 %reduce-scatter.57.cloned.1.call-start = ((), (), s32[]{:S(2)}) async-start(), calls=%async_computation.36 | async-start | bytes 9633792
  1363.5 307.4 %reduce-scatter.41.cloned.1.call-start = ((), (), s32[]{:S(2)}) async-start(), calls=%async_computation.28 | async-start | bytes 6291456 | tf_op jit(solution)/shard_map/reduce_scatter | solution.py:50
  1376.6 314.4 %reduce-scatter.43.cloned.1.call-start = ((), (), s32[]{:S(2)}) async-start(), calls=%async_computation.29 | async-start | bytes 25165824 | tf_op jit(solution)/shard_map/reduce_scatter | solution.py:51
  1427.8 454.7 %reduce-scatter.47.cloned.1.call-start = ((), (), s32[]{:S(2)}) async-start(), calls=%async_computation.31 | async-start | bytes 25165824 | tf_op jit(solution)/shard_map/reduce_scatter | solution.py:52
  1481.3 548.3 %reduce-scatter.39.cloned.1.call-start = ((), (), s32[]{:S(2)}) async-start(), calls=%async_computation.27 | async-start | bytes 18874368 | tf_op jit(solution)/shard_map/reduce_scatter | solution.py:49
  1617.0 469.4 %reduce-scatter.61.cloned.1.call-start = ((), (), s32[]{:S(2)}) async-start(), calls=%async_computation.38 | async-start | bytes 786432
  1669.6 417.9 %reduce-scatter.37.cloned.1.call-start = ((), (), s32[]{:S(2)}) async-start(), calls=%async_computation.26 | async-start | bytes 49152 | tf_op jit(solution)/shard_map/reduce_scatter | solution.py:47
  1670.6 466.0 %reduce-scatter.65.cloned.1.call-start = ((), (), s32[]{:S(2)}) async-start(), calls=%async_computation.40 | async-start | bytes 2228224
  1673.8 559.9 %reduce-scatter.45.cloned.1.call-start = ((), (), s32[]{:S(2)}) async-start(), calls=%async_computation.30 | async-start | bytes 8912896 | tf_op jit(solution)/shard_map/reduce_scatter | solution.py:255
  1691.0 652.2 %reduce-scatter.67.cloned.1.call-start = ((), (), s32[]{:S(2)}) async-start(), calls=%async_computation.41 | async-start | bytes 8912896
  1891.7 540.5 %reduce-scatter.63.cloned.1.call-start = ((), (), s32[]{:S(2)}) async-start(), calls=%async_computation.39 | async-start | bytes 6684672
  (127 other events, 3117.2 us)
Sparse Core Ops, SparseCore 0:
  9.5 81.5 all-gather.10
  101.4 45.7 all-gather.14
  148.7 45.6 all-gather.12
  195.8 33.1 all-gather.16
  231.0 45.6 all-gather.28
  278.0 45.6 all-gather.26
  325.3 45.6 all-gather.24
  372.6 45.6 all-gather.22
  419.8 103.9 all-gather.18
  525.3 103.9 all-gather.20
  816.4 78.5 reduce-scatter.58
  897.3 78.4 reduce-scatter.50
  978.1 78.4 reduce-scatter.54
  1119.4 78.6 reduce-scatter.52
  1269.5 78.8 reduce-scatter.48
  1363.6 78.9 reduce-scatter.56
  1445.3 54.3 reduce-scatter.40
  1501.9 189.0 reduce-scatter.42
  1693.3 189.1 reduce-scatter.46
  1884.7 144.8 reduce-scatter.38
  2062.4 60.2 reduce-scatter.64
  2127.7 105.9 reduce-scatter.44
  2238.9 104.3 reduce-scatter.66
  2348.2 83.9 reduce-scatter.62
  (2 shorter events, 23.8 us)
where the time goes:
time: 2450 us; the launch traced here: 2440 us
  matrix products  1110 us (45%)
  waiting for transfers between devices  836 us (34%)
  other arithmetic  241 us (10%)
  local copies, waits for them, and re-layouts  170 us (7%)
  blocking collectives  66 us (3%)
    unnamed x36, waiting for transfers between devices  203 us
    convert_element_type x3, other arithmetic, backward_pass(): d_scores = (probs * (d_probs - delta[..., None])).astype(jnp.bfloat16)  202 us
    reduce_scatter x1, waiting for transfers between devices, shard_grads(): lax.psum_scatter(weight_grads[6], 'grp', scatter_dimension=0, tiled=True)  191 us
    dot_general x12, matrix products, matmul(): return jnp.dot(left, right, preferred_element_type=jnp.float32)  191 us
    dot_general x3, matrix products, backward_pass(): jnp.einsum('qhd,khd->hqk', context_heads, values.reshape(length, H, HD),...  168 us
    reduce_scatter x1, waiting for transfers between devices, shard_grads(): lax.psum_scatter(weight_grads[3], 'grp', scatter_dimension=0, tiled=True)  130 us
    unnamed x268, local copies, waits for them, and re-layouts  117 us
    sub x3, matrix products, score_probs(): return jax.nn.softmax(raw_scores(query, keys), axis=-1)  110 us
  transfers between devices with their start and end apart: 26, of which 14 were waited for; matrix products, arithmetic and copies ran while one was open for 54% of the time, Pallas kernels for 0%

commit v1 on v0

--- a/solution.py
+++ b/solution.py
@@ -1,13 +1,268 @@
+import functools
+
 import jax
 import jax.numpy as jnp
 from jax import lax
+from jax.experimental import pallas as pl
+from jax.experimental.pallas import tpu as pltpu
+from jax.sharding import Mesh
 from jax.sharding import PartitionSpec as P
 
 H = 16
 HD = 64
-
-
 EPSILON = 1e-06
+
+F32 = jnp.float32
+BF = jnp.bfloat16
+LOG2E = 1.4426950408889634
+SCALE = HD ** -0.5
+BQ = 512
+TK = 224
+LIMIT = 70.0
+
+
+def dot(a, b, dims):
+    return lax.dot_general(a, b, (dims, ((), ())), preferred_element_type=F32)
+
+
+def nt(a, b):
+    return dot(a, b, ((1,), (1,)))
+
+
+def nn(a, b):
+    return dot(a, b, ((1,), (0,)))
+
+
+def tn(a, b):
+    return dot(a, b, ((0,), (0,)))
+
+
+def pair_mask(a):
+    lane = lax.broadcasted_iota(jnp.int32, (1, 128), 1)
+    return (lane < HD) if a == 0 else (lane >= HD)
+
+def norm_peak(x, np_):
+    inner = x.shape[1]
+    r = lax.broadcasted_iota(jnp.int32, (inner, 128), 0)
+    c = lax.broadcasted_iota(jnp.int32, (inner, 128), 1)
+    ones = jnp.where(r // HD == c, 1.0, 0.0).astype(BF)
+    xf = x.astype(F32)
+    return jnp.max(nn((xf * xf).astype(BF), ones), axis=0, keepdims=True)
+
+def attend_kernel(own, rec, oo, orr, ro, rr, p_out, prem_out, q_s, k_s, vt_s, o_s, r_s, fast, *, nb, np_, rem):
+    half = own.shape[0]
+    inner = own.shape[1] // 3
+    full = 2 * half
+    t = pl.program_id(0)
+    last = np_ * nb
+
+    @pl.when(t == 0)
+    def _():
+        q_s[:half] = own[:, :inner]
+        q_s[half:] = rec[:, :inner]
+        k_s[:half] = own[:, inner:2 * inner]
+        k_s[half:] = rec[:, inner:2 * inner]
+        row = lax.broadcasted_iota(jnp.int32, (128, 1), 0)
+        for p in range(np_):
+            cols = slice(2 * inner + p * 128, 2 * inner + (p + 1) * 128)
+            vt = jnp.concatenate([own[:, cols], rec[:, cols]], axis=0).T
+            for a in range(2):
+                mine = (row < HD) if a == 0 else (row >= HD)
+                vt_s[2 * p + a] = jnp.where(mine, vt, 1.0).astype(BF)
+        peak = jnp.max(norm_peak(q_s[...], np_) * norm_peak(k_s[...], np_))
+        fast[0] = (peak * (1.1 * SCALE * SCALE) < LIMIT * LIMIT).astype(jnp.int32)
+
+    def store(o, rows, cols):
+        oa, ob = o
+        ra = 1.0 / oa[HD:]
+        rb = 1.0 / ob[:HD]
+        o_s[rows, cols] = jnp.concatenate([oa[:HD] * ra, ob[HD:] * rb], axis=0).T.astype(BF)
+        r_s[rows, cols] = jnp.concatenate([ra, rb], axis=0).T
+
+    def main(quick):
+        p = t // nb
+        b = t % nb
+        rows = pl.ds(pl.multiple_of(b * BQ, BQ), BQ)
+        cols = pl.ds(pl.multiple_of(p * 128, 128), 128)
+        q = q_s[rows, cols]
+        def weights(a):
+            qa = jnp.where(pair_mask(a), q, 0.0).astype(BF)
+            if quick:
+                for j in range(full // TK):
+                    tile = slice(j * TK, (j + 1) * TK)
+                    s = nt(k_s[tile, cols], qa)
+                    p_out[0, a, tile] = jnp.exp2(s * (LOG2E * SCALE)).astype(BF)
+            else:
+                s = nt(k_s[:, cols], qa)
+                m = jnp.max(s, axis=0, keepdims=True)
+                p_out[0, a] = jnp.exp2((s - m) * (LOG2E * SCALE)).astype(BF)
+        weights(0)
+        weights(1)
+        oa = nn(vt_s[2 * p], p_out[0, 0])
+        ob = nn(vt_s[2 * p + 1], p_out[0, 1])
+        store((oa, ob), rows, cols)
+
+    @pl.when((t < last) & (fast[0] == 1))
+    def _():
+        main(True)
+
+    @pl.when((t < last) & (fast[0] == 0))
+    def _():
+        main(False)
+
+    @pl.when(t == last)
+    def _():
+        if rem:
+            lane = lax.broadcasted_iota(jnp.int32, (1, 256), 1)
+            for u in range(np_ // 2):
+                q = q_s[nb * BQ:, u * 256:(u + 1) * 256]
+                qd = jnp.concatenate([jnp.where(lane // HD == h, q, 0.0).astype(BF) for h in range(4)], axis=0)
+                s = nt(k_s[:, u * 256:(u + 1) * 256], qd)
+                m = jnp.max(s, axis=0, keepdims=True)
+                prem_out[u] = jnp.exp2((s - m) * (LOG2E * SCALE)).astype(BF)
+                for v in range(2):
+                    oa = nn(vt_s[4 * u + 2 * v], prem_out[u])
+                    ob = nn(vt_s[4 * u + 2 * v + 1], prem_out[u])
+                    ra = 1.0 / oa[HD:]
+                    rb = 1.0 / ob[:HD]
+                    x = jnp.concatenate([oa[:HD] * ra, ob[HD:] * rb], axis=0).T
+                    r = jnp.concatenate([ra, rb], axis=0).T
+                    ha, hb = 2 * v, 2 * v + 1
+                    pick = lambda y: jnp.where(pair_mask(0), y[ha * rem:(ha + 1) * rem], y[hb * rem:(hb + 1) * rem])
+                    cols = slice((2 * u + v) * 128, (2 * u + v + 1) * 128)
+                    o_s[nb * BQ:, cols] = pick(x).astype(BF)
+                    r_s[nb * BQ:, cols] = pick(r)
+        oo[...] = o_s[:half]
+        orr[...] = o_s[half:]
+        ro[...] = r_s[:half]
+        rr[...] = r_s[half:]
+
+def attend(own, rec):
+    half, w = own.shape
+    inner = w // 3
+    np_ = inner // 128
+    full = 2 * half
+    nb = full // BQ
+    rem = full - nb * BQ
+    last = np_ * nb
+    whole = lambda shape: pl.BlockSpec(shape, lambda t: (0,) * len(shape))
+    return pl.pallas_call(
+        functools.partial(attend_kernel, nb=nb, np_=np_, rem=rem),
+        grid=(last + 1,),
+        in_specs=[whole((half, w))] * 2,
+        out_specs=[whole((half, inner))] * 4 + [pl.BlockSpec((1, 2, full, BQ), lambda t: (jnp.minimum(t, last - 1), 0, 0, 0)), whole((np_ // 2, full, 4 * rem))],
+        out_shape=[jax.ShapeDtypeStruct((half, inner), BF)] * 2 + [jax.ShapeDtypeStruct((half, inner), F32)] * 2
+        + [jax.ShapeDtypeStruct((last, 2, full, BQ), BF), jax.ShapeDtypeStruct((np_ // 2, full, 4 * rem), BF)],
+        scratch_shapes=[
+            pltpu.VMEM((full, inner), BF), pltpu.VMEM((full, inner), BF), pltpu.VMEM((2 * np_, 128, full), BF),
+            pltpu.VMEM((full, inner), BF), pltpu.VMEM((full, inner), F32), pltpu.SMEM((1,), jnp.int32)],
+        compiler_params=pltpu.CompilerParams(vmem_limit_bytes=60 * 1024 * 1024),
+    )(own, rec)
+
+
+def attend_back_kernel(own, rec, do_o, do_r, o_o, o_r, r_o, r_r, e, erem, out_o, out_r,
+               q_s, k_s, v_s, kt_s, do_s, pr_s, ds_s, dq_s, dk_s, dv_s, *, nb, np_, rem):
+    half = own.shape[0]
+    inner = own.shape[1] // 3
+    full = 2 * half
+    t = pl.program_id(0)
+    last = np_ * nb
+
+    @pl.when(t == 0)
+    def _():
+        for lo, src, d, o, r in ((0, own, do_o, o_o, r_o), (half, rec, do_r, o_r, r_r)):
+            rows = slice(lo, lo + half)
+            q_s[rows] = src[:, :inner]
+            k_s[rows] = src[:, inner:2 * inner]
+            v_s[rows] = src[:, 2 * inner:]
+            dn = (d[...].astype(F32) * r[...]).astype(BF)
+            do_s[rows] = dn
+            pr_s[rows] = dn.astype(F32) * o[...].astype(F32)
+        for p in range(np_):
+            kt_s[p * 128:(p + 1) * 128] = k_s[:, p * 128:(p + 1) * 128].T
+        dk_s[...] = jnp.zeros_like(dk_s)
+        dv_s[...] = jnp.zeros_like(dv_s)
+
+    @pl.when(t < last)
+    def _():
+        p = t // nb
+        b = t % nb
+        rows = pl.ds(pl.multiple_of(b * BQ, BQ), BQ)
+        cols = pl.ds(pl.multiple_of(p * 128, 128), 128)
+        q = q_s[rows, cols]
+        dn = do_s[rows, cols]
+        prod = pr_s[rows, cols].T
+        qs, dns = [], []
+        for a in range(2):
+            qs.append(jnp.where(pair_mask(a), q, 0.0).astype(BF))
+            dns.append(jnp.where(pair_mask(a), dn, 0.0).astype(BF))
+        for a in range(2):
+            delta = jnp.sum(prod[a * HD:(a + 1) * HD], axis=0, keepdims=True)
+            for j in range(full // TK):
+                tile = slice(j * TK, (j + 1) * TK)
+                dp = nt(v_s[tile, cols], dns[a])
+                ds_s[a, tile] = (e[0, a, tile].astype(F32) * (dp - delta)).astype(BF)
+        for j in range(full // TK):
+            tile = slice(j * TK, (j + 1) * TK)
+            dv_s[tile, cols] += nn(e[0, 0, tile], dns[0]) + nn(e[0, 1, tile], dns[1])
+        dqt = []
+        for a in range(2):
+            dqt.append(nn(kt_s[pl.ds(pl.multiple_of(p * 128, 128), 128)], ds_s[a])[a * HD:(a + 1) * HD])
+        dq_s[rows, cols] = (jnp.concatenate(dqt, axis=0) * SCALE).T.astype(BF)
+        for j in range(full // TK):
+            tile = slice(j * TK, (j + 1) * TK)
+            dk_s[tile, cols] += nn(ds_s[0, tile], qs[0]) + nn(ds_s[1, tile], qs[1])
+
+    @pl.when(t == last)
+    def _():
+        if rem:
+            lane = lax.broadcasted_iota(jnp.int32, (1, 256), 1)
+            def spread(x):
+                return jnp.concatenate([jnp.where(lane // HD == h, x, 0.0).astype(x.dtype) for h in range(4)], axis=0)
+            for u in range(np_ // 2):
+                cols = slice(u * 256, (u + 1) * 256)
+                qd = spread(q_s[nb * BQ:, cols])
+                dd = spread(do_s[nb * BQ:, cols])
+                delta = jnp.sum(spread(pr_s[nb * BQ:, cols]).T, axis=0, keepdims=True)
+                dp = nt(v_s[:, cols], dd)
+                ds = (erem[u].astype(F32) * (dp - delta)).astype(BF)
+                dv_s[:, cols] += nn(erem[u], dd)
+                dk_s[:, cols] += nn(ds, qd)
+                x = nn(kt_s[cols], ds).T * SCALE
+                dq = x[:rem]
+                for h in range(1, 4):
+                    dq = jnp.where(lane // HD == h, x[h * rem:(h + 1) * rem], dq)
+                dq_s[nb * BQ:, cols] = dq.astype(BF)
+        for lo, dst in ((0, out_o), (half, out_r)):
+            rows = slice(lo, lo + half)
+            dst[:, :inner] = dq_s[rows]
+            dst[:, inner:2 * inner] = (dk_s[rows] * SCALE).astype(BF)
+            dst[:, 2 * inner:] = dv_s[rows].astype(BF)
+
+def attend_back(own, rec, do_o, do_r, o_o, o_r, r_o, r_r, e, erem):
+    half, w = own.shape
+    inner = w // 3
+    np_ = inner // 128
+    full = 2 * half
+    nb = full // BQ
+    rem = full - nb * BQ
+    last = np_ * nb
+    whole = lambda shape, **kw: pl.BlockSpec(shape, lambda t: (0,) * len(shape), **kw)
+    one = dict(pipeline_mode=pl.Buffered(1))
+    return pl.pallas_call(
+        functools.partial(attend_back_kernel, nb=nb, np_=np_, rem=rem),
+        grid=(last + 1,),
+        in_specs=[whole((half, w), **one)] * 2 + [whole((half, inner), **one)] * 6
+        + [pl.BlockSpec((1, 2, full, BQ), lambda t: (jnp.minimum(t, last - 1), 0, 0, 0)), whole(erem.shape, **one)],
+        out_specs=[whole((half, w), **one)] * 2,
+        out_shape=[jax.ShapeDtypeStruct((half, w), BF)] * 2,
+        scratch_shapes=[
+            pltpu.VMEM((full, inner), BF), pltpu.VMEM((full, inner), BF), pltpu.VMEM((full, inner), BF),
+            pltpu.VMEM((inner, full), BF), pltpu.VMEM((full, inner), BF), pltpu.VMEM((full, inner), F32),
+            pltpu.VMEM((2, full, BQ), BF), pltpu.VMEM((full, inner), BF),
+            pltpu.VMEM((full, inner), F32), pltpu.VMEM((full, inner), F32)],
+        compiler_params=pltpu.CompilerParams(vmem_limit_bytes=62 * 1024 * 1024),
+    )(own, rec, do_o, do_r, o_o, o_r, r_o, r_r, e, erem)
 
 
 def matmul(left, right):
@@ -221,7 +476,7 @@
     return (row_grad, weight_grads)
 
 
-def body(clips, clip_count, cotangent, norm_gain, bias_d, bias_ff, w_qkv, w_o, w_up, w_down):
+def plain_body(clips, clip_count, cotangent, norm_gain, bias_d, bias_ff, w_qkv, w_o, w_up, w_down):
     shards = (w_qkv, w_o, w_up, w_down, norm_gain, bias_d, bias_ff)
     number = clips.shape[0]
     outputs = []
@@ -258,6 +513,172 @@
     return (jnp.stack(outputs), jnp.stack(row_grads)) + tuple(small_sums) + tuple(matrix_sums)
 
 
+def swap_core(x):
+    return lax.ppermute(x, "core", ((0, 1), (1, 0)))
+
+
+def swap_owner(x, sizes):
+    outer = sizes["outer"]
+    pairs = []
+    for k in range(outer):
+        pairs += [(4 * k, 4 * k), (4 * k + 1, 4 * k + 2), (4 * k + 2, 4 * k + 1), (4 * k + 3, 4 * k + 3)]
+    return lax.ppermute(x, ("outer", "core", "grp"), pairs)
+
+
+def two_halves(x, core, axis=0):
+    size = x.shape[axis] // 2
+    return (
+        lax.dynamic_slice_in_dim(x, core * size, size, axis),
+        lax.dynamic_slice_in_dim(x, (1 - core) * size, size, axis),
+    )
+
+
+def join_halves(mine, other, core, axis=0):
+    first = jnp.where(core == 0, mine, other)
+    second = jnp.where(core == 0, other, mine)
+    return jnp.concatenate([first, second], axis)
+
+
+def scatter_blocks(grad, sizes):
+    outer = sizes["outer"]
+    rows, cols = grad.shape
+    x = grad.astype(BF).reshape(2, rows // 2, 2 * outer, cols // (2 * outer)).transpose(2, 0, 1, 3)
+    x = x.reshape(2 * outer * 2, rows // 2, cols // (2 * outer))
+    return lax.psum_scatter(x, ("outer", "core", "grp"), scatter_dimension=0, tiled=True)[0].astype(F32)
+
+
+def gather_rows(shard):
+    core = lax.axis_index("core")
+    part = shard.shape[0] // 2
+    piece = lax.dynamic_slice_in_dim(shard, core * part, part, 0)
+    return lax.all_gather(piece, ("grp", "core"), axis=0, tiled=True)
+
+
+def body(sizes, clips, clip_count, cotangent, norm_gain, bias_d, bias_ff, w_qkv, w_o, w_up, w_down):
+    core = lax.axis_index("core")
+    slots, half, width = clips.shape
+    inner = width // 2
+    qkv_weight = gather_rows(w_qkv)
+    gains = lax.all_gather(norm_gain, "grp", axis=1, tiled=True).astype(F32)
+    biases = lax.all_gather(bias_d, "grp", axis=1, tiled=True).astype(F32)
+    bias_hidden = lax.all_gather(bias_ff, "grp", axis=0, tiled=True).astype(F32)
+    count = swap_owner(clip_count, sizes)[0]
+    out_weight = gather_rows(w_o)
+    up_weight = gather_rows(w_up)
+    down_weight = gather_rows(w_down)
+
+    qkv_parts = [two_halves(qkv_weight[:, i * width : (i + 1) * width], core, 1) for i in range(3)]
+    qkv_mine = jnp.concatenate([part[0] for part in qkv_parts], 1)
+    qkv_other = jnp.concatenate([part[1] for part in qkv_parts], 1)
+    zero = jnp.zeros((inner,), F32)
+    q_shift = two_halves(biases[1], core)
+    v_shift = two_halves(biases[2], core)
+    shift_mine = jnp.concatenate([q_shift[0], zero, v_shift[0]])
+    shift_other = jnp.concatenate([q_shift[1], zero, v_shift[1]])
+    out_mine, out_other = two_halves(out_weight, core)
+
+    inputs, normed, scaled1, inverse1 = [], [], [], []
+    saved, context_mine, context_other = [], [], []
+    for s in range(slots):
+        block = swap_owner(clips[s], sizes).astype(F32)
+        scaled, inverse, norm = layer_norm(block, gains[0], biases[0])
+        norm = norm.astype(BF)
+        other = (nn(norm, qkv_other) + shift_other).astype(BF)
+        received = swap_core(other)
+        mine = (nn(norm, qkv_mine) + shift_mine).astype(BF)
+        here, there, r_here, r_there, weights, weights_rem = attend(mine, received)
+        context_mine.append(here)
+        context_other.append(swap_core(there))
+        saved.append((mine, received, here, there, r_here, r_there, weights, weights_rem))
+        inputs.append(block)
+        normed.append(norm)
+        scaled1.append(scaled)
+        inverse1.append(inverse)
+    live = jnp.repeat((count > jnp.arange(slots)).astype(F32), half)[:, None]
+    cot = jnp.concatenate([swap_owner(cotangent[s], sizes) for s in range(slots)])
+    inputs = jnp.concatenate(inputs)
+    normed = jnp.concatenate(normed)
+    scaled1 = jnp.concatenate(scaled1)
+    inverse1 = jnp.concatenate(inverse1)
+    context_mine = jnp.concatenate(context_mine)
+    context_other = jnp.concatenate(context_other)
+
+    hidden = inputs + nn(context_mine, out_mine) + nn(context_other, out_other) + biases[3]
+    scaled2, inverse2, normed2 = layer_norm(hidden, gains[1], biases[4])
+    normed2 = normed2.astype(BF)
+    pre = nn(normed2, up_weight) + bias_hidden
+    active = jax.nn.gelu(pre, approximate=False).astype(BF)
+    result = ((hidden + nn(active, down_weight) + biases[5]) * live).astype(BF)
+    block_out = jnp.stack([swap_owner(result[s * half : (s + 1) * half], sizes) for s in range(slots)])
+
+    d_out = cot * live.astype(BF)
+    d_out_f = d_out.astype(F32)
+    grad_down = scatter_blocks(tn(active, d_out), sizes)
+    grad_b2 = jnp.sum(d_out_f, 0)
+    d_act = nt(d_out, down_weight)
+    unused, gelu_pull = jax.vjp(lambda x: jax.nn.gelu(x, approximate=False), pre)
+    d_pre = gelu_pull(d_act)[0].astype(BF)
+    grad_up = scatter_blocks(tn(normed2, d_pre), sizes)
+    grad_bias_hidden = jnp.sum(d_pre.astype(F32), 0)
+    d_norm2 = nt(d_pre, up_weight)
+    d_hidden = d_out_f + norm_back(scaled2, inverse2, gains[1], d_norm2)
+    grad_g2 = jnp.sum(d_norm2 * scaled2, 0)
+    grad_beta2 = jnp.sum(d_norm2, 0)
+    d_branch = d_hidden.astype(BF)
+    grad_bo = jnp.sum(d_branch.astype(F32), 0)
+    d_context_other = swap_core(nt(d_branch, out_other).astype(BF))
+    d_context_mine = nt(d_branch, out_mine).astype(BF)
+    grad_out = scatter_blocks(
+        join_halves(tn(context_mine, d_branch), tn(context_other, d_branch), core), sizes
+    )
+
+    d_mine, d_other = [], []
+    for s in range(slots):
+        rows = slice(s * half, (s + 1) * half)
+        mine, received, here, there, r_here, r_there, weights, weights_rem = saved[s]
+        d_here, d_there = attend_back(
+            mine, received, d_context_mine[rows], d_context_other[rows], here, there, r_here, r_there, weights, weights_rem
+        )
+        d_mine.append(d_here)
+        d_other.append(swap_core(d_there))
+    d_mine = jnp.concatenate(d_mine)
+    d_other = jnp.concatenate(d_other)
+    d_norm1 = nt(d_mine, qkv_mine) + nt(d_other, qkv_other)
+    grad_mine = tn(normed, d_mine)
+    grad_other = tn(normed, d_other)
+    grad_qkv = scatter_blocks(
+        jnp.concatenate(
+            [
+                join_halves(grad_mine[:, i * inner : (i + 1) * inner], grad_other[:, i * inner : (i + 1) * inner], core, 1)
+                for i in range(3)
+            ],
+            1,
+        ),
+        sizes,
+    )
+    sum_mine = jnp.sum(d_mine.astype(F32), 0)
+    sum_other = jnp.sum(d_other.astype(F32), 0)
+    grad_bq = join_halves(sum_mine[:inner], sum_other[:inner], core)
+    grad_bv = join_halves(sum_mine[2 * inner :], sum_other[2 * inner :], core)
+    row_grad = (d_hidden + norm_back(scaled1, inverse1, gains[0], d_norm1)).astype(BF)
+    grad_g1 = jnp.sum(d_norm1 * scaled1, 0)
+    grad_beta1 = jnp.sum(d_norm1, 0)
+    input_grad = jnp.stack(
+        [swap_owner(row_grad[s * half : (s + 1) * half], sizes).astype(F32) for s in range(slots)]
+    )
+    small = jnp.concatenate(
+        [
+            jnp.stack([grad_g1, grad_g2, grad_beta1, grad_bq, grad_bv, grad_bo, grad_beta2, grad_b2]),
+            grad_bias_hidden.reshape(4, width),
+        ]
+    )
+    small = lax.psum(small, ("outer", "core", "grp"))
+    x = lax.axis_index("grp")
+    columns = lax.dynamic_slice_in_dim(small[:8], x * inner, inner, 1)
+    hidden_part = lax.dynamic_slice_in_dim(small[8:], 2 * x, 2, 0).reshape(-1)
+    return (block_out, input_grad, columns[:2], columns[2:], hidden_part, grad_qkv, grad_out, grad_up, grad_down)
+
+
 def solution(mesh):
     in_specs = (
         P("rep", "grp", None),
@@ -282,4 +703,15 @@
         P("grp", "rep"),
         P("grp", "rep"),
     )
-    return jax.shard_map(body, mesh=mesh, in_specs=in_specs, out_specs=out_specs, check_vma=False)
+    if mesh.shape["grp"] != 2:
+        return jax.shard_map(plain_body, mesh=mesh, in_specs=in_specs, out_specs=out_specs, check_vma=False)
+    outer = mesh.shape["rep"] // 2
+    split = Mesh(mesh.devices.reshape(outer, 2, 2), ("outer", "core", "grp"))
+    rep = lambda spec: P(*[("outer", "core") if axis == "rep" else axis for axis in spec])
+    return jax.shard_map(
+        functools.partial(body, {"outer": outer}),
+        mesh=split,
+        in_specs=tuple(rep(spec) for spec in in_specs),
+        out_specs=tuple(rep(spec) for spec in out_specs),
+        check_vma=False,
+    )

time: 2450 us -> 1460 us (0.60)
  matrix products: 1110 us -> 388 us
  waiting for transfers between devices: 836 us -> 165 us
  Pallas kernels: 0 us -> 262 us
  blocking collectives: 66 us -> 316 us
  other arithmetic: 241 us -> 89.9 us
  starting transfers between devices: 2.08 us -> 65.1 us
    dot_general x51 -> x22, matrix products: 997 us -> 388 us  [dot(): return lax.dot_general(a, b, (dims, ((), ())), preferred_element_type=F32)]
    reduce_scatter x6 -> x4, waiting for transfers between devices: 435 us -> 10.5 us  [scatter_blocks(): lax.psum_scatter(x, ('outer', 'core', 'grp'), scatter_dimension=0, tiled=...]
    pallas_call x0 -> x6, Pallas kernels: none -> 262 us  [the longest x3 158 us: attend_back(): pl.pallas_call(functools.partial(attend_back_kernel, nb=nb, np_=np_, rem=...]
    unnamed x36 -> x8, waiting for transfers between devices: 203 us -> 0.13 us
    all_gather x10 -> x4, waiting for transfers between devices: 198 us -> 0.03 us  [gather_rows(): return lax.all_gather(piece, ('grp', 'core'), axis=0, tiled=True)]
    convert_element_type x7 -> x11, other arithmetic: 212 us -> 29.7 us  [the longest x1 11.8 us: body(): (d_hidden + norm_back(scaled1, inverse1, gains[0], d_norm1)).astype(BF)]
    psum x1, blocking collectives: 49.1 us -> 208 us  [body(): small = lax.psum(small, ('outer', 'core', 'grp'))]
    ppermute x0 -> x23, waiting for transfers between devices: none -> 154 us  [the longest x13 154 us: swap_owner(): return lax.ppermute(x, ('outer', 'core', 'grp'), pairs)]
  transfers between devices with their start and end apart: 26 -> 31, of which waited for: 14 -> 5; matrix products, arithmetic and copies ran while one was open for 54% -> 36% of each run, Pallas kernels for 0% -> 18%
where the time goes in v1:
time: 1460 us
  matrix products  388 us (27%)
  blocking collectives  316 us (22%)
  Pallas kernels  262 us (18%)
  waiting for transfers between devices  165 us (11%)
  local copies, waits for them, and re-layouts  157 us (11%)
  other arithmetic  89.9 us (6%)
  starting transfers between devices  65.1 us (4%)
  between operations  15.6 us (1%)
    dot_general x22, matrix products, dot(): return lax.dot_general(a, b, (dims, ((), ())), preferred_element_type=F32)  388 us
    psum x1, blocking collectives, body(): small = lax.psum(small, ('outer', 'core', 'grp'))  208 us
    pallas_call x3, Pallas kernels, attend_back(): pl.pallas_call(functools.partial(attend_back_kernel, nb=nb, np_=np_, rem=...  158 us
    ppermute x13, waiting for transfers between devices, swap_owner(): return lax.ppermute(x, ('outer', 'core', 'grp'), pairs)  154 us
    pallas_call x3, Pallas kernels, attend(): pl.pallas_call(functools.partial(attend_kernel, nb=nb, np_=np_, rem=rem),...  103 us
    all_gather x1, blocking collectives, body(): gains = lax.all_gather(norm_gain, 'grp', axis=1, tiled=True).astype(F32)  92.2 us
    ppermute x13, starting transfers between devices, swap_owner(): return lax.ppermute(x, ('outer', 'core', 'grp'), pairs)  37 us
    transpose x5, local copies, waits for them, and re-layouts, scatter_blocks(): grad.astype(BF).reshape(2, rows // 2, 2 * outer, cols // (2 * outer))  36.7 us
  transfers between devices with their start and end apart: 31, of which 5 were waited for; matrix products, arithmetic and copies ran while one was open for 36% of the time, Pallas kernels for 18%

profile of v1, /device:TPU:9, one launch (start us, length us, event | category | flops | bytes accessed | tf_op | source)
XLA Modules:
  0.0 1457.6 jit_solution(15594159036592559453)
XLA Ops:
  28.2 92.2 %all_gather.21 = bf16[2,1024]{1,0:T(2,128)(2,1)S(1)} all-gather(bf16[2,512]{1,0:T(2,128)(2,1)S(1)} %copy-done.54), channel_id=1, replica_groups=mesh['outer'=8,'core'=2,'grp'=2] {'grp'}, dimensions={1}, use_global_device_ids=true | all-gather | bytes 6144 | tf_op jit(solution)/shard_map/all_gather | solution.py:562
  219.4 30.3 %shard_map.169 = (bf16[784,512]{1,0:T(8,128)(2,1)}, bf16[784,512]{1,0:T(8,128)(2,1)}, f32[784,512]{1,0:T(8,128)}, f32[784,512]{1,0:T(8,128)}, bf16[12,2,1568,512...) custom-call(bf16[784,1536]{1,0:T(8,128)(2,1)} %add_convert_fusion.8.own, bf16[784,1536]{1,0:T(8,128)(2,1)} %collective-permute-done.3.rec), custom_call_target="tpu_custom_call" | custom-call | tf_op jit(solution)/shard_map/pallas_call | solution.py:149
  263.5 43.0 %shard_map.171 = (bf16[784,512]{1,0:T(8,128)(2,1)}, bf16[784,512]{1,0:T(8,128)(2,1)}, f32[784,512]{1,0:T(8,128)}, f32[784,512]{1,0:T(8,128)}, bf16[12,2,1568,512...) custom-call(bf16[784,1536]{1,0:T(8,128)(2,1)} %add_convert_fusion.4.own, bf16[784,1536]{1,0:T(8,128)(2,1)} %collective-permute-done.5.rec), custom_call_target="tpu_custom_call" | custom-call | tf_op jit(solution)/shard_map/pallas_call | solution.py:149
  306.6 30.0 %shard_map.170 = (bf16[784,512]{1,0:T(8,128)(2,1)}, bf16[784,512]{1,0:T(8,128)(2,1)}, f32[784,512]{1,0:T(8,128)}, f32[784,512]{1,0:T(8,128)}, bf16[12,2,1568,512...) custom-call(bf16[784,1536]{1,0:T(8,128)(2,1)} %add_convert_fusion.6.own, bf16[784,1536]{1,0:T(8,128)(2,1)} %collective-permute-done.4.rec), custom_call_target="tpu_custom_call" | custom-call | tf_op jit(solution)/shard_map/pallas_call | solution.py:149
  366.1 109.0 %multiply_convert_fusion = (bf16[2352,4096]{1,0:T(8,128)(2,1)}, f32[2352,4096]{1,0:T(8,128)}, f32[2352,4096]{1,0:T(8,128)}) fusion(f32[4096]{0:T(1024)S(1)} %convert_element_type.153, bf16[1024,4096]{1,0:T(8,128)(2,1)} %all-gather.9.cloned.1.call-done, f32[2352,1024]{1,0:T(8,128)} %copy-done.2, f32[1024]{0:T(1024)S(1)} %bitcast.140, f32[1024]{0:T(1024)S(1)} %bitcast.128, ...), kind=kOutput, calls=%fused_computation.4 | convolution fusion | flops 20377878528 | bytes 114403712 | tf_op jit(solution)/shard_map/dot_general | solution.py:25
  475.2 47.8 %convert_reduce_fusion = (f32[4096]{0:T(1024)}, bf16[2352,4096]{1,0:T(8,128)(2,1)}) fusion(f32[2352,4096]{1,0:T(8,128)} %get-tuple-element.69, bf16[4096,1024]{1,0:T(8,128)(2,1)} %all-gather.11.cloned.1.call-done, bf16[784,1024]{1,0:T(8,128)(2,1)} %collective-permute-done.15, bf16[784,1024]{1,0:T(8,128)(2,1)} %collective-permute-done.14, ...), kind=kOutput, calls=%fused_computation.2 | convolution fusion | flops 19913043968 | bytes 109580896 | tf_op jit(solution)/shard_map/dot_general | solution.py:25
  522.9 32.7 %multiply_reduce_fusion = (f32[1024]{0:T(1024)}, f32[2352]{0:T(1024)S(1)}, f32[2352]{0:T(1024)S(1)}, f32[1024]{0:T(1024)}, f32[2352,1024]{1,0:T(8,128)}) fusion(f32[2352,1024]{1,0:T(8,128)} %copy-done.2, f32[2352]{0:T(1024)S(1)} %add_rsqrt_fusion, f32[2352]{0:T(1024)S(1)} %broadcast_multiply_fusion.4, f32[1024]{0:T(1024)S(1)} %bitcast.129, ...), kind=kOutput, calls=%fused_computation.27 | convolution fusion | flops 19751677952 | bytes 46973696 | tf_op jit(solution)/shard_map/dot_general | solution.py:25
  555.7 13.5 convert_reduce_fusion.4
  573.6 11.9 collective-permute-start.16
  609.2 52.8 %shard_map.172 = (bf16[784,1536]{1,0:T(8,128)(2,1)}, bf16[784,1536]{1,0:T(8,128)(2,1)}) custom-call(bf16[784,1536]{1,0:T(8,128)(2,1)} %add_convert_fusion.8.own, bf16[784,1536]{1,0:T(8,128)(2,1)} %collective-permute-done.3.rec, bf16[784,512]{1,0:T(8,128)(2,1)} %get-tuple-element.91.do_o, bf16[784,512]{1,0:T(8,128)(2,1)} %get-tuple-element.88.do_r, ...), custom_call_target="tpu_custom_call" | custom-call | tf_op jit(solution)/shard_map/pallas_call | solution.py:252
  665.4 53.0 %shard_map.174 = (bf16[784,1536]{1,0:T(8,128)(2,1)}, bf16[784,1536]{1,0:T(8,128)(2,1)}) custom-call(bf16[784,1536]{1,0:T(8,128)(2,1)} %add_convert_fusion.4.own, bf16[784,1536]{1,0:T(8,128)(2,1)} %collective-permute-done.5.rec, bf16[784,512]{1,0:T(8,128)(2,1)} %get-tuple-element.89.do_o, bf16[784,512]{1,0:T(8,128)(2,1)} %get-tuple-element.86.do_r, ...), custom_call_target="tpu_custom_call" | custom-call | tf_op jit(solution)/shard_map/pallas_call | solution.py:252
  718.4 52.7 %shard_map.173 = (bf16[784,1536]{1,0:T(8,128)(2,1)}, bf16[784,1536]{1,0:T(8,128)(2,1)}) custom-call(bf16[784,1536]{1,0:T(8,128)(2,1)} %add_convert_fusion.6.own, bf16[784,1536]{1,0:T(8,128)(2,1)} %collective-permute-done.4.rec, bf16[784,512]{1,0:T(8,128)(2,1)} %get-tuple-element.90.do_o, bf16[784,512]{1,0:T(8,128)(2,1)} %get-tuple-element.87.do_r, ...), custom_call_target="tpu_custom_call" | custom-call | tf_op jit(solution)/shard_map/pallas_call | solution.py:252
  834.6 33.5 %convolution_convert_fusion.1 = bf16[1024,4096]{1,0:T(8,128)(2,1)} fusion(bf16[2352,4096]{1,0:T(8,128)(2,1)} %get-tuple-element.130, f32[2352,1024]{1,0:T(8,128)} %copy-done.2, f32[1024]{0:T(1024)S(1)} %bitcast.141, f32[1024]{0:T(1024)S(1)} %bitcast.131, f32[2352]{0:T(1024)S(1)} %add_rsqrt_fusion, f32[2352]{0:T(1024)S(1)} %broadcast_multiply_fusion.4), kind=kOutput, calls=%fused_computation.40 | convolution fusion | flops 19746242560 | bytes 37316992 | tf_op jit(solution)/shard_map/dot_general | solution.py:25
  896.2 29.1 %convolution_convert_fusion = bf16[4096,1024]{1,0:T(8,128)(2,1)} fusion(bf16[2352,4096]{1,0:T(8,128)(2,1)} %get-tuple-element.68, bf16[784,1024]{1,0:T(8,128)(2,1)} %collective-permute-done.15, bf16[784,1024]{1,0:T(8,128)(2,1)} %collective-permute-done.14, bf16[784,1024]{1,0:T(8,128)(2,1)} %collective-permute-done.13, bf16[2352]{0:T(1024)(128)(2,1)S(1)} %copy-done.43), kind=kOutput, calls=%fused_computation.39 | convolution fusion | flops 19753467904 | bytes 32477792 | tf_op jit(solution)/shard_map/dot_general | solution.py:25
  925.4 11.8 copy.39
  937.2 14.5 reshape.180
  963.1 26.4 %multiply_convert_fusion.1 = bf16[2352,1024]{1,0:T(8,128)(2,1)S(1)} fusion(f32[2352,1024]{1,0:T(8,128)} %copy-done.2, bf16[2352,4096]{1,0:T(8,128)(2,1)} %get-tuple-element.68, bf16[4096,1024]{1,0:T(8,128)(2,1)} %all-gather.11.cloned.1.call-done, f32[2352]{0:T(1024)S(1)} %copy-done.35, f32[1024]{0:T(1024)S(1)} %bitcast.139), kind=kOutput, calls=%fused_computation.32 | convolution fusion | flops 19739639808 | bytes 42120384 | tf_op jit(solution)/shard_map/dot_general | solution.py:25
  999.7 49.1 %collective-permute-done.10 = bf16[784,1024]{1,0:T(8,128)(2,1)} collective-permute-done((bf16[784,1024]{1,0:T(8,128)(2,1)}, bf16[784,1024]{1,0:T(8,128)(2,1)}, u32[]{:S(2)}, u32[]{:S(2)}) %collective-permute-start.10) | collective-permute-done | bytes 1605664 | tf_op jit(solution)/shard_map/ppermute | solution.py:525
  1048.8 51.6 %collective-permute-done.11 = bf16[784,1024]{1,0:T(8,128)(2,1)} collective-permute-done((bf16[784,1024]{1,0:T(8,128)(2,1)}, bf16[784,1024]{1,0:T(8,128)(2,1)}, u32[]{:S(2)}, u32[]{:S(2)}) %collective-permute-start.11) | collective-permute-done | bytes 1605664 | tf_op jit(solution)/shard_map/ppermute | solution.py:525
  1100.4 51.5 %collective-permute-done.12 = bf16[784,1024]{1,0:T(8,128)(2,1)} collective-permute-done((bf16[784,1024]{1,0:T(8,128)(2,1)S(1)}, bf16[784,1024]{1,0:T(8,128)(2,1)}, u32[]{:S(2)}, u32[]{:S(2)}) %collective-permute-start.12) | collective-permute-done | bytes 1605664 | tf_op jit(solution)/shard_map/ppermute | solution.py:525
  1157.3 12.3 fusion.32
  1169.7 17.0 %multiply_reduce_fusion.1 = (f32[1024]{0:T(1024)S(1)}, f32[2352]{0:T(1024)S(1)}, f32[2352]{0:T(1024)S(1)}, f32[1024]{0:T(1024)S(1)}, f32[2352,1024]{1,0:T(8,128)}) fusion(f32[784,1024]{1,0:T(8,128)} %get-tuple-element.104, f32[784,1024]{1,0:T(8,128)} %get-tuple-element.102, f32[784,1024]{1,0:T(8,128)} %get-tuple-element.100, f32[1024]{0:T(1024)S(1)} %bitcast.120, ...), kind=kOutput, calls=%fused_computation.28 | convolution fusion | flops 7432266752 | bytes 39303552 | tf_op jit(solution)/shard_map/dot_general | solution.py:25
  1186.7 11.8 add_convert_fusion.1
  1218.0 207.6 %psum.7 = f32[12,1024]{1,0:T(8,128)S(1)} all-reduce(f32[12,1024]{1,0:T(8,128)S(1)} %concatenate.70), channel_id=1, replica_groups=mesh['outer'=8,'core'=2,'grp'=2] {'outer','core','grp'}, use_global_device_ids=true, to_apply=%region_21.22 | all-reduce | flops 12288 | bytes 98304 | tf_op jit(solution)/shard_map/psum | solution.py:675
  (310 shorter events, 356.8 us)
Async XLA Ops:
  7.2 138.3 %all-gather.5.cloned.1.call-start = ((), (), s32[]{:S(2)}) async-start(), calls=%async_computation.4 | async-start | bytes 7864320 | tf_op jit(solution)/shard_map/all_gather | solution.py:554
  10.1 330.1 %all-gather.7.cloned.1.call-start = ((), (), s32[]{:S(2)}) async-start(), calls=%async_computation.5 | async-start | bytes 2621440 | tf_op jit(solution)/shard_map/all_gather | solution.py:554
  11.0 355.1 %all-gather.9.cloned.1.call-start = ((), (), s32[]{:S(2)}) async-start(), calls=%async_computation.6 | async-start | bytes 10485760 | tf_op jit(solution)/shard_map/all_gather | solution.py:554
  14.2 461.0 %all-gather.11.cloned.1.call-start = ((), (), s32[]{:S(2)}) async-start(), calls=%async_computation.7 | async-start | bytes 10485760 | tf_op jit(solution)/shard_map/all_gather | solution.py:554
  19.0 106.6 %collective-permute-start.1 = (bf16[784,1024]{1,0:T(8,128)(2,1)}, bf16[784,1024]{1,0:T(8,128)(2,1)S(1)}, u32[]{:S(2)}, u32[]{:S(2)}) collective-permute-start(bf16[784,1024]{1,0:T(8,128)(2,1)} %get-tuple-element.85), channel_id=1, source_target_pairs={{0,0},{1,2},{2,1},{3,3},{4,4},{5,6},{6,5},{7,7},{8,8},{9,10},{10,9... | collective-permute-start | bytes 4816904 | tf_op jit(solution)/shard_map/ppermute | solution.py:525
  22.6 103.2 %collective-permute-start = (bf16[784,1024]{1,0:T(8,128)(2,1)}, bf16[784,1024]{1,0:T(8,128)(2,1)}, u32[]{:S(2)}, u32[]{:S(2)}) collective-permute-start(bf16[784,1024]{1,0:T(8,128)(2,1)} %get-tuple-element.84), channel_id=1, source_target_pairs={{0,0},{1,2},{2,1},{3,3},{4,4},{5,6},{6,5},{7,7},{8,8},{9,10},{10,9... | collective-permute-start | bytes 4816904 | tf_op jit(solution)/shard_map/ppermute | solution.py:525
  24.6 103.0 %collective-permute-start.2 = (bf16[784,1024]{1,0:T(8,128)(2,1)}, bf16[784,1024]{1,0:T(8,128)(2,1)}, u32[]{:S(2)}, u32[]{:S(2)}) collective-permute-start(bf16[784,1024]{1,0:T(8,128)(2,1)} %get-tuple-element.83), channel_id=1, source_target_pairs={{0,0},{1,2},{2,1},{3,3},{4,4},{5,6},{6,5},{7,7},{8,8},{9,10},{10,9... | collective-permute-start | bytes 4816904 | tf_op jit(solution)/shard_map/ppermute | solution.py:525
  156.2 150.4 %collective-permute-start.4 = (bf16[784,1536]{1,0:T(8,128)(2,1)}, bf16[784,1536]{1,0:T(8,128)(2,1)}, u32[]{:S(2)}, u32[]{:S(2)}) collective-permute-start(bf16[784,1536]{1,0:T(8,128)(2,1)} %add_convert_fusion.5), channel_id=1, source_target_pairs={{0,2},{2,0},{1,3},{3,1},{4,6},{6,4},{5,7},{7,5},{8,10},{10,8},{9,1... | collective-permute-start | bytes 7225352 | tf_op jit(solution)/shard_map/ppermute | solution.py:517
  167.3 96.2 %collective-permute-start.5 = (bf16[784,1536]{1,0:T(8,128)(2,1)}, bf16[784,1536]{1,0:T(8,128)(2,1)}, u32[]{:S(2)}, u32[]{:S(2)}) collective-permute-start(bf16[784,1536]{1,0:T(8,128)(2,1)} %add_convert_fusion.3), channel_id=1, source_target_pairs={{0,2},{2,0},{1,3},{3,1},{4,6},{6,4},{5,7},{7,5},{8,10},{10,8},{9,1... | collective-permute-start | bytes 7225352 | tf_op jit(solution)/shard_map/ppermute | solution.py:517
  170.1 304.9 %collective-permute-start.13 = (bf16[784,1024]{1,0:T(8,128)(2,1)}, bf16[784,1024]{1,0:T(8,128)(2,1)}, u32[]{:S(2)}, u32[]{:S(2)}) collective-permute-start(bf16[784,1024]{1,0:T(8,128)(2,1)} %get-tuple-element.77), channel_id=1, source_target_pairs={{0,0},{1,2},{2,1},{3,3},{4,4},{5,6},{6,5},{7,7},{8,8},{9,10},{10,9... | collective-permute-start | bytes 4816904 | tf_op jit(solution)/shard_map/ppermute | solution.py:525
  179.1 1033.1 %reduce-scatter.7.cloned.1.call-start = ((), (), s32[]{:S(2)}) async-start(), calls=%async_computation.9 | async-start | bytes 2162688 | tf_op jit(solution)/shard_map/reduce_scatter | solution.py:547
  192.7 282.4 %collective-permute-start.14 = (bf16[784,1024]{1,0:T(8,128)(2,1)}, bf16[784,1024]{1,0:T(8,128)(2,1)}, u32[]{:S(2)}, u32[]{:S(2)}) collective-permute-start(bf16[784,1024]{1,0:T(8,128)(2,1)} %get-tuple-element.79), channel_id=1, source_target_pairs={{0,0},{1,2},{2,1},{3,3},{4,4},{5,6},{6,5},{7,7},{8,8},{9,10},{10,9... | collective-permute-start | bytes 4816904 | tf_op jit(solution)/shard_map/ppermute | solution.py:525
  249.6 99.0 %collective-permute-start.6 = (bf16[784,512]{1,0:T(8,128)(2,1)}, bf16[784,512]{1,0:T(8,128)(2,1)S(1)}, u32[]{:S(2)}, u32[]{:S(2)}) collective-permute-start(bf16[784,512]{1,0:T(8,128)(2,1)} %get-tuple-element.36.o_r), channel_id=1, source_target_pairs={{0,2},{2,0},{1,3},{3,1},{4,6},{6,4},{5,7},{7,5},{8,10},{10,8},{9,1... | collective-permute-start | bytes 2408456 | tf_op jit(solution)/shard_map/ppermute | solution.py:517
  348.6 126.5 %collective-permute-start.15 = (bf16[784,1024]{1,0:T(8,128)(2,1)}, bf16[784,1024]{1,0:T(8,128)(2,1)}, u32[]{:S(2)}, u32[]{:S(2)}) collective-permute-start(bf16[784,1024]{1,0:T(8,128)(2,1)} %get-tuple-element.78), channel_id=1, source_target_pairs={{0,0},{1,2},{2,1},{3,3},{4,4},{5,6},{6,5},{7,7},{8,8},{9,10},{10,9... | collective-permute-start | bytes 4816904 | tf_op jit(solution)/shard_map/ppermute | solution.py:525
  599.2 835.4 %reduce-scatter.5.cloned.1.call-start = ((), (), s32[]{:S(2)}) async-start(), calls=%async_computation.8 | async-start | bytes 6488064 | tf_op jit(solution)/shard_map/reduce_scatter | solution.py:547
  718.4 70.1 %collective-permute-start.19 = (bf16[784,1536]{1,0:T(8,128)(2,1)}, bf16[784,1536]{1,0:T(8,128)(2,1)}, u32[]{:S(2)}, u32[]{:S(2)}) collective-permute-start(bf16[784,1536]{1,0:T(8,128)(2,1)} %get-tuple-element.56), channel_id=1, source_target_pairs={{0,2},{2,0},{1,3},{3,1},{4,6},{6,4},{5,7},{7,5},{8,10},{10,8},{9,1... | collective-permute-start | bytes 7225352 | tf_op jit(solution)/shard_map/ppermute | solution.py:517
  833.9 602.4 %reduce-scatter.9.cloned.1.call-start = ((), (), s32[]{:S(2)}) async-start(), calls=%async_computation.10 | async-start | bytes 8650752 | tf_op jit(solution)/shard_map/reduce_scatter | solution.py:547
  895.6 553.0 %reduce-scatter.11.cloned.1.call-start = ((), (), s32[]{:S(2)}) async-start(), calls=%async_computation.11 | async-start | bytes 8650752 | tf_op jit(solution)/shard_map/reduce_scatter | solution.py:547
  992.0 56.8 %collective-permute-start.10 = (bf16[784,1024]{1,0:T(8,128)(2,1)}, bf16[784,1024]{1,0:T(8,128)(2,1)}, u32[]{:S(2)}, u32[]{:S(2)}) collective-permute-start(bf16[784,1024]{1,0:T(8,128)(2,1)} %get-tuple-element.80), channel_id=1, source_target_pairs={{0,0},{1,2},{2,1},{3,3},{4,4},{5,6},{6,5},{7,7},{8,8},{9,10},{10,9... | collective-permute-start | bytes 4816904 | tf_op jit(solution)/shard_map/ppermute | solution.py:525
  993.9 106.6 %collective-permute-start.11 = (bf16[784,1024]{1,0:T(8,128)(2,1)}, bf16[784,1024]{1,0:T(8,128)(2,1)}, u32[]{:S(2)}, u32[]{:S(2)}) collective-permute-start(bf16[784,1024]{1,0:T(8,128)(2,1)} %get-tuple-element.82), channel_id=1, source_target_pairs={{0,0},{1,2},{2,1},{3,3},{4,4},{5,6},{6,5},{7,7},{8,8},{9,10},{10,9... | collective-permute-start | bytes 4816904 | tf_op jit(solution)/shard_map/ppermute | solution.py:525
  997.5 154.4 %collective-permute-start.12 = (bf16[784,1024]{1,0:T(8,128)(2,1)S(1)}, bf16[784,1024]{1,0:T(8,128)(2,1)}, u32[]{:S(2)}, u32[]{:S(2)}) collective-permute-start(bf16[784,1024]{1,0:T(8,128)(2,1)S(1)} %get-tuple-element.81), channel_id=1, source_target_pairs={{0,0},{1,2},{2,1},{3,3},{4,4},{5,6},{6,5},{7,7},{8,8},{9,10},{10,9... | collective-permute-start | bytes 4816904 | tf_op jit(solution)/shard_map/ppermute | solution.py:525
  1200.9 226.6 %collective-permute-start.20 = (bf16[784,1024]{1,0:T(8,128)(2,1)}, bf16[784,1024]{1,0:T(8,128)(2,1)}, u32[]{:S(2)}, u32[]{:S(2)}) collective-permute-start(bf16[784,1024]{1,0:T(8,128)(2,1)} %get-tuple-element.74), channel_id=1, source_target_pairs={{0,0},{1,2},{2,1},{3,3},{4,4},{5,6},{6,5},{7,7},{8,8},{9,10},{10,9... | collective-permute-start | bytes 4816904 | tf_op jit(solution)/shard_map/ppermute | solution.py:525
  1205.4 222.1 %collective-permute-start.21 = (bf16[784,1024]{1,0:T(8,128)(2,1)}, bf16[784,1024]{1,0:T(8,128)(2,1)}, u32[]{:S(2)}, u32[]{:S(2)}) collective-permute-start(bf16[784,1024]{1,0:T(8,128)(2,1)} %get-tuple-element.76), channel_id=1, source_target_pairs={{0,0},{1,2},{2,1},{3,3},{4,4},{5,6},{6,5},{7,7},{8,8},{9,10},{10,9... | collective-permute-start | bytes 4816904 | tf_op jit(solution)/shard_map/ppermute | solution.py:525
  1207.4 220.1 %collective-permute-start.22 = (bf16[784,1024]{1,0:T(8,128)(2,1)S(1)}, bf16[784,1024]{1,0:T(8,128)(2,1)}, u32[]{:S(2)}, u32[]{:S(2)}) collective-permute-start(bf16[784,1024]{1,0:T(8,128)(2,1)S(1)} %get-tuple-element.75), channel_id=1, source_target_pairs={{0,0},{1,2},{2,1},{3,3},{4,4},{5,6},{6,5},{7,7},{8,8},{9,10},{10,9... | collective-permute-start | bytes 4816904 | tf_op jit(solution)/shard_map/ppermute | solution.py:525
  (69 other events, 1316.7 us)
Sparse Core Ops, SparseCore 0:
  10.2 64.1 all-gather.4
  76.5 28.0 all-gather.6
  106.2 61.8 all-gather.8
  179.3 82.8 all-gather.10
  599.3 145.2 reduce-scatter.6
  834.0 137.1 reduce-scatter.4
  973.5 238.5 reduce-scatter.8
  1214.4 234.0 reduce-scatter.10

commit v2 on v1

--- a/solution.py
+++ b/solution.py
@@ -16,8 +16,10 @@
 BF = jnp.bfloat16
 LOG2E = 1.4426950408889634
 SCALE = HD ** -0.5
+AXES = ("z", "mid", "core", "grp")
 BQ = 512
 TK = 224
+COST = 0.4
 LIMIT = 70.0
 
 
@@ -156,6 +158,7 @@
         scratch_shapes=[
             pltpu.VMEM((full, inner), BF), pltpu.VMEM((full, inner), BF), pltpu.VMEM((2 * np_, 128, full), BF),
             pltpu.VMEM((full, inner), BF), pltpu.VMEM((full, inner), F32), pltpu.SMEM((1,), jnp.int32)],
+        cost_estimate=pl.CostEstimate(flops=int(3.5e10 * COST), bytes_accessed=0, transcendentals=0),
         compiler_params=pltpu.CompilerParams(vmem_limit_bytes=60 * 1024 * 1024),
     )(own, rec)
 
@@ -239,7 +242,7 @@
             dst[:, inner:2 * inner] = (dk_s[rows] * SCALE).astype(BF)
             dst[:, 2 * inner:] = dv_s[rows].astype(BF)
 
-def attend_back(own, rec, do_o, do_r, o_o, o_r, r_o, r_r, e, erem):
+def attend_back(slot, own, rec, do_o, do_r, o_o, o_r, r_o, r_r, e, erem):
     half, w = own.shape
     inner = w // 3
     np_ = inner // 128
@@ -252,7 +255,9 @@
     return pl.pallas_call(
         functools.partial(attend_back_kernel, nb=nb, np_=np_, rem=rem),
         grid=(last + 1,),
-        in_specs=[whole((half, w), **one)] * 2 + [whole((half, inner), **one)] * 6
+        in_specs=[whole((half, w), **one)] * 2
+        + [whole((half, inner), **one), pl.BlockSpec((None, half, inner), lambda t: (slot, 0, 0), **one)]
+        + [whole((half, inner), **one)] * 4
         + [pl.BlockSpec((1, 2, full, BQ), lambda t: (jnp.minimum(t, last - 1), 0, 0, 0)), whole(erem.shape, **one)],
         out_specs=[whole((half, w), **one)] * 2,
         out_shape=[jax.ShapeDtypeStruct((half, w), BF)] * 2,
@@ -261,6 +266,7 @@
             pltpu.VMEM((inner, full), BF), pltpu.VMEM((full, inner), BF), pltpu.VMEM((full, inner), F32),
             pltpu.VMEM((2, full, BQ), BF), pltpu.VMEM((full, inner), BF),
             pltpu.VMEM((full, inner), F32), pltpu.VMEM((full, inner), F32)],
+        cost_estimate=pl.CostEstimate(flops=int(6e10 * COST), bytes_accessed=0, transcendentals=0),
         compiler_params=pltpu.CompilerParams(vmem_limit_bytes=62 * 1024 * 1024),
     )(own, rec, do_o, do_r, o_o, o_r, r_o, r_r, e, erem)
 
@@ -513,170 +519,759 @@
     return (jnp.stack(outputs), jnp.stack(row_grads)) + tuple(small_sums) + tuple(matrix_sums)
 
 
-def swap_core(x):
-    return lax.ppermute(x, "core", ((0, 1), (1, 0)))
-
-
-def swap_owner(x, sizes):
-    outer = sizes["outer"]
+def row_stats(values):
+    centred = values - jnp.mean(values, -1, keepdims=True)
+    inverse = lax.rsqrt(jnp.mean(centred * centred, -1, keepdims=True) + EPSILON)
+    return centred * inverse, inverse
+
+
+def whole(shape, **kw):
+    return pl.BlockSpec(shape, lambda *_: (0,) * len(shape), **kw)
+
+
+def call(kernel, ids, grid, in_specs, out_specs, out_shape, args, scratch=(), flops=0, limit=60, aliases=()):
+    return pl.pallas_call(
+        kernel,
+        grid_spec=pltpu.PrefetchScalarGridSpec(
+            num_scalar_prefetch=1, grid=grid, in_specs=in_specs, out_specs=out_specs, scratch_shapes=list(scratch)
+        ),
+        out_shape=out_shape,
+        cost_estimate=pl.CostEstimate(flops=int(flops * COST), bytes_accessed=0, transcendentals=0),
+        input_output_aliases=dict(aliases),
+        compiler_params=pltpu.CompilerParams(vmem_limit_bytes=limit * 1024 * 1024),
+    )(ids, *args)
+
+
+def slot_of(shape, s):
+    return pl.BlockSpec((None,) + shape, lambda *_: (s,) + (0,) * len(shape))
+
+
+def piece_places(ids):
+    y, core = ids[4], ids[0]
+    return (2 * y + core, 2 * (1 - y) + core, 2 * y + 1 - core, 2 * (1 - y) + 1 - core)
+
+
+def lay_pieces(ids, target, pieces):
+    size = target.shape[0] // len(pieces)
+    for piece, place in zip(pieces, piece_places(ids)):
+        target[pl.ds(pl.multiple_of(place * size, size), size)] = piece[...]
+
+
+def by_rows(ids, x, near, far):
+    size = near.shape[0]
+    own = pl.ds(pl.multiple_of(ids[3] * size, size), size)
+    across = pl.ds(pl.multiple_of((1 - ids[3]) * size, size), size)
+    return nn(x[:, own], near[...]) + nn(x[:, across], far[...])
+
+
+def project_other_kernel(ids, mine, got, gain, shift, near, p0, p1, p2, p3, bias, block, normed, out, far_s):
+    @pl.when(pl.program_id(0) == 0)
+    def _():
+        x = jnp.where(ids[1] == 1, got[...], mine[...])
+        block[...] = x
+        hat, unused = row_stats(x.astype(F32))
+        normed[...] = (hat * gain[...] + shift[...]).astype(BF)
+
+    lay_pieces(ids, far_s, (p0, p1, p2, p3))
+    out[...] = (by_rows(ids, normed, near, far_s) + bias[...]).astype(BF)
+
+
+def project_other(ids, mine, mine_slot, got, got_slot, gain, shift, near, far, bias):
+    rows, width = mine.shape[1:]
+    inner = width // 2
+    columns = lambda i, ids: (0, 2 * i + 1 - ids[0])
+    return call(
+        project_other_kernel,
+        ids,
+        (3,),
+        [
+            slot_of((rows, width), mine_slot),
+            slot_of((rows, width), got_slot),
+            whole((1, width)),
+            whole((1, width)),
+            pl.BlockSpec((inner, inner), columns),
+        ]
+        + [pl.BlockSpec((inner // 4, inner), columns)] * 4
+        + [pl.BlockSpec((1, inner), columns)],
+        [whole((rows, width)), whole((rows, width)), pl.BlockSpec((rows, inner), lambda i, ids: (0, i))],
+        [
+            jax.ShapeDtypeStruct((rows, width), BF),
+            jax.ShapeDtypeStruct((rows, width), BF),
+            jax.ShapeDtypeStruct((rows, 3 * inner), BF),
+        ],
+        (mine, got, gain, shift, near, *far, bias),
+        scratch=[pltpu.VMEM((inner, inner), BF)],
+        flops=2 * rows * width * 3 * inner,
+    )
+
+
+def project_mine_kernel(ids, normed, near, p0, p1, p2, p3, bias, out, far_s):
+    lay_pieces(ids, far_s, (p0, p1, p2, p3))
+    out[...] = (by_rows(ids, normed, near, far_s) + bias[...]).astype(BF)
+
+
+def project_mine(ids, normed, near, far, bias):
+    rows, width = normed.shape
+    inner = width // 2
+    columns = lambda i, ids: (0, 2 * i + ids[0])
+    return call(
+        project_mine_kernel,
+        ids,
+        (3,),
+        [whole((rows, width)), pl.BlockSpec((inner, inner), columns)]
+        + [pl.BlockSpec((inner // 4, inner), columns)] * 4
+        + [pl.BlockSpec((1, inner), columns)],
+        pl.BlockSpec((rows, inner), lambda i, ids: (0, i)),
+        jax.ShapeDtypeStruct((rows, 3 * inner), BF),
+        (normed, near, *far, bias),
+        scratch=[pltpu.VMEM((inner, inner), BF)],
+        flops=2 * rows * width * 3 * inner,
+    )
+
+
+def feed_kernel(
+    ids, block, ctx_mine, ctx_other, cot_mine, cot_got, out_near, o0, o1, o2, o3, up_near, u0, u1, u2, u3,
+    down_near, d0, d1, d2, d3, gain, biases, bias_hidden, *rest,
+):
+    (
+        active, d_pre, normed2, d_out, result, d_hidden, d_branch, d_ctx_mine, d_ctx_other, sums, sum_hidden,
+        hidden_s, total_s, d_norm_s, up_far, w_down,
+    ) = rest[-16:]
+    j = pl.program_id(0)
+    half = pl.num_programs(0) // 2
+    inner = ctx_mine.shape[1]
+    live = ids[2].astype(F32)
+    own = pl.ds(pl.multiple_of(ids[3] * inner, inner), inner)
+    across = pl.ds(pl.multiple_of((1 - ids[3]) * inner, inner), inner)
+    lay_pieces(ids, up_far, (u0, u1, u2, u3))
+
+    out_far = w_down.at[:inner]
+
+    straight = ids[0] == ids[3]
+
+    @pl.when(j == 0)
+    def _():
+        lay_pieces(ids, out_far, (o0, o1, o2, o3))
+        w_mine = jnp.where(straight, out_near[...], out_far[...])
+        w_other = jnp.where(straight, out_far[...], out_near[...])
+        hidden = block[...].astype(F32) + (nn(ctx_mine[...], w_mine) + nn(ctx_other[...], w_other))
+        hidden = hidden + biases[3:4]
+        hidden_s[...] = hidden
+        hat, unused = row_stats(hidden)
+        normed2[...] = (hat * gain[1:2] + biases[4:5]).astype(BF)
+        d = (jnp.where(ids[1] == 1, cot_got[...], cot_mine[...]).astype(F32) * live).astype(BF)
+        d_out[...] = d
+
+    @pl.when(j < half)
+    def _():
+        w_down[...] = down_near[...]
+
+    @pl.when(j >= half)
+    def _():
+        here = ids[4] == j - half
+        size = d0.shape[0]
+        w_down[pl.ds(pl.multiple_of(ids[0] * size, size), size)] = jnp.where(here, d0[...], d1[...])
+        w_down[pl.ds(pl.multiple_of((1 - ids[0]) * size, size), size)] = jnp.where(here, d2[...], d3[...])
+
+    pre = by_rows(ids, normed2, up_near, up_far) + bias_hidden[...]
+    phi = 0.5 + 0.5 * lax.erf(pre * 0.7071067811865476)
+    act = (pre * phi).astype(BF)
+    active[...] = act
+    slope = phi + pre * (jnp.exp2(pre * pre * (-0.5 * LOG2E)) * 0.3989422804014327)
+    dp = nt(d_out[...], w_down[...]) * slope
+    sum_hidden[...] = jnp.broadcast_to(jnp.sum(dp.astype(BF).astype(F32), 0, keepdims=True), sum_hidden.shape)
+    dp = dp.astype(BF)
+    d_pre[...] = dp
+    forward = nn(act, w_down[...])
+    back = nt(dp, up_near[...])
+    back_far = nt(dp, up_far[...])
+
+    @pl.when(j == 0)
+    def _():
+        total_s[...] = forward
+        d_norm_s[:, own] = back
+        d_norm_s[:, across] = back_far
+
+    @pl.when(j > 0)
+    def _():
+        total_s[...] += forward
+        d_norm_s[:, own] += back
+        d_norm_s[:, across] += back_far
+
+    @pl.when(j == pl.num_programs(0) - 1)
+    def _():
+        hidden = hidden_s[...]
+        result[...] = ((hidden + total_s[...] + biases[5:6]) * live).astype(BF)
+        hat, inverse = row_stats(hidden)
+        d_norm = d_norm_s[...]
+        weighted = d_norm * gain[1:2]
+        first = jnp.mean(weighted, -1, keepdims=True)
+        second = jnp.mean(weighted * hat, -1, keepdims=True)
+        d = d_out[...].astype(F32)
+        d_hid = d + inverse * (weighted - first - hat * second)
+        d_hidden[...] = d_hid
+        branch = d_hid.astype(BF)
+        d_branch[...] = branch
+        sums[...] = jnp.concatenate(
+            [
+                jnp.sum(d_norm * hat, 0, keepdims=True),
+                jnp.sum(d_norm, 0, keepdims=True),
+                jnp.sum(branch.astype(F32), 0, keepdims=True),
+                jnp.sum(d, 0, keepdims=True),
+                jnp.zeros((4, d.shape[1]), F32),
+            ],
+            0,
+        )
+        lay_pieces(ids, out_far, (o0, o1, o2, o3))
+        w_mine = jnp.where(straight, out_near[...], out_far[...])
+        w_other = jnp.where(straight, out_far[...], out_near[...])
+        d_ctx_mine[...] = nt(branch, w_mine).astype(BF)
+        d_ctx_other[...] = nt(branch, w_other).astype(BF)
+
+
+def feed(ids, slot, slots, block, ctx_mine, ctx_other, cot_mine, cot_got, w_out, w_up, w_down, far, far_down, gain, biases, bias_hidden, before):
+    rows, width = block.shape
+    inner = width // 2
+    ff = w_up.shape[1]
+    chunk = width
+    steps = ff // chunk
+    one = dict(pipeline_mode=pl.Buffered(1))
+    full = whole((rows, width), **one)
+    part = whole((rows, inner), **one)
+    place = lambda j, ids: (0, (ids[3] * (steps // 2) + j) % steps)
+    columns = pl.BlockSpec((rows, chunk), place)
+    one_slot = lambda shape: pl.BlockSpec((None,) + shape, lambda *_: (slot, 0, 0), **one)
+    wide = jax.ShapeDtypeStruct((rows, width), BF)
+    args = (
+        block, ctx_mine, ctx_other, cot_mine, cot_got, w_out, *far, w_up, *far, w_down, *far_down, gain, biases, bias_hidden,
+    )
+    return call(
+        feed_kernel,
+        ids,
+        (steps,),
+        [full, part, part, one_slot((rows, width)), one_slot((rows, width)), whole((inner, width), **one)]
+        + [pl.BlockSpec((inner // 4, width), lambda j, ids: (steps, 0), **one)] * 4
+        + [pl.BlockSpec((inner, chunk), place)]
+        + [pl.BlockSpec((inner // 4, chunk), lambda j, ids: (place(j, ids)[1], 0))] * 4
+        + [pl.BlockSpec((chunk, width), lambda j, ids: (jnp.minimum(j, steps // 2 - 1), 0), **one)]
+        + [whole((ff // 8, width), **one)] * 4
+        + [whole(gain.shape), whole(biases.shape), pl.BlockSpec((1, chunk), place)]
+        + [pl.BlockSpec(memory_space=pl.ANY)] * len(before),
+        [
+            columns, columns, full, full, full, full, full, part, one_slot((rows, inner)),
+            whole((8, width)),
+            pl.BlockSpec((8, chunk), place),
+        ],
+        [
+            jax.ShapeDtypeStruct((rows, ff), BF), jax.ShapeDtypeStruct((rows, ff), BF),
+            wide, wide, wide, jax.ShapeDtypeStruct((rows, width), F32), wide,
+            jax.ShapeDtypeStruct((rows, inner), BF), jax.ShapeDtypeStruct((slots, rows, inner), BF),
+            jax.ShapeDtypeStruct((8, width), F32), jax.ShapeDtypeStruct((8, ff), F32),
+        ],
+        args + tuple(before),
+        scratch=[pltpu.VMEM((rows, width), F32)] * 3
+        + [pltpu.VMEM((inner, chunk), BF), pltpu.VMEM((chunk, width), BF)],
+        flops=2 * rows * width * (4 * ff + 2 * width),
+        limit=62,
+        aliases=[(1 + len(args), 8)] if before else (),
+    )
+
+
+def outer_sum(left, right):
+    total = None
+    for a, b in zip(left, right):
+        term = tn(a, b)
+        total = term if total is None else total + term
+    return total
+
+
+def put_block(ids, outs, rec, piece, x, y, z, rows):
+    place = 2 * (x != ids[3]).astype(jnp.int32) + (y != ids[4]).astype(jnp.int32)
+    if rec is None:
+        outs[0][place, z, rows] = piece.astype(BF)
+        return
+    for i, out in enumerate(outs):
+
+        @pl.when(place == i)
+        def _(i=i, out=out):
+            out[z, rows] = (piece + rec[i, z, rows].astype(F32)).astype(BF)
+
+
+def split_refs(refs, counts):
+    parts, at = [], 0
+    for count in counts:
+        parts.append(refs[at : at + count])
+        at += count
+    rest = refs[at:]
+    return parts + ([None, rest] if len(rest) == 1 else [rest[0], rest[-4:]])
+
+
+def grad_down_kernel(ids, *refs, slots):
+    left, right, rec, outs = split_refs(refs, (slots, slots))
+    step = pl.program_id(0)
+    x = jnp.where(step == 0, 1 - ids[3], ids[3])
+    total = outer_sum([a[...] for a in left], [b[...] for b in right])
+    chips, rows, cols = outs[0].shape[-3:]
+    parts = total.shape[1] // cols
+    rows = rows // parts
+    for z in range(chips):
+        for y in range(2):
+            at = (2 * z + y) * rows
+            for part in range(parts):
+                piece = total[at : at + rows, part * cols : (part + 1) * cols]
+                put_block(ids, outs, rec, piece, x, jnp.int32(y), z, slice(part * rows, (part + 1) * rows))
+
+
+def grad_up_kernel(ids, *refs, slots):
+    left, first, last, rec, outs = split_refs(refs, (slots, slots, slots))
+    z = pl.program_id(0)
+    right = [jnp.concatenate([a[...], b[...]], 1) for a, b in zip(first, last)]
+    total = outer_sum([a[...] for a in left], right)
+    rows, cols = outs[0].shape[-2:]
+    for x in range(2):
+        for y in range(2):
+            piece = total[y * rows : (y + 1) * rows, x * cols : (x + 1) * cols]
+            put_block(ids, outs, rec, piece, jnp.int32(x), jnp.int32(y), z, slice(0, rows))
+
+
+def grad_out_kernel(ids, *refs, slots):
+    left, mine, other, rec, outs = split_refs(refs, (slots, slots, slots))
+    right = [jnp.concatenate([a[...], b[...]], 1) for a, b in zip(mine, other)]
+    total = outer_sum([a[...] for a in left], right)
+    chips, rows, cols = outs[0].shape[-3:]
+    for near in range(2):
+        x = ids[0] if near == 0 else 1 - ids[0]
+        for z in range(chips):
+            for y in range(2):
+                at = (2 * z + y) * rows
+                piece = total[at : at + rows, near * cols : (near + 1) * cols]
+                put_block(ids, outs, rec, piece, x, jnp.int32(y), z, slice(0, rows))
+
+
+def grad_qkv_kernel(ids, *refs, slots, steps):
+    mine, other, first, last, rec, outs = split_refs(refs, (slots, slots, slots, slots))
+    right = [jnp.concatenate([a[...], b[...]], 1) for a, b in zip(first, last)]
+    near = outer_sum([a[...] for a in mine], right)
+    far = outer_sum([a[...] for a in other], right)
+    total = jnp.concatenate([jnp.where(ids[0] == 0, near, far), jnp.where(ids[0] == 0, far, near)])
+    chips, rows, cols = outs[0].shape[-3:]
+    span = total.shape[0]
+    for step in range(steps):
+
+        @pl.when(pl.program_id(0) == step)
+        def _(step=step):
+            for block in range(2 * chips):
+                begin = max(block * rows, step * span)
+                end = min((block + 1) * rows, (step + 1) * span)
+                if begin >= end:
+                    continue
+                for x in range(2):
+                    piece = total[begin - step * span : end - step * span, x * cols : (x + 1) * cols]
+                    put_block(
+                        ids, outs, rec, piece, jnp.int32(x), jnp.int32(block % 2), block // 2,
+                        slice(begin - block * rows, end - block * rows),
+                    )
+
+
+def grad_call(kernel, ids, grid, groups, shape, rec, flops, joint=None, **kw):
+    specs, args = [], []
+    for arrays, block, index in groups:
+        specs += [pl.BlockSpec(block, index)] * len(arrays)
+        args += arrays
+    if rec is None:
+        out_specs, out_shapes, aliases = whole(shape, pipeline_mode=pl.Buffered(1)), jax.ShapeDtypeStruct(shape, BF), ()
+    else:
+        specs.append(whole(shape, pipeline_mode=pl.Buffered(1)))
+        args.append(rec)
+        all_rows, at, arrays = joint
+        out_specs = [pl.BlockSpec(shape[1:], lambda *_: (0, at, 0), pipeline_mode=pl.Buffered(1))] * 4
+        out_shapes = [jax.ShapeDtypeStruct((shape[1], all_rows, shape[3]), BF)] * 4
+        aliases = [(1 + len(args) + i, i) for i in range(len(arrays))]
+        specs += [pl.BlockSpec(memory_space=pl.ANY)] * len(arrays)
+        args += arrays
+    return call(
+        functools.partial(kernel, slots=len(groups[0][0]), **kw),
+        ids, grid, specs, out_specs, out_shapes, tuple(args), flops=flops, aliases=aliases,
+    )
+
+
+def column_half(ids, rec):
+    return 1 - ids[0] if rec is None else ids[0]
+
+
+def grad_down_part(ids, chips, d_out, active, rec, joint=None):
+    rows, width = d_out[0].shape
+    ff = active[0].shape[1]
+    cols = ff // 4
+    parts = 4 * cols // width
+    block = lambda i, ids: (0, 2 * jnp.where(i == 0, 1 - ids[3], ids[3]) + column_half(ids, rec))
+    groups = [(d_out, (rows, width), lambda i, ids: (0, 0)), (active, (rows, cols), block)]
+    flops = 2 * len(d_out) * rows * width * 2 * cols
+    shape = (4, chips, parts * width // (2 * chips), cols // parts)
+    return grad_call(grad_down_kernel, ids, (2,), groups, shape, rec, flops, joint)
+
+
+def grad_up_part(ids, chips, d_pre, normed, rec, joint=None):
+    rows, width = normed[0].shape
+    ff = d_pre[0].shape[1]
+    cols = width // 4
+    groups = [
+        (d_pre, (rows, ff // chips), lambda i, ids: (0, i)),
+        (normed, (rows, cols), lambda i, ids: (0, column_half(ids, rec))),
+        (normed, (rows, cols), lambda i, ids: (0, 2 + column_half(ids, rec))),
+    ]
+    flops = 2 * len(d_pre) * rows * ff * 2 * cols
+    return grad_call(grad_up_kernel, ids, (chips,), groups, (4, chips, ff // (2 * chips), cols), rec, flops, joint)
+
+
+def grad_out_part(ids, chips, d_branch, mine, other, rec, joint=None):
+    rows, width = d_branch[0].shape
+    cols = width // 4
+    half = lambda i, ids: (0, column_half(ids, rec))
+    groups = [(d_branch, (rows, width), lambda i, ids: (0, 0)), (mine, (rows, cols), half), (other, (rows, cols), half)]
+    flops = 2 * len(d_branch) * rows * width * 2 * cols
+    return grad_call(grad_out_kernel, ids, (1,), groups, (4, chips, width // (2 * chips), cols), rec, flops, joint)
+
+
+def grad_qkv_part(ids, chips, mine, other, normed, rec, joint=None):
+    rows, width = normed[0].shape
+    cols = width // 4
+    columns = lambda i, ids: (0, i)
+    groups = [
+        (mine, (rows, width // 2), columns),
+        (other, (rows, width // 2), columns),
+        (normed, (rows, cols), lambda i, ids: (0, column_half(ids, rec))),
+        (normed, (rows, cols), lambda i, ids: (0, 2 + column_half(ids, rec))),
+    ]
+    flops = 2 * len(mine) * rows * 3 * width * 2 * cols
+    return grad_call(
+        grad_qkv_kernel, ids, (3,), groups, (4, chips, 3 * width // (2 * chips), cols), rec, flops, joint, steps=3
+    )
+
+
+def add_kernel(ids, *refs):
+    refs[-1][...] = sum(term[...].astype(F32) for term in refs[:-1]).astype(BF)
+
+
+def add_chips(ids, terms, chips, rows):
+    cols = terms[0].shape[1]
+    return call(
+        add_kernel,
+        ids,
+        (chips,),
+        [pl.BlockSpec((rows, cols), lambda i, ids: (ids[5] ^ i, 0))] * len(terms),
+        pl.BlockSpec((None, rows, cols), lambda i, ids: (i, 0, 0)),
+        jax.ShapeDtypeStruct((chips, rows, cols), BF),
+        tuple(terms),
+    )
+
+
+def finish_kernel(
+    ids, d_mine, d_other, mine_near, m0, m1, m2, m3, other_near, o0, o1, o2, o3, block, d_hidden, gain,
+    row_grad, sums, sum_mine, sum_other, total_s, mine_far, other_far,
+):
+    i = pl.program_id(0)
+    size = mine_near.shape[0]
+    lay_pieces(ids, mine_far, (m0, m1, m2, m3))
+    lay_pieces(ids, other_far, (o0, o1, o2, o3))
+    own = pl.ds(pl.multiple_of(ids[3] * size, size), size)
+    across = pl.ds(pl.multiple_of((1 - ids[3]) * size, size), size)
+    term = nt(d_mine[...], mine_near[...]) + nt(d_other[...], other_near[...])
+    term_far = nt(d_mine[...], mine_far[...]) + nt(d_other[...], other_far[...])
+    sum_mine[...] = jnp.broadcast_to(jnp.sum(d_mine[...].astype(F32), 0, keepdims=True), sum_mine.shape)
+    sum_other[...] = jnp.broadcast_to(jnp.sum(d_other[...].astype(F32), 0, keepdims=True), sum_other.shape)
+
+    @pl.when(i == 0)
+    def _():
+        total_s[:, own] = term
+        total_s[:, across] = term_far
+
+    @pl.when(i > 0)
+    def _():
+        total_s[:, own] += term
+        total_s[:, across] += term_far
+
+    @pl.when(i == pl.num_programs(0) - 1)
+    def _():
+        hat, inverse = row_stats(block[...].astype(F32))
+        d_norm = total_s[...]
+        weighted = d_norm * gain[0:1]
+        first = jnp.mean(weighted, -1, keepdims=True)
+        second = jnp.mean(weighted * hat, -1, keepdims=True)
+        row_grad[...] = (d_hidden[...] + inverse * (weighted - first - hat * second)).astype(BF)
+        sums[...] = jnp.concatenate(
+            [jnp.sum(d_norm * hat, 0, keepdims=True), jnp.sum(d_norm, 0, keepdims=True), jnp.zeros((6, d_norm.shape[1]), F32)], 0
+        )
+
+
+def finish(ids, d_mine, d_other, near, far, block, d_hidden, gain):
+    rows, width = block.shape
+    inner = width // 2
+    full = whole((rows, width))
+    part = pl.BlockSpec((rows, inner), lambda i, ids: (0, i))
+    row = pl.BlockSpec((8, inner), lambda i, ids: (0, i))
+    mine = lambda i, ids: (0, 2 * i + ids[0])
+    other = lambda i, ids: (0, 2 * i + 1 - ids[0])
+    return call(
+        finish_kernel,
+        ids,
+        (3,),
+        [
+            part, part,
+            pl.BlockSpec((inner, inner), mine), *[pl.BlockSpec((inner // 4, inner), mine)] * 4,
+            pl.BlockSpec((inner, inner), other), *[pl.BlockSpec((inner // 4, inner), other)] * 4,
+            full, full, whole(gain.shape),
+        ],
+        [full, whole((8, width)), row, row],
+        [
+            jax.ShapeDtypeStruct((rows, width), BF), jax.ShapeDtypeStruct((8, width), F32),
+            jax.ShapeDtypeStruct((8, 3 * inner), F32), jax.ShapeDtypeStruct((8, 3 * inner), F32),
+        ],
+        (d_mine, d_other, near, *far, near, *far, block, d_hidden, gain),
+        scratch=[pltpu.VMEM((rows, width), F32)] + [pltpu.VMEM((inner, inner), BF)] * 2,
+        flops=2 * rows * width * 3 * width,
+    )
+
+
+def swap_axis(x, axis, step=1):
+    size = lax.axis_size(axis)
+    return lax.ppermute(x, axis, [(i, i ^ step) for i in range(size)])
+
+
+def swap_across(x):
+    return lax.ppermute(x, ("mid", "grp"), [(0, 3), (1, 2), (2, 1), (3, 0)])
+
+
+def swap_owner(x, chips):
     pairs = []
-    for k in range(outer):
-        pairs += [(4 * k, 4 * k), (4 * k + 1, 4 * k + 2), (4 * k + 2, 4 * k + 1), (4 * k + 3, 4 * k + 3)]
-    return lax.ppermute(x, ("outer", "core", "grp"), pairs)
-
-
-def two_halves(x, core, axis=0):
+    for k in range(2 * chips):
+        pairs += [(4 * k + 1, 4 * k + 2), (4 * k + 2, 4 * k + 1)]
+    return lax.ppermute(x, AXES, pairs)
+
+
+def after(values, first):
+    return lax.optimization_barrier((values, first))[0]
+
+
+def in_order(index, mine, other, axis=0):
+    return jnp.concatenate([jnp.where(index == 0, mine, other), jnp.where(index == 0, other, mine)], axis)
+
+
+def own_half(x, index, axis=0):
     size = x.shape[axis] // 2
-    return (
-        lax.dynamic_slice_in_dim(x, core * size, size, axis),
-        lax.dynamic_slice_in_dim(x, (1 - core) * size, size, axis),
-    )
-
-
-def join_halves(mine, other, core, axis=0):
-    first = jnp.where(core == 0, mine, other)
-    second = jnp.where(core == 0, other, mine)
-    return jnp.concatenate([first, second], axis)
-
-
-def scatter_blocks(grad, sizes):
-    outer = sizes["outer"]
-    rows, cols = grad.shape
-    x = grad.astype(BF).reshape(2, rows // 2, 2 * outer, cols // (2 * outer)).transpose(2, 0, 1, 3)
-    x = x.reshape(2 * outer * 2, rows // 2, cols // (2 * outer))
-    return lax.psum_scatter(x, ("outer", "core", "grp"), scatter_dimension=0, tiled=True)[0].astype(F32)
-
-
-def gather_rows(shard):
-    core = lax.axis_index("core")
-    part = shard.shape[0] // 2
-    piece = lax.dynamic_slice_in_dim(shard, core * part, part, 0)
-    return lax.all_gather(piece, ("grp", "core"), axis=0, tiled=True)
-
-
-def body(sizes, clips, clip_count, cotangent, norm_gain, bias_d, bias_ff, w_qkv, w_o, w_up, w_down):
-    core = lax.axis_index("core")
+    return lax.dynamic_slice_in_dim(x, index * size, size, axis)
+
+
+def send_piece(piece):
+    return swap_axis(piece, "grp")
+
+
+def own_piece(shard):
+    place = 2 * lax.axis_index("mid") + lax.axis_index("core")
+    part = shard.shape[0] // 4
+    return lax.dynamic_slice_in_dim(shard, place * part, part, 0)
+
+
+def as_lines(x, cols):
+    parts = []
+    for _ in range(3):
+        part = lax.reduce_precision(x, 8, 7)
+        parts.append(part.astype(BF))
+        x = x - part
+    return jnp.concatenate(parts).reshape(-1, cols)
+
+
+def from_lines(lines, shape):
+    return lines.astype(F32).reshape((3,) + shape).sum(0)
+
+
+def send_sums(part):
+    return [part[0], swap_axis(part[1], "mid"), swap_axis(part[2], "grp"), swap_across(part[3])]
+
+
+def send_chips(part):
+    return [part[0]] + [swap_axis(part[i], "z", i) for i in range(1, lax.axis_size("z"))]
+
+
+def settle(total, parts, core):
+    mine = jnp.concatenate([lax.dynamic_index_in_dim(part, core, 0, False) for part in parts])
+    other = jnp.concatenate([lax.dynamic_index_in_dim(part, 1 - core, 0, False) for part in parts])
+    return mine, swap_axis(other, "core")
+
+
+def body(chips, clips, clip_count, cotangent, norm_gain, bias_d, bias_ff, w_qkv, w_o, w_up, w_down):
+    core, x, y, z = (lax.axis_index(axis) for axis in ("core", "grp", "mid", "z"))
     slots, half, width = clips.shape
     inner = width // 2
-    qkv_weight = gather_rows(w_qkv)
-    gains = lax.all_gather(norm_gain, "grp", axis=1, tiled=True).astype(F32)
-    biases = lax.all_gather(bias_d, "grp", axis=1, tiled=True).astype(F32)
-    bias_hidden = lax.all_gather(bias_ff, "grp", axis=0, tiled=True).astype(F32)
-    count = swap_owner(clip_count, sizes)[0]
-    out_weight = gather_rows(w_o)
-    up_weight = gather_rows(w_up)
-    down_weight = gather_rows(w_down)
-
-    qkv_parts = [two_halves(qkv_weight[:, i * width : (i + 1) * width], core, 1) for i in range(3)]
-    qkv_mine = jnp.concatenate([part[0] for part in qkv_parts], 1)
-    qkv_other = jnp.concatenate([part[1] for part in qkv_parts], 1)
-    zero = jnp.zeros((inner,), F32)
-    q_shift = two_halves(biases[1], core)
-    v_shift = two_halves(biases[2], core)
-    shift_mine = jnp.concatenate([q_shift[0], zero, v_shift[0]])
-    shift_other = jnp.concatenate([q_shift[1], zero, v_shift[1]])
-    out_mine, out_other = two_halves(out_weight, core)
-
-    inputs, normed, scaled1, inverse1 = [], [], [], []
-    saved, context_mine, context_other = [], [], []
+    ff = w_up.shape[1]
+    swap = (core != x).astype(jnp.int32)
+
+    qkv_piece = own_piece(w_qkv)
+    small = jnp.concatenate([norm_gain.reshape(-1), bias_d.reshape(-1), bias_ff]).reshape(-1, 128)
+    qkv_0 = send_piece(qkv_piece)
+    got_small = swap_axis(after(small, qkv_piece), "grp")
+    got_first = swap_owner(after(clips[:1], qkv_piece), chips)
+    other_count = swap_axis(clip_count, "core")
+    qkv_1 = swap_axis(qkv_0, "mid")
+    qkv_2 = swap_axis(qkv_0, "core")
+    got_rest = swap_owner(after(clips[1:], qkv_0), chips)
+    piece = own_piece(w_up).reshape(-1, ff // width, width).transpose(1, 0, 2).reshape(-1, width)
+    piece = jnp.concatenate([piece, own_piece(w_o)])
+    down_piece = own_piece(w_down)
+    qkv_3 = swap_axis(qkv_1, "core")
+    qkv_far = (qkv_0, qkv_1, qkv_2, qkv_3)
+    far_0 = send_piece(after(piece, qkv_1))
+    down_0 = send_piece(after(down_piece, qkv_1))
+
+    pair = in_order(x, small[None], got_small[None]).reshape(2, -1).astype(F32)
+    gains = pair[:, : 2 * inner].reshape(2, 2, inner).transpose(1, 0, 2).reshape(2, width)
+    biases = pair[:, 2 * inner : 8 * inner].reshape(2, 6, inner).transpose(1, 0, 2).reshape(6, width)
+    bias_hidden = pair[:, 8 * inner :].reshape(1, -1)
+    count = jnp.where(swap == 1, other_count, clip_count)[0]
+    qkv_bias = jnp.concatenate([biases[1], jnp.zeros_like(biases[1]), biases[2]])[None]
+    ids = [jnp.stack([core, swap, (count > s).astype(jnp.int32), x, y, z]).astype(jnp.int32) for s in range(slots)]
+
+    blocks, normed, saved, ctx_mine, ctx_other = [], [], [], [], []
     for s in range(slots):
-        block = swap_owner(clips[s], sizes).astype(F32)
-        scaled, inverse, norm = layer_norm(block, gains[0], biases[0])
-        norm = norm.astype(BF)
-        other = (nn(norm, qkv_other) + shift_other).astype(BF)
-        received = swap_core(other)
-        mine = (nn(norm, qkv_mine) + shift_mine).astype(BF)
+        got, slot = (got_first, 0) if s == 0 else (got_rest, s - 1)
+        block, norm, other = project_other(ids[s], clips, s, got, slot, gains[0:1], biases[0:1], w_qkv, qkv_far, qkv_bias)
+        received = swap_axis(other, "core")
+        mine = project_mine(ids[s], norm, w_qkv, qkv_far, qkv_bias)
+        if s == 0:
+            mine = after(mine, (piece, down_piece))
+        elif s == 2:
+            mine = after(mine, (far_2, far_3))
         here, there, r_here, r_there, weights, weights_rem = attend(mine, received)
-        context_mine.append(here)
-        context_other.append(swap_core(there))
         saved.append((mine, received, here, there, r_here, r_there, weights, weights_rem))
-        inputs.append(block)
+        ctx_mine.append(here)
+        ctx_other.append(swap_axis(there, "core"))
+        blocks.append(block)
         normed.append(norm)
-        scaled1.append(scaled)
-        inverse1.append(inverse)
-    live = jnp.repeat((count > jnp.arange(slots)).astype(F32), half)[:, None]
-    cot = jnp.concatenate([swap_owner(cotangent[s], sizes) for s in range(slots)])
-    inputs = jnp.concatenate(inputs)
-    normed = jnp.concatenate(normed)
-    scaled1 = jnp.concatenate(scaled1)
-    inverse1 = jnp.concatenate(inverse1)
-    context_mine = jnp.concatenate(context_mine)
-    context_other = jnp.concatenate(context_other)
-
-    hidden = inputs + nn(context_mine, out_mine) + nn(context_other, out_other) + biases[3]
-    scaled2, inverse2, normed2 = layer_norm(hidden, gains[1], biases[4])
-    normed2 = normed2.astype(BF)
-    pre = nn(normed2, up_weight) + bias_hidden
-    active = jax.nn.gelu(pre, approximate=False).astype(BF)
-    result = ((hidden + nn(active, down_weight) + biases[5]) * live).astype(BF)
-    block_out = jnp.stack([swap_owner(result[s * half : (s + 1) * half], sizes) for s in range(slots)])
-
-    d_out = cot * live.astype(BF)
-    d_out_f = d_out.astype(F32)
-    grad_down = scatter_blocks(tn(active, d_out), sizes)
-    grad_b2 = jnp.sum(d_out_f, 0)
-    d_act = nt(d_out, down_weight)
-    unused, gelu_pull = jax.vjp(lambda x: jax.nn.gelu(x, approximate=False), pre)
-    d_pre = gelu_pull(d_act)[0].astype(BF)
-    grad_up = scatter_blocks(tn(normed2, d_pre), sizes)
-    grad_bias_hidden = jnp.sum(d_pre.astype(F32), 0)
-    d_norm2 = nt(d_pre, up_weight)
-    d_hidden = d_out_f + norm_back(scaled2, inverse2, gains[1], d_norm2)
-    grad_g2 = jnp.sum(d_norm2 * scaled2, 0)
-    grad_beta2 = jnp.sum(d_norm2, 0)
-    d_branch = d_hidden.astype(BF)
-    grad_bo = jnp.sum(d_branch.astype(F32), 0)
-    d_context_other = swap_core(nt(d_branch, out_other).astype(BF))
-    d_context_mine = nt(d_branch, out_mine).astype(BF)
-    grad_out = scatter_blocks(
-        join_halves(tn(context_mine, d_branch), tn(context_other, d_branch), core), sizes
-    )
-
-    d_mine, d_other = [], []
+        if s == 0:
+            far_0 = after(far_0, here)
+            far_1 = swap_axis(far_0, "mid")
+            far_2 = swap_axis(far_0, "core")
+            got_rest = after(got_rest, (here, far_0))
+        elif s == 1:
+            far_1 = after(far_1, here)
+            far_3 = swap_axis(far_1, "core")
+            down_0 = after(down_0, here)
+            down_1 = swap_axis(down_0, "mid")
+            got_cot = swap_owner(after(cotangent, down_0), chips)
+            got_rest = after(got_rest, (here, far_1, down_0))
+        elif s == 2:
+            down_2 = swap_axis(after(down_0, here), "core")
+            down_1 = after(down_1, here)
+            down_3 = swap_axis(down_1, "core")
+    far = (far_0, far_1, far_2, far_3)
+    far_down = (down_0, down_1, down_2, down_3)
+
+    fed, got_result = [], []
+    before = ()
     for s in range(slots):
-        rows = slice(s * half, (s + 1) * half)
+        fed.append(
+            feed(
+                ids[s], s, slots, blocks[s], ctx_mine[s], ctx_other[s], cotangent, got_cot, w_o, w_up, w_down, far, far_down,
+                gains, biases, bias_hidden, before,
+            )
+        )
+        before = (fed[-1][8],)
+        got_result.append(swap_owner(fed[-1][4], chips))
+    active, d_pre, normed2, d_out, result, d_hidden, d_branch, d_ctx_mine, d_ctx_other, sums2, sums_hidden = map(list, zip(*fed))
+    d_ctx_got = swap_axis(d_ctx_other[-1], "core")
+
+    sent_down = grad_down_part(ids[0], chips, d_out, active, None)
+    sent_up = grad_up_part(ids[0], chips, d_pre, normed2, None)
+    sent_out = grad_out_part(ids[0], chips, d_branch, ctx_mine, ctx_other, None)
+    rows_down, rows_up, rows_out = (part.shape[2] for part in (sent_down, sent_up, sent_out))
+    rows = rows_down + rows_up + rows_out
+    joint = grad_down_part(ids[0], chips, d_out, active, swap_axis(sent_down, "core"), (rows, 0, []))
+    joint = grad_up_part(
+        ids[0], chips, d_pre, normed2, swap_axis(sent_up, "core"), (rows, rows_down // rows_up, joint)
+    )
+    joint = grad_out_part(
+        ids[0], chips, d_branch, ctx_mine, ctx_other, swap_axis(sent_out, "core"),
+        (rows, (rows_down + rows_up) // rows_out, joint),
+    )
+    cols = joint[0].shape[-1]
+    sums = send_sums([part.reshape(-1, cols) for part in joint])
+    early = jnp.concatenate([sum(sums2)[:4], sum(sums_hidden)[0].reshape(-1, width)])
+
+    d_mine, d_other, row_grads, sums1, sums_mine, sums_other = [], [], [], [], [], []
+
+    def complete(s, first):
+        row_grad, sum1, sum_mine, sum_other = finish(
+            ids[s], d_mine[s], after(d_other[s], first), w_qkv, qkv_far, blocks[s], d_hidden[s], gains
+        )
+        row_grads.append(jnp.where(swap == 1, swap_owner(row_grad, chips), row_grad).astype(F32))
+        sums1.append(sum1)
+        sums_mine.append(sum_mine[0])
+        sums_other.append(sum_other[0])
+        return row_grad
+
+    outs = jnp.stack([jnp.where(swap == 1, got_result[s], result[s]) for s in range(slots)])
+    gate = (joint, outs)
+    for s in range(slots):
         mine, received, here, there, r_here, r_there, weights, weights_rem = saved[s]
         d_here, d_there = attend_back(
-            mine, received, d_context_mine[rows], d_context_other[rows], here, there, r_here, r_there, weights, weights_rem
+            s, mine, received, after(d_ctx_mine[s], gate), d_ctx_got, here, there, r_here, r_there, weights, weights_rem
         )
         d_mine.append(d_here)
-        d_other.append(swap_core(d_there))
-    d_mine = jnp.concatenate(d_mine)
-    d_other = jnp.concatenate(d_other)
-    d_norm1 = nt(d_mine, qkv_mine) + nt(d_other, qkv_other)
-    grad_mine = tn(normed, d_mine)
-    grad_other = tn(normed, d_other)
-    grad_qkv = scatter_blocks(
-        jnp.concatenate(
-            [
-                join_halves(grad_mine[:, i * inner : (i + 1) * inner], grad_other[:, i * inner : (i + 1) * inner], core, 1)
-                for i in range(3)
-            ],
-            1,
-        ),
-        sizes,
-    )
-    sum_mine = jnp.sum(d_mine.astype(F32), 0)
-    sum_other = jnp.sum(d_other.astype(F32), 0)
-    grad_bq = join_halves(sum_mine[:inner], sum_other[:inner], core)
-    grad_bv = join_halves(sum_mine[2 * inner :], sum_other[2 * inner :], core)
-    row_grad = (d_hidden + norm_back(scaled1, inverse1, gains[0], d_norm1)).astype(BF)
-    grad_g1 = jnp.sum(d_norm1 * scaled1, 0)
-    grad_beta1 = jnp.sum(d_norm1, 0)
-    input_grad = jnp.stack(
-        [swap_owner(row_grad[s * half : (s + 1) * half], sizes).astype(F32) for s in range(slots)]
-    )
-    small = jnp.concatenate(
-        [
-            jnp.stack([grad_g1, grad_g2, grad_beta1, grad_bq, grad_bv, grad_bo, grad_beta2, grad_b2]),
-            grad_bias_hidden.reshape(4, width),
-        ]
-    )
-    small = lax.psum(small, ("outer", "core", "grp"))
-    x = lax.axis_index("grp")
-    columns = lax.dynamic_slice_in_dim(small[:8], x * inner, inner, 1)
-    hidden_part = lax.dynamic_slice_in_dim(small[8:], 2 * x, 2, 0).reshape(-1)
-    return (block_out, input_grad, columns[:2], columns[2:], hidden_part, grad_qkv, grad_out, grad_up, grad_down)
+        d_other.append(swap_axis(d_there, "core"))
+        gate = (d_here,)
+        if s == 0:
+            sums[3] = after(sums[3], d_here)
+            gate = (d_here, sums[3])
+        elif s == 1:
+            sums = add_chips(ids[0], after(sums, d_here), chips, rows)
+            gate = sums
+            terms = send_chips(sums)
+        if s > 0:
+            gate = (gate, complete(s - 1, d_here))
+    terms = after(terms, gate)
+    sent_qkv = grad_qkv_part(ids[0], chips, d_mine, after(d_other, (gate, terms)), normed, None)
+    row_grad = complete(slots - 1, sent_qkv)
+    part_qkv = grad_qkv_part(
+        ids[0], chips, d_mine, d_other, normed, after(swap_axis(sent_qkv, "core"), row_grad),
+        (sent_qkv.shape[2], 0, []),
+    )
+    total1 = sum(sums1)
+    total_mine, total_other = sum(sums_mine), sum(sums_other)
+    grad_bq = in_order(core, total_mine[:inner], total_other[:inner])
+    grad_bv = in_order(core, total_mine[2 * inner :], total_other[2 * inner :])
+    lines = jnp.concatenate(
+        [jnp.stack([total1[0], early[0], total1[1], grad_bq, grad_bv, early[2], early[1], early[3]]), early[4:]]
+    )
+    lines = lines + swap_axis(lines, "core")
+    shape = lines.shape
+    under = as_lines(lines, cols)
+    qkv_rows = part_qkv[0].shape[1]
+    qkv_terms = send_sums([jnp.concatenate([part.reshape(-1, cols), under]) for part in part_qkv])
+
+    total = sum(term.astype(F32) for term in after(terms, part_qkv))
+    chunks = rows_down // rows_out
+    down = total[:rows_down].reshape(chunks, 2, -1, cols).transpose(1, 0, 2, 3).reshape(2, -1, cols)
+    up = total[rows_down : rows_down + rows_up].reshape(2, -1, cols)
+    out = total[rows_down + rows_up :].reshape(2, -1, cols)
+    mine, other = settle(total, (down, up, out), core)
+    whole_rows = in_order(core, mine, other, 1)
+    n_down, n_up = rows_down // 2, rows_up // 2
+    own_down = in_order(core, mine[:n_down].reshape(chunks, -1, cols), other[:n_down].reshape(chunks, -1, cols))
+    grad_down = own_down.transpose(0, 2, 1).reshape(2 * chunks * cols, -1)
+    grad_up = whole_rows[n_down : n_down + n_up].T
+    grad_out = whole_rows[n_down + n_up :].T
+
+    sums = add_chips(ids[0], qkv_terms, chips, qkv_rows)
+    lines = sum(from_lines(term[chips * qkv_rows :], shape) for term in qkv_terms)
+    under = as_lines(lines, cols)
+    qkv_terms = send_chips([jnp.concatenate([sums[i], under]) for i in range(chips)])
+    lines = sum(from_lines(term[qkv_rows:], shape) for term in qkv_terms)
+    columns = own_half(lines[:8], x, 1)
+    hidden_part = own_half(lines[8:], x).reshape(-1)
+    total = sum(term[:qkv_rows].astype(F32) for term in qkv_terms)
+    mine, other = settle(total, (total.reshape(2, -1, cols),), core)
+    grad_qkv = in_order(core, mine, other, 1).T
+    return (outs, jnp.stack(row_grads), columns[:2], columns[2:], hidden_part, grad_qkv, grad_out, grad_up, grad_down)
 
 
 def solution(mesh):
@@ -703,13 +1298,13 @@
         P("grp", "rep"),
         P("grp", "rep"),
     )
-    if mesh.shape["grp"] != 2:
+    if mesh.shape["grp"] != 2 or mesh.shape["rep"] != 16:
         return jax.shard_map(plain_body, mesh=mesh, in_specs=in_specs, out_specs=out_specs, check_vma=False)
-    outer = mesh.shape["rep"] // 2
-    split = Mesh(mesh.devices.reshape(outer, 2, 2), ("outer", "core", "grp"))
-    rep = lambda spec: P(*[("outer", "core") if axis == "rep" else axis for axis in spec])
+    chips = mesh.shape["rep"] // 4
+    split = Mesh(mesh.devices.reshape(chips, 2, 2, 2), AXES)
+    rep = lambda spec: P(*[AXES[:3] if axis == "rep" else axis for axis in spec])
     return jax.shard_map(
-        functools.partial(body, {"outer": outer}),
+        functools.partial(body, chips),
         mesh=split,
         in_specs=tuple(rep(spec) for spec in in_specs),
         out_specs=tuple(rep(spec) for spec in out_specs),

time: 1460 us -> 972 us (0.67)
  Pallas kernels: 262 us -> 658 us
  matrix products: 388 us -> 0 us
  blocking collectives: 316 us -> 0 us
  local copies, waits for them, and re-layouts: 157 us -> 44.1 us
  other arithmetic: 89.9 us -> 33.1 us
    pallas_call x0 -> x22, Pallas kernels: none -> 410 us  [call(): pl.pallas_call(kernel, grid_spec=pltpu.PrefetchScalarGridSpec(num_scalar_...]
    dot_general x22 -> x0, matrix products: 388 us -> none  [dot(): return lax.dot_general(a, b, (dims, ((), ())), preferred_element_type=F32)]
    psum x1 -> x0, blocking collectives: 208 us -> none  [body(): small = lax.psum(small, ('outer', 'core', 'grp'))]
    all_gather x3 -> x0, blocking collectives: 108 us -> none  [the longest x1 92.2 us: body(): gains = lax.all_gather(norm_gain, 'grp', axis=1, tiled=True).astype(F32)]
    transpose x5 -> x1, local copies, waits for them, and re-layouts: 36.7 us -> 2.29 us  [body(): own_piece(w_up).reshape(-1, ff // width, width).transpose(1, 0, 2)]
    convert_element_type x11 -> x4, other arithmetic: 29.7 us -> 0.12 us  [the longest x1 0.06 us: body(): pair = in_order(x, small[None], got_small[None]).reshape(2, -1).astype(F32)]
    reduce_sum x10 -> x8, other arithmetic: 28.1 us -> 0.12 us  [from_lines(): return lines.astype(F32).reshape((3,) + shape).sum(0)]
    convert_element_type x3 -> x2, local copies, waits for them, and re-layouts: 26.2 us -> 0.03 us  [from_lines(): return lines.astype(F32).reshape((3,) + shape).sum(0)]
  transfers between devices with their start and end apart: 31 -> 52, of which waited for: 5 -> 20; matrix products, arithmetic and copies ran while one was open for 36% -> 6% of each run, Pallas kernels for 18% -> 56%
where the time goes in v2:
time: 972 us; the launch traced here: 967 us
  Pallas kernels  658 us (68%)
  waiting for transfers between devices  171 us (18%)
  starting transfers between devices  57.5 us (6%)
  local copies, waits for them, and re-layouts  44.1 us (5%)
  other arithmetic  33.1 us (3%)
    pallas_call x22, Pallas kernels, call(): pl.pallas_call(kernel, grid_spec=pltpu.PrefetchScalarGridSpec(num_scalar_...  410 us
    pallas_call x3, Pallas kernels, attend_back(): pl.pallas_call(functools.partial(attend_back_kernel, nb=nb, np_=np_, rem=...  159 us
    ppermute x41, waiting for transfers between devices, swap_axis(): return lax.ppermute(x, axis, [(i, i ^ step) for i in range(size)])  103 us
    pallas_call x3, Pallas kernels, attend(): pl.pallas_call(functools.partial(attend_kernel, nb=nb, np_=np_, rem=rem),...  89.5 us
    ppermute x9, waiting for transfers between devices, swap_owner(): return lax.ppermute(x, AXES, pairs)  50 us
    ppermute x41, starting transfers between devices, swap_axis(): return lax.ppermute(x, axis, [(i, i ^ step) for i in range(size)])  28.3 us
    ppermute x9, starting transfers between devices, swap_owner(): return lax.ppermute(x, AXES, pairs)  27.3 us
  transfers between devices with their start and end apart: 52, of which 20 were waited for; matrix products, arithmetic and copies ran while one was open for 6% of the time, Pallas kernels for 56%

profile of v2, /device:TPU:9, one launch (start us, length us, event | category | flops | bytes accessed | tf_op | source)
XLA Modules:
  0.0 966.8 jit_solution(8172628790309192071)
XLA Ops:
  24.0 14.0 %collective-permute-done.4.p1.m1.o1 = bf16[128,3072]{1,0:T(8,128)(2,1)S(1)} collective-permute-done((bf16[128,3072]{1,0:T(8,128)(2,1)S(1)}, bf16[128,3072]{1,0:T(8,128)(2,1)S(1)}, u32[]{:S(2)}, u32[]{:S(2)}) %collective-permute-start.4) | collective-permute-done | bytes 786464 | tf_op jit(solution)/shard_map/ppermute | solution.py:1038
  79.5 29.9 %shard_map.171 = (bf16[784,512]{1,0:T(8,128)(2,1)}, bf16[784,512]{1,0:T(8,128)(2,1)}, f32[784,512]{1,0:T(8,128)}, f32[784,512]{1,0:T(8,128)}, bf16[12,2,1568,512...) custom-call(bf16[784,1536]{1,0:T(8,128)(2,1)} %shard_map.170.own, bf16[784,1536]{1,0:T(8,128)(2,1)} %collective-permute-done.7.rec), custom_call_target="tpu_custom_call" | custom-call | flops 14000000000 | tf_op jit(solution)/shard_map/pallas_call | solution.py:151
  109.4 14.0 %collective-permute-done.11.o0.u0 = bf16[640,1024]{1,0:T(8,128)(2,1)} collective-permute-done((bf16[640,1024]{1,0:T(8,128)(2,1)}, bf16[640,1024]{1,0:T(8,128)(2,1)}, u32[]{:S(2)}, u32[]{:S(2)}) %collective-permute-start.11) | collective-permute-done | bytes 1310752 | tf_op jit(solution)/shard_map/ppermute | solution.py:1038
  146.4 29.9 %shard_map.174 = (bf16[784,512]{1,0:T(8,128)(2,1)}, bf16[784,512]{1,0:T(8,128)(2,1)}, f32[784,512]{1,0:T(8,128)}, f32[784,512]{1,0:T(8,128)}, bf16[12,2,1568,512...) custom-call(bf16[784,1536]{1,0:T(8,128)(2,1)} %shard_map.173.own, bf16[784,1536]{1,0:T(8,128)(2,1)} %copy-done.27), custom_call_target="tpu_custom_call" | custom-call | flops 14000000000 | tf_op jit(solution)/shard_map/pallas_call | solution.py:151
  199.5 29.7 %shard_map.177 = (bf16[784,512]{1,0:T(8,128)(2,1)}, bf16[784,512]{1,0:T(8,128)(2,1)}, f32[784,512]{1,0:T(8,128)}, f32[784,512]{1,0:T(8,128)}, bf16[12,2,1568,512...) custom-call(bf16[784,1536]{1,0:T(8,128)(2,1)} %shard_map.176.own, bf16[784,1536]{1,0:T(8,128)(2,1)} %copy-done.28), custom_call_target="tpu_custom_call" | custom-call | flops 14000000000 | tf_op jit(solution)/shard_map/pallas_call | solution.py:151
  235.2 55.0 %shard_map.178 = (bf16[784,4096]{1,0:T(8,128)(2,1)}, bf16[784,4096]{1,0:T(8,128)(2,1)}, bf16[784,1024]{1,0:T(8,128)(2,1)}, bf16[784,1024]{1,0:T(8,128)(2,1)}, bf...) custom-call(s32[6]{0:T(128)} %stack.78.ids, ...), custom_call_target="tpu_custom_call" | custom-call | flops 11838003200 | tf_op jit(solution)/shard_map/pallas_call | solution.py:533
  291.1 55.1 %shard_map.179 = (bf16[784,4096]{1,0:T(8,128)(2,1)}, bf16[784,4096]{1,0:T(8,128)(2,1)}, bf16[784,1024]{1,0:T(8,128)(2,1)}, bf16[784,1024]{1,0:T(8,128)(2,1)}, bf...) custom-call(s32[6]{0:T(128)} %stack.79.ids, ...), custom_call_target="tpu_custom_call", output_to_operand_aliasing={{8}: (24, {})} | custom-call | flops 11838003200 | tf_op jit(solution)/shard_map/pallas_call | solution.py:533
  346.3 55.5 %shard_map.180 = (bf16[784,4096]{1,0:T(8,128)(2,1)}, bf16[784,4096]{1,0:T(8,128)(2,1)}, bf16[784,1024]{1,0:T(8,128)(2,1)}, bf16[784,1024]{1,0:T(8,128)(2,1)}, bf...) custom-call(s32[6]{0:T(128)} %stack.80.ids, ...), custom_call_target="tpu_custom_call", output_to_operand_aliasing={{8}: (24, {})} | custom-call | flops 11838003200 | tf_op jit(solution)/shard_map/pallas_call | solution.py:533
  401.8 20.5 %shard_map.183 = bf16[4,4,512,256]{3,2,1,0:T(8,128)(2,1)} custom-call(s32[6]{0:T(128)} %stack.78.ids, bf16[784,1024]{1,0:T(8,128)(2,1)} %get-tuple-element.186.refs_0_, bf16[784,1024]{1,0:T(8,128)(2,1)} %get-tuple-element.187.refs_1_, bf16[784,1024]{1,0:T(8,128)(2,1)} %get-tuple-element.188.refs_2_, bf16[784,4096]{1,0:T(8,128)(2,1)} %get-tuple-element.189.refs_3_, ...), custom_call_target="tpu_custom_call" | custom-call | flops 3946001152 | tf_op jit(solution)/shard_map/pallas_call | solution.py:533
  422.6 20.6 %shard_map.182 = bf16[4,4,512,256]{3,2,1,0:T(8,128)(2,1)} custom-call(s32[6]{0:T(128)} %stack.78.ids, bf16[784,4096]{1,0:T(8,128)(2,1)} %get-tuple-element.180.refs_0_, bf16[784,4096]{1,0:T(8,128)(2,1)} %get-tuple-element.181.refs_1_, bf16[784,4096]{1,0:T(8,128)(2,1)} %get-tuple-element.182.refs_2_, bf16[784,1024]{1,0:T(8,128)(2,1)} %get-tuple-element.183.refs_3_.refs_6_, ...), custom_call_target="tpu_custom_call" | custom-call | flops 3946001152 | tf_op jit(solution)/shard_map/pallas_call | solution.py:533
  451.4 14.1 %collective-permute-done.21 = bf16[784,1024]{1,0:T(8,128)(2,1)S(1)} collective-permute-done((bf16[784,1024]{1,0:T(8,128)(2,1)S(1)}, bf16[784,1024]{1,0:T(8,128)(2,1)S(1)}, u32[]{:S(2)}, u32[]{:S(2)}) %collective-permute-start.21) | collective-permute-done | bytes 1605664 | tf_op jit(solution)/shard_map/ppermute | solution.py:1049
  484.4 15.6 %collective-permute-done.25 = bf16[784,1024]{1,0:T(8,128)(2,1)} collective-permute-done((bf16[784,1024]{1,0:T(8,128)(2,1)}, bf16[784,1024]{1,0:T(8,128)(2,1)}, u32[]{:S(2)}, u32[]{:S(2)}) %collective-permute-start.25) | collective-permute-done | bytes 1605664 | tf_op jit(solution)/shard_map/ppermute | solution.py:1049
  504.3 23.8 %shard_map.184 = (bf16[4,1152,256]{2,1,0:T(8,128)(2,1)}, bf16[4,1152,256]{2,1,0:T(8,128)(2,1)}, bf16[4,1152,256]{2,1,0:T(8,128)(2,1)}, bf16[4,1152,256]{2,1,0:T(8,128)(2,1)}) custom-call(s32[6]{0:T(128)} %stack.78.ids, bf16[784,1024]{1,0:T(8,128)(2,1)} %get-tuple-element.186.refs_0_, bf16[784,1024]{1,0:T(8,128)(2,1)} %get-tuple-element.187.refs_1_, ...), custom_call_target="tpu_custom_call" | custom-call | flops 3946001152 | tf_op jit(solution)/shard_map/pallas_call | solution.py:533
  528.2 22.7 %shard_map.185 = (bf16[4,1152,256]{2,1,0:T(8,128)(2,1)}, bf16[4,1152,256]{2,1,0:T(8,128)(2,1)}, bf16[4,1152,256]{2,1,0:T(8,128)(2,1)}, bf16[4,1152,256]{2,1,0:T(8,128)(2,1)}) custom-call(s32[6]{0:T(128)} %stack.78.ids, bf16[784,4096]{1,0:T(8,128)(2,1)} %get-tuple-element.180.refs_0_, ...), custom_call_target="tpu_custom_call", output_to_operand_aliasing={{0}: (11, {}), {1}: (12, {}), {2}: (13, {}), {3}: (14, {})} | custom-call | flops 3946001152 | tf_op jit(solution)/shard_map/pallas_call | solution.py:533
  561.1 52.8 %shard_map.187 = (bf16[784,1536]{1,0:T(8,128)(2,1)}, bf16[784,1536]{1,0:T(8,128)(2,1)}) custom-call(bf16[784,1536]{1,0:T(8,128)(2,1)} %shard_map.170.own, bf16[784,1536]{1,0:T(8,128)(2,1)} %collective-permute-done.7.rec, bf16[784,512]{1,0:T(8,128)(2,1)} %get-tuple-element.204.do_o, bf16[3,784,512]{2,1,0:T(8,128)(2,1)} %collective-permute-done.29.do_r, ...), custom_call_target="tpu_custom_call" | custom-call | flops 24000000000 | tf_op jit(solution)/shard_map/pallas_call | solution.py:255
  616.5 53.2 %shard_map.188 = (bf16[784,1536]{1,0:T(8,128)(2,1)}, bf16[784,1536]{1,0:T(8,128)(2,1)}) custom-call(bf16[784,1536]{1,0:T(8,128)(2,1)} %shard_map.173.own, bf16[784,1536]{1,0:T(8,128)(2,1)} %copy-done.27, bf16[784,512]{1,0:T(8,128)(2,1)} %get-tuple-element.214.do_o, bf16[3,784,512]{2,1,0:T(8,128)(2,1)} %collective-permute-done.29.do_r, ...), custom_call_target="tpu_custom_call" | custom-call | flops 24000000000 | tf_op jit(solution)/shard_map/pallas_call | solution.py:255
  677.4 14.7 %shard_map.189 = (bf16[784,1024]{1,0:T(8,128)(2,1)}, f32[8,1024]{1,0:T(8,128)}, f32[8,1536]{1,0:T(8,128)}, f32[8,1536]{1,0:T(8,128)}) custom-call(s32[6]{0:T(128)} %stack.78.ids, bf16[784,1536]{1,0:T(8,128)(2,1)} %get-tuple-element.210.d_mine.refs_0_, bf16[784,1536]{1,0:T(8,128)(2,1)} %collective-permute-done.30.d_other.refs_3_, ...), custom_call_target="tpu_custom_call" | custom-call | flops 1973000576 | tf_op jit(solution)/shard_map/pallas_call | solution.py:533
  692.1 52.7 %shard_map.191 = (bf16[784,1536]{1,0:T(8,128)(2,1)}, bf16[784,1536]{1,0:T(8,128)(2,1)}) custom-call(bf16[784,1536]{1,0:T(8,128)(2,1)} %shard_map.176.own, bf16[784,1536]{1,0:T(8,128)(2,1)} %copy-done.28, bf16[784,512]{1,0:T(8,128)(2,1)} %get-tuple-element.229.do_o, bf16[3,784,512]{2,1,0:T(8,128)(2,1)} %collective-permute-done.29.do_r, ...), custom_call_target="tpu_custom_call" | custom-call | flops 24000000000 | tf_op jit(solution)/shard_map/pallas_call | solution.py:255
  754.9 14.9 %shard_map.192 = (bf16[784,1024]{1,0:T(8,128)(2,1)}, f32[8,1024]{1,0:T(8,128)}, f32[8,1536]{1,0:T(8,128)}, f32[8,1536]{1,0:T(8,128)}) custom-call(s32[6]{0:T(128)} %stack.79.ids, bf16[784,1536]{1,0:T(8,128)(2,1)} %get-tuple-element.219.d_mine.refs_1_, bf16[784,1536]{1,0:T(8,128)(2,1)} %collective-permute-done.33.d_other.refs_4_, ...), custom_call_target="tpu_custom_call" | custom-call | flops 1973000576 | tf_op jit(solution)/shard_map/pallas_call | solution.py:533
  777.2 25.2 %collective-permute-done.40 = bf16[1152,256]{1,0:T(8,128)(2,1)} collective-permute-done((bf16[1152,256]{1,0:T(8,128)(2,1)S(1)}, bf16[1152,256]{1,0:T(8,128)(2,1)}, u32[]{:S(2)}, u32[]{:S(2)}) %collective-permute-start.40) | collective-permute-done | bytes 589856 | tf_op jit(solution)/shard_map/ppermute | solution.py:1038
  803.8 16.8 %shard_map.193 = bf16[4,4,384,256]{3,2,1,0:T(8,128)(2,1)} custom-call(s32[6]{0:T(128)} %stack.78.ids, bf16[784,1536]{1,0:T(8,128)(2,1)} %get-tuple-element.210.d_mine.refs_0_, bf16[784,1536]{1,0:T(8,128)(2,1)} %get-tuple-element.219.d_mine.refs_1_, bf16[784,1536]{1,0:T(8,128)(2,1)} %get-tuple-element.234.refs_2_.d_mine, ...), custom_call_target="tpu_custom_call" | custom-call | flops 2959500800 | tf_op jit(solution)/shard_map/pallas_call | solution.py:533
  822.2 14.8 %shard_map.194 = (bf16[784,1024]{1,0:T(8,128)(2,1)}, f32[8,1024]{1,0:T(8,128)}, f32[8,1536]{1,0:T(8,128)}, f32[8,1536]{1,0:T(8,128)}) custom-call(s32[6]{0:T(128)} %stack.80.ids, bf16[784,1536]{1,0:T(8,128)(2,1)} %get-tuple-element.234.refs_2_.d_mine, bf16[784,1536]{1,0:T(8,128)(2,1)} %copy-done.4, bf16[512,3072]{1,0:T(8,128)(2,1)} %other_near.5, ...), custom_call_target="tpu_custom_call" | custom-call | flops 1973000576 | tf_op jit(solution)/shard_map/pallas_call | solution.py:533
  862.2 18.4 %shard_map.195 = (bf16[4,384,256]{2,1,0:T(8,128)(2,1)}, bf16[4,384,256]{2,1,0:T(8,128)(2,1)}, bf16[4,384,256]{2,1,0:T(8,128)(2,1)}, bf16[4,384,256]{2,1,0:T(8,128)(2,1)}) custom-call(s32[6]{0:T(128)} %stack.78.ids, bf16[784,1536]{1,0:T(8,128)(2,1)} %get-tuple-element.210.d_mine.refs_0_, bf16[784,1536]{1,0:T(8,128)(2,1)} %get-tuple-element.219.d_mine.refs_1_, ...), custom_call_target="tpu_custom_call" | custom-call | flops 2959500800 | tf_op jit(solution)/shard_map/pallas_call | solution.py:533
  907.7 18.2 %collective-permute-done.46.refs_3_ = bf16[1680,256]{1,0:T(8,128)(2,1)} collective-permute-done((bf16[1680,256]{1,0:T(8,128)(2,1)S(1)}, bf16[1680,256]{1,0:T(8,128)(2,1)}, u32[]{:S(2)}, u32[]{:S(2)}) %collective-permute-start.46) | collective-permute-done | bytes 860192 | tf_op jit(solution)/shard_map/ppermute | solution.py:1042
  (277 shorter events, 281.5 us)
Async XLA Ops:
  56.8 66.7 %collective-permute-start.10 = (bf16[2,784,1024]{2,1,0:T(8,128)(2,1)}, bf16[2,784,1024]{2,1,0:T(8,128)(2,1)S(1)}, u32[]{:S(2)}, u32[]{:S(2)}) collective-permute-start(bf16[2,784,1024]{2,1,0:T(8,128)(2,1)} %slice.189), channel_id=1, source_target_pairs={{1,2},{2,1},{5,6},{6,5},{9,10},{10,9},{13,14},{14,13},{17,18},{18,... | collective-permute-start | bytes 9633800 | tf_op jit(solution)/shard_map/ppermute | solution.py:1049
  72.3 51.1 %collective-permute-start.11 = (bf16[640,1024]{1,0:T(8,128)(2,1)}, bf16[640,1024]{1,0:T(8,128)(2,1)}, u32[]{:S(2)}, u32[]{:S(2)}) collective-permute-start(bf16[640,1024]{1,0:T(8,128)(2,1)} %pad_maximum_fusion.5), channel_id=1, source_target_pairs={{0,1},{1,0},{2,3},{3,2},{4,5},{5,4},{6,7},{7,6},{8,9},{9,8},{10,11... | collective-permute-start | bytes 3932168 | tf_op jit(solution)/shard_map/ppermute | solution.py:1038
  136.4 40.0 %collective-permute-start.9 = (bf16[512,1024]{1,0:T(8,128)(2,1)}, bf16[512,1024]{1,0:T(8,128)(2,1)}, u32[]{:S(2)}, u32[]{:S(2)}) collective-permute-start(bf16[512,1024]{1,0:T(8,128)(2,1)} %constant_dynamic-slice_fusion.2), channel_id=1, source_target_pairs={{0,1},{1,0},{2,3},{3,2},{4,5},{5,4},{6,7},{7,6},{8,9},{9,8},{10,11... | collective-permute-start | bytes 3145736 | tf_op jit(solution)/shard_map/ppermute | solution.py:1038
  136.6 39.7 %collective-permute-start.14 = (bf16[640,1024]{1,0:T(8,128)(2,1)}, bf16[640,1024]{1,0:T(8,128)(2,1)}, u32[]{:S(2)}, u32[]{:S(2)}) collective-permute-start(bf16[640,1024]{1,0:T(8,128)(2,1)} %collective-permute-done.11.o0.u0), channel_id=1, source_target_pairs={{0,4},{4,0},{1,5},{5,1},{2,6},{6,2},{3,7},{7,3},{8,12},{12,8},{9,1... | collective-permute-start | bytes 3932168 | tf_op jit(solution)/shard_map/ppermute | solution.py:1038
  176.3 58.8 %collective-permute-start.13 = (bf16[3,784,1024]{2,1,0:T(8,128)(2,1)}, bf16[3,784,1024]{2,1,0:T(8,128)(2,1)}, u32[]{:S(2)}, u32[]{:S(2)}) collective-permute-start(bf16[3,784,1024]{2,1,0:T(8,128)(2,1)} %cot_mine.5), channel_id=1, source_target_pairs={{1,2},{2,1},{5,6},{6,5},{9,10},{10,9},{13,14},{14,13},{17,18},{18,... | collective-permute-start | bytes 14450696 | tf_op jit(solution)/shard_map/ppermute | solution.py:1049
  190.1 39.4 %collective-permute-start.17 = (bf16[512,1024]{1,0:T(8,128)(2,1)}, bf16[512,1024]{1,0:T(8,128)(2,1)}, u32[]{:S(2)}, u32[]{:S(2)}) collective-permute-start(bf16[512,1024]{1,0:T(8,128)(2,1)} %collective-permute-done.9.d0), channel_id=1, source_target_pairs={{0,4},{4,0},{1,5},{5,1},{2,6},{6,2},{3,7},{7,3},{8,12},{12,8},{9,1... | collective-permute-start | bytes 3145736 | tf_op jit(solution)/shard_map/ppermute | solution.py:1038
  231.2 59.0 %collective-permute-start.22 = (bf16[784,512]{1,0:T(8,128)(2,1)}, bf16[784,512]{1,0:T(8,128)(2,1)S(1)}, u32[]{:S(2)}, u32[]{:S(2)}) collective-permute-start(bf16[784,512]{1,0:T(8,128)(2,1)} %get-tuple-element.169.o_r), channel_id=1, source_target_pairs={{0,2},{2,0},{1,3},{3,1},{4,6},{6,4},{5,7},{7,5},{8,10},{10,8},{9,1... | collective-permute-start | bytes 2408456 | tf_op jit(solution)/shard_map/ppermute | solution.py:1038
  234.3 112.0 %collective-permute-start.24 = (bf16[784,512]{1,0:T(8,128)(2,1)}, bf16[784,512]{1,0:T(8,128)(2,1)}, u32[]{:S(2)}, u32[]{:S(2)}) collective-permute-start(bf16[784,512]{1,0:T(8,128)(2,1)} %get-tuple-element.173.o_r), channel_id=1, source_target_pairs={{0,2},{2,0},{1,3},{3,1},{4,6},{6,4},{5,7},{7,5},{8,10},{10,8},{9,1... | collective-permute-start | bytes 2408456 | tf_op jit(solution)/shard_map/ppermute | solution.py:1038
  422.3 82.1 %collective-permute-start.28 = (bf16[4,4,512,256]{3,2,1,0:T(8,128)(2,1)}, bf16[4,4,512,256]{3,2,1,0:T(8,128)(2,1)}, u32[]{:S(2)}, u32[]{:S(2)}) collective-permute-start(bf16[4,4,512,256]{3,2,1,0:T(8,128)(2,1)} %shard_map.183), channel_id=1, source_target_pairs={{0,2},{2,0},{1,3},{3,1},{4,6},{6,4},{5,7},{7,5},{8,10},{10,8},{9,1... | collective-permute-start | bytes 12582920 | tf_op jit(solution)/shard_map/ppermute | solution.py:1038
  443.2 85.0 %collective-permute-start.27 = (bf16[4,4,512,256]{3,2,1,0:T(8,128)(2,1)}, bf16[4,4,512,256]{3,2,1,0:T(8,128)(2,1)}, u32[]{:S(2)}, u32[]{:S(2)}) collective-permute-start(bf16[4,4,512,256]{3,2,1,0:T(8,128)(2,1)} %shard_map.182), channel_id=1, source_target_pairs={{0,2},{2,0},{1,3},{3,1},{4,6},{6,4},{5,7},{7,5},{8,10},{10,8},{9,1... | collective-permute-start | bytes 12582920 | tf_op jit(solution)/shard_map/ppermute | solution.py:1038
  449.0 51.0 %collective-permute-start.25 = (bf16[784,1024]{1,0:T(8,128)(2,1)}, bf16[784,1024]{1,0:T(8,128)(2,1)}, u32[]{:S(2)}, u32[]{:S(2)}) collective-permute-start(bf16[784,1024]{1,0:T(8,128)(2,1)} %get-tuple-element.175), channel_id=1, source_target_pairs={{1,2},{2,1},{5,6},{6,5},{9,10},{10,9},{13,14},{14,13},{17,18},{18,... | collective-permute-start | bytes 4816904 | tf_op jit(solution)/shard_map/ppermute | solution.py:1049
  466.6 94.4 %collective-permute-start.29 = (bf16[3,784,512]{2,1,0:T(8,128)(2,1)}, bf16[3,784,512]{2,1,0:T(8,128)(2,1)}, u32[]{:S(2)}, u32[]{:S(2)}) collective-permute-start(bf16[3,784,512]{2,1,0:T(8,128)(2,1)} %get-tuple-element.205), channel_id=1, source_target_pairs={{0,2},{2,0},{1,3},{3,1},{4,6},{6,4},{5,7},{7,5},{8,10},{10,8},{9,1... | collective-permute-start | bytes 7225352 | tf_op jit(solution)/shard_map/ppermute | solution.py:1038
  482.8 68.0 %collective-permute-start.26 = (bf16[4,4,128,256]{3,2,1,0:T(8,128)(2,1)}, bf16[4,4,128,256]{3,2,1,0:T(8,128)(2,1)S(1)}, u32[]{:S(2)}, u32[]{:S(2)}) collective-permute-start(bf16[4,4,128,256]{3,2,1,0:T(8,128)(2,1)} %shard_map.181), channel_id=1, source_target_pairs={{0,2},{2,0},{1,3},{3,1},{4,6},{6,4},{5,7},{7,5},{8,10},{10,8},{9,1... | collective-permute-start | bytes 3145736 | tf_op jit(solution)/shard_map/ppermute | solution.py:1038
  561.0 55.5 %collective-permute-start.31 = (bf16[4608,256]{1,0:T(8,128)(2,1)}, bf16[4608,256]{1,0:T(8,128)(2,1)}, u32[]{:S(2)}, u32[]{:S(2)}) collective-permute-start(bf16[4608,256]{1,0:T(8,128)(2,1)} %bitcast.135), channel_id=1, source_target_pairs={{0,5},{1,4},{4,1},{5,0},{2,7},{3,6},{6,3},{7,2},{8,13},{9,12},{12,... | collective-permute-start | bytes 7077896 | tf_op jit(solution)/shard_map/ppermute | solution.py:1042
  613.9 63.5 %collective-permute-start.30 = (bf16[784,1536]{1,0:T(8,128)(2,1)}, bf16[784,1536]{1,0:T(8,128)(2,1)}, u32[]{:S(2)}, u32[]{:S(2)}) collective-permute-start(bf16[784,1536]{1,0:T(8,128)(2,1)} %get-tuple-element.211), channel_id=1, source_target_pairs={{0,2},{2,0},{1,3},{3,1},{4,6},{6,4},{5,7},{7,5},{8,10},{10,8},{9,1... | collective-permute-start | bytes 7225352 | tf_op jit(solution)/shard_map/ppermute | solution.py:1038
  615.5 54.2 %collective-permute-start.34 = (bf16[4608,256]{1,0:T(8,128)(2,1)}, bf16[4608,256]{1,0:T(8,128)(2,1)}, u32[]{:S(2)}, u32[]{:S(2)}) collective-permute-start(bf16[4608,256]{1,0:T(8,128)(2,1)} %bitcast.133), channel_id=1, source_target_pairs={{0,4},{4,0},{1,5},{5,1},{2,6},{6,2},{3,7},{7,3},{8,12},{12,8},{9,1... | collective-permute-start | bytes 7077896 | tf_op jit(solution)/shard_map/ppermute | solution.py:1038
  615.9 53.8 %collective-permute-start.35 = (bf16[4608,256]{1,0:T(8,128)(2,1)}, bf16[4608,256]{1,0:T(8,128)(2,1)}, u32[]{:S(2)}, u32[]{:S(2)}) collective-permute-start(bf16[4608,256]{1,0:T(8,128)(2,1)} %bitcast.134), channel_id=1, source_target_pairs={{0,1},{1,0},{2,3},{3,2},{4,5},{5,4},{6,7},{7,6},{8,9},{9,8},{10,11... | collective-permute-start | bytes 7077896 | tf_op jit(solution)/shard_map/ppermute | solution.py:1038
  669.7 81.8 %collective-permute-start.33 = (bf16[784,1536]{1,0:T(8,128)(2,1)}, bf16[784,1536]{1,0:T(8,128)(2,1)}, u32[]{:S(2)}, u32[]{:S(2)}) collective-permute-start(bf16[784,1536]{1,0:T(8,128)(2,1)} %get-tuple-element.223), channel_id=1, source_target_pairs={{0,2},{2,0},{1,3},{3,1},{4,6},{6,4},{5,7},{7,5},{8,10},{10,8},{9,1... | collective-permute-start | bytes 7225352 | tf_op jit(solution)/shard_map/ppermute | solution.py:1038
  744.8 57.6 %collective-permute-start.37 = (bf16[784,1536]{1,0:T(8,128)(2,1)}, bf16[784,1536]{1,0:T(8,128)(2,1)S(1)}, u32[]{:S(2)}, u32[]{:S(2)}) collective-permute-start(bf16[784,1536]{1,0:T(8,128)(2,1)} %get-tuple-element.238), channel_id=1, source_target_pairs={{0,2},{2,0},{1,3},{3,1},{4,6},{6,4},{5,7},{7,5},{8,10},{10,8},{9,1... | collective-permute-start | bytes 7225352 | tf_op jit(solution)/shard_map/ppermute | solution.py:1038
  751.2 51.1 %collective-permute-start.40 = (bf16[1152,256]{1,0:T(8,128)(2,1)S(1)}, bf16[1152,256]{1,0:T(8,128)(2,1)}, u32[]{:S(2)}, u32[]{:S(2)}) collective-permute-start(bf16[1152,256]{1,0:T(8,128)(2,1)S(1)} %get-tuple-element.302), channel_id=1, source_target_pairs={{0,24},{8,16},{16,8},{24,0},{1,25},{9,17},{17,9},{25,1},{2,26},{10... | collective-permute-start | bytes 1769480 | tf_op jit(solution)/shard_map/ppermute | solution.py:1038
  751.5 90.6 %collective-permute-start.32 = (bf16[784,1024]{1,0:T(8,128)(2,1)}, bf16[784,1024]{1,0:T(8,128)(2,1)}, u32[]{:S(2)}, u32[]{:S(2)}) collective-permute-start(bf16[784,1024]{1,0:T(8,128)(2,1)} %get-tuple-element.222), channel_id=1, source_target_pairs={{1,2},{2,1},{5,6},{6,5},{9,10},{10,9},{13,14},{14,13},{17,18},{18,... | collective-permute-start | bytes 4816904 | tf_op jit(solution)/shard_map/ppermute | solution.py:1049
  773.4 70.4 %collective-permute-start.36 = (bf16[784,1024]{1,0:T(8,128)(2,1)}, bf16[784,1024]{1,0:T(8,128)(2,1)}, u32[]{:S(2)}, u32[]{:S(2)}) collective-permute-start(bf16[784,1024]{1,0:T(8,128)(2,1)} %get-tuple-element.237), channel_id=1, source_target_pairs={{1,2},{2,1},{5,6},{6,5},{9,10},{10,9},{13,14},{14,13},{17,18},{18,... | collective-permute-start | bytes 4816904 | tf_op jit(solution)/shard_map/ppermute | solution.py:1049
  820.6 41.6 %collective-permute-start.43 = (bf16[4,4,384,256]{3,2,1,0:T(8,128)(2,1)}, bf16[4,4,384,256]{3,2,1,0:T(8,128)(2,1)}, u32[]{:S(2)}, u32[]{:S(2)}) collective-permute-start(bf16[4,4,384,256]{3,2,1,0:T(8,128)(2,1)} %shard_map.193), channel_id=1, source_target_pairs={{0,2},{2,0},{1,3},{3,1},{4,6},{6,4},{5,7},{7,5},{8,10},{10,8},{9,1... | collective-permute-start | bytes 9437192 | tf_op jit(solution)/shard_map/ppermute | solution.py:1038
  886.4 39.5 %collective-permute-start.46 = (bf16[1680,256]{1,0:T(8,128)(2,1)S(1)}, bf16[1680,256]{1,0:T(8,128)(2,1)}, u32[]{:S(2)}, u32[]{:S(2)}) collective-permute-start(bf16[1680,256]{1,0:T(8,128)(2,1)S(1)} %get-tuple-element.331), channel_id=1, source_target_pairs={{0,5},{1,4},{4,1},{5,0},{2,7},{3,6},{6,3},{7,2},{8,13},{9,12},{12,... | collective-permute-start | bytes 2580488 | tf_op jit(solution)/shard_map/ppermute | solution.py:1042
  (58 other events, 685.4 us)

commit v3 on v2

--- a/solution.py
+++ b/solution.py
@@ -19,7 +19,7 @@
 AXES = ("z", "mid", "core", "grp")
 BQ = 512
 TK = 224
-COST = 0.4
+COST = 5 * 10**10
 LIMIT = 70.0
 
 
@@ -158,7 +158,7 @@
         scratch_shapes=[
             pltpu.VMEM((full, inner), BF), pltpu.VMEM((full, inner), BF), pltpu.VMEM((2 * np_, 128, full), BF),
             pltpu.VMEM((full, inner), BF), pltpu.VMEM((full, inner), F32), pltpu.SMEM((1,), jnp.int32)],
-        cost_estimate=pl.CostEstimate(flops=int(3.5e10 * COST), bytes_accessed=0, transcendentals=0),
+        cost_estimate=pl.CostEstimate(flops=0, bytes_accessed=0, transcendentals=0),
         compiler_params=pltpu.CompilerParams(vmem_limit_bytes=60 * 1024 * 1024),
     )(own, rec)
 
@@ -266,7 +266,7 @@
             pltpu.VMEM((inner, full), BF), pltpu.VMEM((full, inner), BF), pltpu.VMEM((full, inner), F32),
             pltpu.VMEM((2, full, BQ), BF), pltpu.VMEM((full, inner), BF),
             pltpu.VMEM((full, inner), F32), pltpu.VMEM((full, inner), F32)],
-        cost_estimate=pl.CostEstimate(flops=int(6e10 * COST), bytes_accessed=0, transcendentals=0),
+        cost_estimate=pl.CostEstimate(flops=COST, bytes_accessed=0, transcendentals=0),
         compiler_params=pltpu.CompilerParams(vmem_limit_bytes=62 * 1024 * 1024),
     )(own, rec, do_o, do_r, o_o, o_r, r_o, r_r, e, erem)
 
@@ -536,7 +536,7 @@
             num_scalar_prefetch=1, grid=grid, in_specs=in_specs, out_specs=out_specs, scratch_shapes=list(scratch)
         ),
         out_shape=out_shape,
-        cost_estimate=pl.CostEstimate(flops=int(flops * COST), bytes_accessed=0, transcendentals=0),
+        cost_estimate=pl.CostEstimate(flops=int(flops), bytes_accessed=0, transcendentals=0),
         input_output_aliases=dict(aliases),
         compiler_params=pltpu.CompilerParams(vmem_limit_bytes=limit * 1024 * 1024),
     )(ids, *args)
@@ -601,7 +601,6 @@
         ],
         (mine, got, gain, shift, near, *far, bias),
         scratch=[pltpu.VMEM((inner, inner), BF)],
-        flops=2 * rows * width * 3 * inner,
     )
 
 
@@ -625,7 +624,6 @@
         jax.ShapeDtypeStruct((rows, 3 * inner), BF),
         (normed, near, *far, bias),
         scratch=[pltpu.VMEM((inner, inner), BF)],
-        flops=2 * rows * width * 3 * inner,
     )
 
 
@@ -634,9 +632,9 @@
     down_near, d0, d1, d2, d3, gain, biases, bias_hidden, *rest,
 ):
     (
-        active, d_pre, normed2, d_out, result, d_hidden, d_branch, d_ctx_mine, d_ctx_other, sums, sum_hidden,
+        active, d_pre, normed2, d_out, result, d_branch, d_ctx_mine, d_ctx_other, sums, sum_hidden,
         hidden_s, total_s, d_norm_s, up_far, w_down,
-    ) = rest[-16:]
+    ) = rest[-15:]
     j = pl.program_id(0)
     half = pl.num_programs(0) // 2
     inner = ctx_mine.shape[1]
@@ -673,30 +671,43 @@
         w_down[pl.ds(pl.multiple_of(ids[0] * size, size), size)] = jnp.where(here, d0[...], d1[...])
         w_down[pl.ds(pl.multiple_of((1 - ids[0]) * size, size), size)] = jnp.where(here, d2[...], d3[...])
 
-    pre = by_rows(ids, normed2, up_near, up_far) + bias_hidden[...]
-    phi = 0.5 + 0.5 * lax.erf(pre * 0.7071067811865476)
-    act = (pre * phi).astype(BF)
-    active[...] = act
-    slope = phi + pre * (jnp.exp2(pre * pre * (-0.5 * LOG2E)) * 0.3989422804014327)
-    dp = nt(d_out[...], w_down[...]) * slope
-    sum_hidden[...] = jnp.broadcast_to(jnp.sum(dp.astype(BF).astype(F32), 0, keepdims=True), sum_hidden.shape)
-    dp = dp.astype(BF)
-    d_pre[...] = dp
-    forward = nn(act, w_down[...])
-    back = nt(dp, up_near[...])
-    back_far = nt(dp, up_far[...])
+    rows = block.shape[0]
+    parts = (slice(0, rows // 32 * 16), slice(rows // 32 * 16, rows))
+
+    def begin(part):
+        pre = nn(normed2[part, own], up_near[...]) + nn(normed2[part, across], up_far[...])
+        return pre, nt(d_out[part], w_down[...])
+
+    def middle(part, pre, d_act):
+        pre = pre + bias_hidden[...]
+        phi = 0.5 + 0.5 * lax.erf(pre * 0.7071067811865476)
+        act = (pre * phi).astype(BF)
+        active[part] = act
+        slope = phi + pre * (jnp.exp2(pre * pre * (-0.5 * LOG2E)) * 0.3989422804014327)
+        dp = d_act * slope
+        total = jnp.sum(dp, 0, keepdims=True)
+        dp = dp.astype(BF)
+        d_pre[part] = dp
+        return act, dp, total
+
+    def end(part, act, dp):
+        total_s[part] += nn(act, w_down[...])
+        d_norm_s[part, own] += nt(dp, up_near[...])
+        d_norm_s[part, across] += nt(dp, up_far[...])
 
     @pl.when(j == 0)
     def _():
-        total_s[...] = forward
-        d_norm_s[:, own] = back
-        d_norm_s[:, across] = back_far
-
-    @pl.when(j > 0)
-    def _():
-        total_s[...] += forward
-        d_norm_s[:, own] += back
-        d_norm_s[:, across] += back_far
+        total_s[...] = jnp.zeros_like(total_s)
+        d_norm_s[...] = jnp.zeros_like(d_norm_s)
+
+    first, second = parts
+    begun = begin(first)
+    begun_second = begin(second)
+    act, dp, total = middle(first, *begun)
+    end(first, act, dp)
+    act, dp, total_second = middle(second, *begun_second)
+    end(second, act, dp)
+    sum_hidden[...] = jnp.broadcast_to(total + total_second, sum_hidden.shape)
 
     @pl.when(j == pl.num_programs(0) - 1)
     def _():
@@ -708,9 +719,7 @@
         first = jnp.mean(weighted, -1, keepdims=True)
         second = jnp.mean(weighted * hat, -1, keepdims=True)
         d = d_out[...].astype(F32)
-        d_hid = d + inverse * (weighted - first - hat * second)
-        d_hidden[...] = d_hid
-        branch = d_hid.astype(BF)
+        branch = (d + inverse * (weighted - first - hat * second)).astype(BF)
         d_branch[...] = branch
         sums[...] = jnp.concatenate(
             [
@@ -729,7 +738,7 @@
         d_ctx_other[...] = nt(branch, w_other).astype(BF)
 
 
-def feed(ids, slot, slots, block, ctx_mine, ctx_other, cot_mine, cot_got, w_out, w_up, w_down, far, far_down, gain, biases, bias_hidden, before):
+def feed(ids, slot, slots, block, ctx_mine, ctx_other, cot_mine, cot_got, got_slot, w_out, w_up, w_down, far, far_down, gain, biases, bias_hidden, before):
     rows, width = block.shape
     inner = width // 2
     ff = w_up.shape[1]
@@ -740,7 +749,7 @@
     part = whole((rows, inner), **one)
     place = lambda j, ids: (0, (ids[3] * (steps // 2) + j) % steps)
     columns = pl.BlockSpec((rows, chunk), place)
-    one_slot = lambda shape: pl.BlockSpec((None,) + shape, lambda *_: (slot, 0, 0), **one)
+    one_slot = lambda shape, at=slot: pl.BlockSpec((None,) + shape, lambda *_: (at, 0, 0), **one)
     wide = jax.ShapeDtypeStruct((rows, width), BF)
     args = (
         block, ctx_mine, ctx_other, cot_mine, cot_got, w_out, *far, w_up, *far, w_down, *far_down, gain, biases, bias_hidden,
@@ -749,7 +758,7 @@
         feed_kernel,
         ids,
         (steps,),
-        [full, part, part, one_slot((rows, width)), one_slot((rows, width)), whole((inner, width), **one)]
+        [full, part, part, one_slot((rows, width)), one_slot((rows, width), got_slot), whole((inner, width), **one)]
         + [pl.BlockSpec((inner // 4, width), lambda j, ids: (steps, 0), **one)] * 4
         + [pl.BlockSpec((inner, chunk), place)]
         + [pl.BlockSpec((inner // 4, chunk), lambda j, ids: (place(j, ids)[1], 0))] * 4
@@ -758,31 +767,26 @@
         + [whole(gain.shape), whole(biases.shape), pl.BlockSpec((1, chunk), place)]
         + [pl.BlockSpec(memory_space=pl.ANY)] * len(before),
         [
-            columns, columns, full, full, full, full, full, part, one_slot((rows, inner)),
+            columns, columns, full, full, full, full, part, one_slot((rows, inner)),
             whole((8, width)),
             pl.BlockSpec((8, chunk), place),
         ],
         [
             jax.ShapeDtypeStruct((rows, ff), BF), jax.ShapeDtypeStruct((rows, ff), BF),
-            wide, wide, wide, jax.ShapeDtypeStruct((rows, width), F32), wide,
+            wide, wide, wide, wide,
             jax.ShapeDtypeStruct((rows, inner), BF), jax.ShapeDtypeStruct((slots, rows, inner), BF),
             jax.ShapeDtypeStruct((8, width), F32), jax.ShapeDtypeStruct((8, ff), F32),
         ],
         args + tuple(before),
         scratch=[pltpu.VMEM((rows, width), F32)] * 3
         + [pltpu.VMEM((inner, chunk), BF), pltpu.VMEM((chunk, width), BF)],
-        flops=2 * rows * width * (4 * ff + 2 * width),
         limit=62,
-        aliases=[(1 + len(args), 8)] if before else (),
+        aliases=[(1 + len(args), 7)] if before else (),
     )
 
 
 def outer_sum(left, right):
-    total = None
-    for a, b in zip(left, right):
-        term = tn(a, b)
-        total = term if total is None else total + term
-    return total
+    return tn(jnp.concatenate(left), jnp.concatenate(right))
 
 
 def put_block(ids, outs, rec, piece, x, y, z, rows):
@@ -906,9 +910,8 @@
     parts = 4 * cols // width
     block = lambda i, ids: (0, 2 * jnp.where(i == 0, 1 - ids[3], ids[3]) + column_half(ids, rec))
     groups = [(d_out, (rows, width), lambda i, ids: (0, 0)), (active, (rows, cols), block)]
-    flops = 2 * len(d_out) * rows * width * 2 * cols
     shape = (4, chips, parts * width // (2 * chips), cols // parts)
-    return grad_call(grad_down_kernel, ids, (2,), groups, shape, rec, flops, joint)
+    return grad_call(grad_down_kernel, ids, (2,), groups, shape, rec, 0, joint)
 
 
 def grad_up_part(ids, chips, d_pre, normed, rec, joint=None):
@@ -920,8 +923,7 @@
         (normed, (rows, cols), lambda i, ids: (0, column_half(ids, rec))),
         (normed, (rows, cols), lambda i, ids: (0, 2 + column_half(ids, rec))),
     ]
-    flops = 2 * len(d_pre) * rows * ff * 2 * cols
-    return grad_call(grad_up_kernel, ids, (chips,), groups, (4, chips, ff // (2 * chips), cols), rec, flops, joint)
+    return grad_call(grad_up_kernel, ids, (chips,), groups, (4, chips, ff // (2 * chips), cols), rec, 0, joint)
 
 
 def grad_out_part(ids, chips, d_branch, mine, other, rec, joint=None):
@@ -929,8 +931,7 @@
     cols = width // 4
     half = lambda i, ids: (0, column_half(ids, rec))
     groups = [(d_branch, (rows, width), lambda i, ids: (0, 0)), (mine, (rows, cols), half), (other, (rows, cols), half)]
-    flops = 2 * len(d_branch) * rows * width * 2 * cols
-    return grad_call(grad_out_kernel, ids, (1,), groups, (4, chips, width // (2 * chips), cols), rec, flops, joint)
+    return grad_call(grad_out_kernel, ids, (1,), groups, (4, chips, width // (2 * chips), cols), rec, 0, joint)
 
 
 def grad_qkv_part(ids, chips, mine, other, normed, rec, joint=None):
@@ -943,7 +944,7 @@
         (normed, (rows, cols), lambda i, ids: (0, column_half(ids, rec))),
         (normed, (rows, cols), lambda i, ids: (0, 2 + column_half(ids, rec))),
     ]
-    flops = 2 * len(mine) * rows * 3 * width * 2 * cols
+    flops = COST // 2
     return grad_call(
         grad_qkv_kernel, ids, (3,), groups, (4, chips, 3 * width // (2 * chips), cols), rec, flops, joint, steps=3
     )
@@ -998,7 +999,7 @@
         weighted = d_norm * gain[0:1]
         first = jnp.mean(weighted, -1, keepdims=True)
         second = jnp.mean(weighted * hat, -1, keepdims=True)
-        row_grad[...] = (d_hidden[...] + inverse * (weighted - first - hat * second)).astype(BF)
+        row_grad[...] = (d_hidden[...].astype(F32) + inverse * (weighted - first - hat * second)).astype(BF)
         sums[...] = jnp.concatenate(
             [jnp.sum(d_norm * hat, 0, keepdims=True), jnp.sum(d_norm, 0, keepdims=True), jnp.zeros((6, d_norm.shape[1]), F32)], 0
         )
@@ -1029,7 +1030,7 @@
         ],
         (d_mine, d_other, near, *far, near, *far, block, d_hidden, gain),
         scratch=[pltpu.VMEM((rows, width), F32)] + [pltpu.VMEM((inner, inner), BF)] * 2,
-        flops=2 * rows * width * 3 * width,
+        flops=COST,
     )
 
 
@@ -1114,14 +1115,16 @@
     other_count = swap_axis(clip_count, "core")
     qkv_1 = swap_axis(qkv_0, "mid")
     qkv_2 = swap_axis(qkv_0, "core")
-    got_rest = swap_owner(after(clips[1:], qkv_0), chips)
+    rest = after(clips[1:], qkv_0)
+    got_rest = swap_owner(rest, chips)
     piece = own_piece(w_up).reshape(-1, ff // width, width).transpose(1, 0, 2).reshape(-1, width)
     piece = jnp.concatenate([piece, own_piece(w_o)])
     down_piece = own_piece(w_down)
     qkv_3 = swap_axis(qkv_1, "core")
     qkv_far = (qkv_0, qkv_1, qkv_2, qkv_3)
-    far_0 = send_piece(after(piece, qkv_1))
-    down_0 = send_piece(after(down_piece, qkv_1))
+    piece, down_piece = after((piece, down_piece), qkv_1)
+    far_0 = send_piece(piece)
+    down_0 = send_piece(down_piece)
 
     pair = in_order(x, small[None], got_small[None]).reshape(2, -1).astype(F32)
     gains = pair[:, : 2 * inner].reshape(2, 2, inner).transpose(1, 0, 2).reshape(2, width)
@@ -1131,16 +1134,13 @@
     qkv_bias = jnp.concatenate([biases[1], jnp.zeros_like(biases[1]), biases[2]])[None]
     ids = [jnp.stack([core, swap, (count > s).astype(jnp.int32), x, y, z]).astype(jnp.int32) for s in range(slots)]
 
+    got_first = after(got_first, (rest, piece, down_piece))
     blocks, normed, saved, ctx_mine, ctx_other = [], [], [], [], []
     for s in range(slots):
         got, slot = (got_first, 0) if s == 0 else (got_rest, s - 1)
         block, norm, other = project_other(ids[s], clips, s, got, slot, gains[0:1], biases[0:1], w_qkv, qkv_far, qkv_bias)
         received = swap_axis(other, "core")
         mine = project_mine(ids[s], norm, w_qkv, qkv_far, qkv_bias)
-        if s == 0:
-            mine = after(mine, (piece, down_piece))
-        elif s == 2:
-            mine = after(mine, (far_2, far_3))
         here, there, r_here, r_there, weights, weights_rem = attend(mine, received)
         saved.append((mine, received, here, there, r_here, r_there, weights, weights_rem))
         ctx_mine.append(here)
@@ -1148,46 +1148,49 @@
         blocks.append(block)
         normed.append(norm)
         if s == 0:
-            far_0 = after(far_0, here)
+            down_0 = after(down_0, here)
+            down_1 = swap_axis(down_0, "mid")
+            down_2 = swap_axis(down_0, "core")
+            got_rest = after(got_rest, (here, down_0))
+        elif s == 1:
+            down_1, far_0 = after((down_1, far_0), here)
+            down_3 = swap_axis(down_1, "core")
             far_1 = swap_axis(far_0, "mid")
             far_2 = swap_axis(far_0, "core")
-            got_rest = after(got_rest, (here, far_0))
-        elif s == 1:
+            got_rest = after(got_rest, (here, down_1, far_0))
+        elif s == 2:
             far_1 = after(far_1, here)
             far_3 = swap_axis(far_1, "core")
-            down_0 = after(down_0, here)
-            down_1 = swap_axis(down_0, "mid")
-            got_cot = swap_owner(after(cotangent, down_0), chips)
-            got_rest = after(got_rest, (here, far_1, down_0))
-        elif s == 2:
-            down_2 = swap_axis(after(down_0, here), "core")
-            down_1 = after(down_1, here)
-            down_3 = swap_axis(down_1, "core")
     far = (far_0, far_1, far_2, far_3)
     far_down = (down_0, down_1, down_2, down_3)
 
+    first, others = swap_owner(cotangent[:1], chips), swap_owner(cotangent[1:], chips)
+    got_cot = [(first, 0)] + [(others, s - 1) for s in range(1, slots)]
     fed, got_result = [], []
     before = ()
     for s in range(slots):
+        if s == 2:
+            got_cot[s] = (after(others, got_result[0]), s - 1)
         fed.append(
             feed(
-                ids[s], s, slots, blocks[s], ctx_mine[s], ctx_other[s], cotangent, got_cot, w_o, w_up, w_down, far, far_down,
+                ids[s], s, slots, blocks[s], ctx_mine[s], ctx_other[s], cotangent, *got_cot[s], w_o, w_up, w_down, far, far_down,
                 gains, biases, bias_hidden, before,
             )
         )
-        before = (fed[-1][8],)
+        before = (fed[-1][7],)
         got_result.append(swap_owner(fed[-1][4], chips))
-    active, d_pre, normed2, d_out, result, d_hidden, d_branch, d_ctx_mine, d_ctx_other, sums2, sums_hidden = map(list, zip(*fed))
+    active, d_pre, normed2, d_out, result, d_branch, d_ctx_mine, d_ctx_other, sums2, sums_hidden = map(list, zip(*fed))
     d_ctx_got = swap_axis(d_ctx_other[-1], "core")
 
-    sent_down = grad_down_part(ids[0], chips, d_out, active, None)
+    sent_down = grad_down_part(ids[0], chips, after(d_out, got_result[1]), active, None)
     sent_up = grad_up_part(ids[0], chips, d_pre, normed2, None)
     sent_out = grad_out_part(ids[0], chips, d_branch, ctx_mine, ctx_other, None)
     rows_down, rows_up, rows_out = (part.shape[2] for part in (sent_down, sent_up, sent_out))
     rows = rows_down + rows_up + rows_out
     joint = grad_down_part(ids[0], chips, d_out, active, swap_axis(sent_down, "core"), (rows, 0, []))
     joint = grad_up_part(
-        ids[0], chips, d_pre, normed2, swap_axis(sent_up, "core"), (rows, rows_down // rows_up, joint)
+        ids[0], chips, d_pre, normed2, after(swap_axis(sent_up, "core"), got_result[2]),
+        (rows, rows_down // rows_up, joint),
     )
     joint = grad_out_part(
         ids[0], chips, d_branch, ctx_mine, ctx_other, swap_axis(sent_out, "core"),
@@ -1197,20 +1200,21 @@
     sums = send_sums([part.reshape(-1, cols) for part in joint])
     early = jnp.concatenate([sum(sums2)[:4], sum(sums_hidden)[0].reshape(-1, width)])
 
+    got_rows = []
     d_mine, d_other, row_grads, sums1, sums_mine, sums_other = [], [], [], [], [], []
 
     def complete(s, first):
         row_grad, sum1, sum_mine, sum_other = finish(
-            ids[s], d_mine[s], after(d_other[s], first), w_qkv, qkv_far, blocks[s], d_hidden[s], gains
+            ids[s], d_mine[s], after(d_other[s], first), w_qkv, qkv_far, blocks[s], d_branch[s], gains
         )
-        row_grads.append(jnp.where(swap == 1, swap_owner(row_grad, chips), row_grad).astype(F32))
+        row_grads.append(row_grad)
+        got_rows.append(swap_owner(row_grad, chips))
         sums1.append(sum1)
         sums_mine.append(sum_mine[0])
         sums_other.append(sum_other[0])
         return row_grad
 
-    outs = jnp.stack([jnp.where(swap == 1, got_result[s], result[s]) for s in range(slots)])
-    gate = (joint, outs)
+    gate = joint
     for s in range(slots):
         mine, received, here, there, r_here, r_there, weights, weights_rem = saved[s]
         d_here, d_there = attend_back(
@@ -1226,13 +1230,14 @@
             sums = add_chips(ids[0], after(sums, d_here), chips, rows)
             gate = sums
             terms = send_chips(sums)
-        if s > 0:
-            gate = (gate, complete(s - 1, d_here))
-    terms = after(terms, gate)
-    sent_qkv = grad_qkv_part(ids[0], chips, d_mine, after(d_other, (gate, terms)), normed, None)
+            gate = (gate, [sums[i] for i in range(chips)])
+        if s == 2:
+            gate = complete(0, (d_here, terms))
+            gate = complete(1, gate)
+    sent_qkv = grad_qkv_part(ids[0], chips, d_mine, after(d_other, gate), normed, None)
     row_grad = complete(slots - 1, sent_qkv)
     part_qkv = grad_qkv_part(
-        ids[0], chips, d_mine, d_other, normed, after(swap_axis(sent_qkv, "core"), row_grad),
+        ids[0], chips, d_mine, d_other, normed, after(swap_axis(sent_qkv, "core"), (row_grad, got_rows[0])),
         (sent_qkv.shape[2], 0, []),
     )
     total1 = sum(sums1)
@@ -1248,7 +1253,12 @@
     qkv_rows = part_qkv[0].shape[1]
     qkv_terms = send_sums([jnp.concatenate([part.reshape(-1, cols), under]) for part in part_qkv])
 
-    total = sum(term.astype(F32) for term in after(terms, part_qkv))
+    sums = add_chips(ids[0], qkv_terms, chips, qkv_rows)
+    lines = sum(from_lines(term[chips * qkv_rows :], shape) for term in qkv_terms)
+    under = as_lines(lines, cols)
+    sends = [jnp.concatenate([sums[i], under]) for i in range(chips)]
+    qkv_terms = send_chips(sends)
+    total = sum(term.astype(F32) for term in after(terms, sends))
     chunks = rows_down // rows_out
     down = total[:rows_down].reshape(chunks, 2, -1, cols).transpose(1, 0, 2, 3).reshape(2, -1, cols)
     up = total[rows_down : rows_down + rows_up].reshape(2, -1, cols)
@@ -1261,17 +1271,15 @@
     grad_up = whole_rows[n_down : n_down + n_up].T
     grad_out = whole_rows[n_down + n_up :].T
 
-    sums = add_chips(ids[0], qkv_terms, chips, qkv_rows)
-    lines = sum(from_lines(term[chips * qkv_rows :], shape) for term in qkv_terms)
-    under = as_lines(lines, cols)
-    qkv_terms = send_chips([jnp.concatenate([sums[i], under]) for i in range(chips)])
+    outs = jnp.stack([jnp.where(swap == 1, after(got_result[s], sends), result[s]) for s in range(slots)])
+    input_grad = jnp.stack([jnp.where(swap == 1, after(got_rows[s], sends), row_grads[s]) for s in range(slots)]).astype(F32)
     lines = sum(from_lines(term[qkv_rows:], shape) for term in qkv_terms)
     columns = own_half(lines[:8], x, 1)
     hidden_part = own_half(lines[8:], x).reshape(-1)
     total = sum(term[:qkv_rows].astype(F32) for term in qkv_terms)
     mine, other = settle(total, (total.reshape(2, -1, cols),), core)
     grad_qkv = in_order(core, mine, other, 1).T
-    return (outs, jnp.stack(row_grads), columns[:2], columns[2:], hidden_part, grad_qkv, grad_out, grad_up, grad_down)
+    return (outs, input_grad, columns[:2], columns[2:], hidden_part, grad_qkv, grad_out, grad_up, grad_down)
 
 
 def solution(mesh):

time: 972 us -> 881 us (0.906)
  waiting for transfers between devices: 171 us -> 88.7 us
  Pallas kernels: 658 us -> 636 us
    ppermute x41, waiting for transfers between devices: 103 us -> 35.8 us  [swap_axis(): return lax.ppermute(x, axis, [(i, i ^ step) for i in range(size)])]
    pallas_call x22, Pallas kernels: 410 us -> 388 us  [call(): pl.pallas_call(kernel, grid_spec=pltpu.PrefetchScalarGridSpec(num_scalar_...]
    ppermute x9 -> x10, waiting for transfers between devices: 50 us -> 33.8 us  [swap_owner(): return lax.ppermute(x, AXES, pairs)]
    ppermute x9 -> x10, starting transfers between devices: 27.3 us -> 30.2 us  [swap_owner(): return lax.ppermute(x, AXES, pairs)]
  transfers between devices with their start and end apart: 52 -> 53, of which waited for: 20 -> 12; matrix products, arithmetic and copies ran while one was open for 6% -> 8% of each run, Pallas kernels for 56% -> 67%
where the time goes in v3:
time: 881 us; the launch traced here: 868 us
  Pallas kernels  636 us (72%)
  waiting for transfers between devices  88.7 us (10%)
  starting transfers between devices  58.3 us (7%)
  local copies, waits for them, and re-layouts  45.3 us (5%)
  other arithmetic  36 us (4%)
    pallas_call x22, Pallas kernels, call(): pl.pallas_call(kernel, grid_spec=pltpu.PrefetchScalarGridSpec(num_scalar_...  388 us
    pallas_call x3, Pallas kernels, attend_back(): pl.pallas_call(functools.partial(attend_back_kernel, nb=nb, np_=np_, rem=...  158 us
    pallas_call x3, Pallas kernels, attend(): pl.pallas_call(functools.partial(attend_kernel, nb=nb, np_=np_, rem=rem),...  89.2 us
    ppermute x41, waiting for transfers between devices, swap_axis(): return lax.ppermute(x, axis, [(i, i ^ step) for i in range(size)])  35.8 us
    ppermute x10, waiting for transfers between devices, swap_owner(): return lax.ppermute(x, AXES, pairs)  33.8 us
    ppermute x10, starting transfers between devices, swap_owner(): return lax.ppermute(x, AXES, pairs)  30.2 us
    ppermute x41, starting transfers between devices, swap_axis(): return lax.ppermute(x, axis, [(i, i ^ step) for i in range(size)])  25.6 us
    ppermute x2, waiting for transfers between devices, swap_across(): return lax.ppermute(x, ('mid', 'grp'), [(0, 3), (1, 2), (2, 1), (3, 0)])  19.2 us
  transfers between devices with their start and end apart: 53, of which 12 were waited for; matrix products, arithmetic and copies ran while one was open for 8% of the time, Pallas kernels for 67%

profile of v3, /device:TPU:9, one launch (start us, length us, event | category | flops | bytes accessed | tf_op | source)
XLA Modules:
  0.0 867.6 jit_solution(5340145108442717761)
XLA Ops:
  10.0 10.3 %collective-permute-done.2.p0.m0.o0 = bf16[128,3072]{1,0:T(8,128)(2,1)S(1)} collective-permute-done((bf16[128,3072]{1,0:T(8,128)(2,1)S(1)}, bf16[128,3072]{1,0:T(8,128)(2,1)S(1)}, u32[]{:S(2)}, u32[]{:S(2)}) %collective-permute-start.2) | collective-permute-done | bytes 786464 | tf_op jit(solution)/shard_map/ppermute | solution.py:1039
  65.8 29.7 %shard_map.171 = (bf16[784,512]{1,0:T(8,128)(2,1)}, bf16[784,512]{1,0:T(8,128)(2,1)}, f32[784,512]{1,0:T(8,128)}, f32[784,512]{1,0:T(8,128)}, bf16[12,2,1568,512...) custom-call(bf16[784,1536]{1,0:T(8,128)(2,1)} %shard_map.170.own, bf16[784,1536]{1,0:T(8,128)(2,1)} %copy-done.12), custom_call_target="tpu_custom_call" | custom-call | tf_op jit(solution)/shard_map/pallas_call | solution.py:151
  119.0 29.8 %shard_map.174 = (bf16[784,512]{1,0:T(8,128)(2,1)}, bf16[784,512]{1,0:T(8,128)(2,1)}, f32[784,512]{1,0:T(8,128)}, f32[784,512]{1,0:T(8,128)}, bf16[12,2,1568,512...) custom-call(bf16[784,1536]{1,0:T(8,128)(2,1)} %shard_map.173.own, bf16[784,1536]{1,0:T(8,128)(2,1)} %collective-permute-done.14.rec), custom_call_target="tpu_custom_call" | custom-call | tf_op jit(solution)/shard_map/pallas_call | solution.py:151
  148.8 9.3 %shard_map.175 = (bf16[784,1024]{1,0:T(8,128)(2,1)}, bf16[784,1024]{1,0:T(8,128)(2,1)}, bf16[784,1536]{1,0:T(8,128)(2,1)}) custom-call(s32[6]{0:T(128)} %stack.74.ids, bf16[3,784,1024]{2,1,0:T(8,128)(2,1)} %mine.5, bf16[2,784,1024]{2,1,0:T(8,128)(2,1)} %collective-permute-done.13.got, f32[1,1024]{1,0:T(1,128)} %bitcast.180, f32[1,1024]{1,0:T(1,128)} %bitcast.183, ...), custom_call_target="tpu_custom_call" | custom-call | tf_op jit(solution)/shard_map/pallas_call | solution.py:533
  179.3 29.7 %shard_map.177 = (bf16[784,512]{1,0:T(8,128)(2,1)}, bf16[784,512]{1,0:T(8,128)(2,1)}, f32[784,512]{1,0:T(8,128)}, f32[784,512]{1,0:T(8,128)}, bf16[12,2,1568,512...) custom-call(bf16[784,1536]{1,0:T(8,128)(2,1)} %shard_map.176.own, bf16[784,1536]{1,0:T(8,128)(2,1)} %collective-permute-done.16.rec), custom_call_target="tpu_custom_call" | custom-call | tf_op jit(solution)/shard_map/pallas_call | solution.py:151
  209.1 10.3 %collective-permute-done.9.cot_got = bf16[1,784,1024]{2,1,0:T(8,128)(2,1)} collective-permute-done((bf16[1,784,1024]{2,1,0:T(8,128)(2,1)}, bf16[1,784,1024]{2,1,0:T(8,128)(2,1)}, u32[]{:S(2)}, u32[]{:S(2)}) %collective-permute-start.9) | collective-permute-done | bytes 1605664 | tf_op jit(solution)/shard_map/ppermute | solution.py:1050
  227.1 52.3 %shard_map.178 = (bf16[784,4096]{1,0:T(8,128)(2,1)}, bf16[784,4096]{1,0:T(8,128)(2,1)}, bf16[784,1024]{1,0:T(8,128)(2,1)}, bf16[784,1024]{1,0:T(8,128)(2,1)}, bf...) custom-call(s32[6]{0:T(128)} %stack.72.ids, ...), custom_call_target="tpu_custom_call" | custom-call | tf_op jit(solution)/shard_map/pallas_call | solution.py:533
  282.9 52.7 %shard_map.179 = (bf16[784,4096]{1,0:T(8,128)(2,1)}, bf16[784,4096]{1,0:T(8,128)(2,1)}, bf16[784,1024]{1,0:T(8,128)(2,1)}, bf16[784,1024]{1,0:T(8,128)(2,1)}, bf...) custom-call(s32[6]{0:T(128)} %stack.73.ids, ...), custom_call_target="tpu_custom_call", output_to_operand_aliasing={{7}: (24, {})} | custom-call | tf_op jit(solution)/shard_map/pallas_call | solution.py:533
  341.0 52.4 %shard_map.180 = (bf16[784,4096]{1,0:T(8,128)(2,1)}, bf16[784,4096]{1,0:T(8,128)(2,1)}, bf16[784,1024]{1,0:T(8,128)(2,1)}, bf16[784,1024]{1,0:T(8,128)(2,1)}, bf...) custom-call(s32[6]{0:T(128)} %stack.74.ids, ...), custom_call_target="tpu_custom_call", output_to_operand_aliasing={{7}: (24, {})} | custom-call | tf_op jit(solution)/shard_map/pallas_call | solution.py:533
  393.5 18.2 %shard_map.182 = bf16[4,4,512,256]{3,2,1,0:T(8,128)(2,1)} custom-call(s32[6]{0:T(128)} %stack.72.ids, bf16[784,4096]{1,0:T(8,128)(2,1)} %get-tuple-element.177.refs_0_, bf16[784,4096]{1,0:T(8,128)(2,1)} %get-tuple-element.178.refs_1_, bf16[784,4096]{1,0:T(8,128)(2,1)} %get-tuple-element.179.refs_2_, bf16[784,1024]{1,0:T(8,128)(2,1)} %get-tuple-element.180.refs_3_.refs_6_, ...), custom_call_target="tpu_custom_call" | custom-call | tf_op jit(solution)/shard_map/pallas_call | solution.py:533
  411.8 18.3 %shard_map.183 = bf16[4,4,512,256]{3,2,1,0:T(8,128)(2,1)} custom-call(s32[6]{0:T(128)} %stack.72.ids, bf16[784,1024]{1,0:T(8,128)(2,1)} %get-tuple-element.192.refs_0_, bf16[784,1024]{1,0:T(8,128)(2,1)} %get-tuple-element.193.refs_1_, bf16[784,1024]{1,0:T(8,128)(2,1)} %get-tuple-element.194.refs_2_, bf16[784,4096]{1,0:T(8,128)(2,1)} %get-tuple-element.188.refs_3_, ...), custom_call_target="tpu_custom_call" | custom-call | tf_op jit(solution)/shard_map/pallas_call | solution.py:533
  453.1 22.0 %shard_map.184 = (bf16[4,1152,256]{2,1,0:T(8,128)(2,1)}, bf16[4,1152,256]{2,1,0:T(8,128)(2,1)}, bf16[4,1152,256]{2,1,0:T(8,128)(2,1)}, bf16[4,1152,256]{2,1,0:T(8,128)(2,1)}) custom-call(s32[6]{0:T(128)} %stack.72.ids, bf16[784,1024]{1,0:T(8,128)(2,1)} %get-tuple-element.192.refs_0_, bf16[784,1024]{1,0:T(8,128)(2,1)} %get-tuple-element.193.refs_1_, ...), custom_call_target="tpu_custom_call" | custom-call | tf_op jit(solution)/shard_map/pallas_call | solution.py:533
  475.0 20.6 %shard_map.185 = (bf16[4,1152,256]{2,1,0:T(8,128)(2,1)}, bf16[4,1152,256]{2,1,0:T(8,128)(2,1)}, bf16[4,1152,256]{2,1,0:T(8,128)(2,1)}, bf16[4,1152,256]{2,1,0:T(8,128)(2,1)}) custom-call(s32[6]{0:T(128)} %stack.72.ids, bf16[784,4096]{1,0:T(8,128)(2,1)} %get-tuple-element.177.refs_0_, ...), custom_call_target="tpu_custom_call", output_to_operand_aliasing={{0}: (11, {}), {1}: (12, {}), {2}: (13, {}), {3}: (14, {})} | custom-call | tf_op jit(solution)/shard_map/pallas_call | solution.py:533
  507.7 52.7 %shard_map.187 = (bf16[784,1536]{1,0:T(8,128)(2,1)}, bf16[784,1536]{1,0:T(8,128)(2,1)}) custom-call(bf16[784,1536]{1,0:T(8,128)(2,1)} %shard_map.170.own, bf16[784,1536]{1,0:T(8,128)(2,1)} %copy-done.12, bf16[784,512]{1,0:T(8,128)(2,1)} %get-tuple-element.207.do_o, bf16[3,784,512]{2,1,0:T(8,128)(2,1)} %collective-permute-done.30.do_r, ...), custom_call_target="tpu_custom_call" | custom-call | flops 49999998976 | tf_op jit(solution)/shard_map/pallas_call | solution.py:255
  561.2 52.8 %shard_map.188 = (bf16[784,1536]{1,0:T(8,128)(2,1)}, bf16[784,1536]{1,0:T(8,128)(2,1)}) custom-call(bf16[784,1536]{1,0:T(8,128)(2,1)} %shard_map.173.own, bf16[784,1536]{1,0:T(8,128)(2,1)} %collective-permute-done.14.rec, bf16[784,512]{1,0:T(8,128)(2,1)} %get-tuple-element.216.do_o, bf16[3,784,512]{2,1,0:T(8,128)(2,1)} %collective-permute-done.30.do_r, ...), custom_call_target="tpu_custom_call" | custom-call | flops 49999998976 | tf_op jit(solution)/shard_map/pallas_call | solution.py:255
  626.7 52.8 %shard_map.190 = (bf16[784,1536]{1,0:T(8,128)(2,1)}, bf16[784,1536]{1,0:T(8,128)(2,1)}) custom-call(bf16[784,1536]{1,0:T(8,128)(2,1)} %shard_map.176.own, bf16[784,1536]{1,0:T(8,128)(2,1)} %collective-permute-done.16.rec, bf16[784,512]{1,0:T(8,128)(2,1)} %get-tuple-element.227.do_o, bf16[3,784,512]{2,1,0:T(8,128)(2,1)} %collective-permute-done.30.do_r, ...), custom_call_target="tpu_custom_call" | custom-call | flops 49999998976 | tf_op jit(solution)/shard_map/pallas_call | solution.py:255
  679.6 14.4 %shard_map.191 = (bf16[784,1024]{1,0:T(8,128)(2,1)}, f32[8,1024]{1,0:T(8,128)}, f32[8,1536]{1,0:T(8,128)}, f32[8,1536]{1,0:T(8,128)}) custom-call(s32[6]{0:T(128)} %stack.72.ids, bf16[784,1536]{1,0:T(8,128)(2,1)} %get-tuple-element.213.d_mine.refs_0_, bf16[784,1536]{1,0:T(8,128)(2,1)} %collective-permute-done.34.d_other.refs_3_, ...), custom_call_target="tpu_custom_call" | custom-call | flops 49999998976 | tf_op jit(solution)/shard_map/pallas_call | solution.py:533
  698.0 14.5 %shard_map.192 = (bf16[784,1024]{1,0:T(8,128)(2,1)}, f32[8,1024]{1,0:T(8,128)}, f32[8,1536]{1,0:T(8,128)}, f32[8,1536]{1,0:T(8,128)}) custom-call(s32[6]{0:T(128)} %stack.73.ids, bf16[784,1536]{1,0:T(8,128)(2,1)} %get-tuple-element.221.d_mine.refs_1_, bf16[784,1536]{1,0:T(8,128)(2,1)} %collective-permute-done.35.d_other.refs_4_, ...), custom_call_target="tpu_custom_call" | custom-call | flops 49999998976 | tf_op jit(solution)/shard_map/pallas_call | solution.py:533
  712.6 15.1 %shard_map.193 = bf16[4,4,384,256]{3,2,1,0:T(8,128)(2,1)} custom-call(s32[6]{0:T(128)} %stack.72.ids, bf16[784,1536]{1,0:T(8,128)(2,1)} %get-tuple-element.213.d_mine.refs_0_, bf16[784,1536]{1,0:T(8,128)(2,1)} %get-tuple-element.221.d_mine.refs_1_, bf16[784,1536]{1,0:T(8,128)(2,1)} %get-tuple-element.232.refs_2_.d_mine, ...), custom_call_target="tpu_custom_call" | custom-call | flops 24999999488 | tf_op jit(solution)/shard_map/pallas_call | solution.py:533
  727.9 14.6 %shard_map.194 = (bf16[784,1024]{1,0:T(8,128)(2,1)}, f32[8,1024]{1,0:T(8,128)}, f32[8,1536]{1,0:T(8,128)}, f32[8,1536]{1,0:T(8,128)}) custom-call(s32[6]{0:T(128)} %stack.74.ids, bf16[784,1536]{1,0:T(8,128)(2,1)} %get-tuple-element.232.refs_2_.d_mine, bf16[784,1536]{1,0:T(8,128)(2,1)} %collective-permute-done.36.refs_5_.d_other, ...), custom_call_target="tpu_custom_call" | custom-call | flops 49999998976 | tf_op jit(solution)/shard_map/pallas_call | solution.py:533
  746.8 17.0 %shard_map.195 = (bf16[4,384,256]{2,1,0:T(8,128)(2,1)}, bf16[4,384,256]{2,1,0:T(8,128)(2,1)}, bf16[4,384,256]{2,1,0:T(8,128)(2,1)}, bf16[4,384,256]{2,1,0:T(8,128)(2,1)}) custom-call(s32[6]{0:T(128)} %stack.72.ids, bf16[784,1536]{1,0:T(8,128)(2,1)} %get-tuple-element.213.d_mine.refs_0_, bf16[784,1536]{1,0:T(8,128)(2,1)} %get-tuple-element.221.d_mine.refs_1_, ...), custom_call_target="tpu_custom_call" | custom-call | flops 24999999488 | tf_op jit(solution)/shard_map/pallas_call | solution.py:533
  775.6 12.4 %collective-permute-done.43.refs_1_ = bf16[1680,256]{1,0:T(8,128)(2,1)} collective-permute-done((bf16[1680,256]{1,0:T(8,128)(2,1)}, bf16[1680,256]{1,0:T(8,128)(2,1)}, u32[]{:S(2)}, u32[]{:S(2)}) %collective-permute-start.43) | collective-permute-done | bytes 860192 | tf_op jit(solution)/shard_map/ppermute | solution.py:1039
  788.1 19.2 %collective-permute-done.45.refs_3_ = bf16[1680,256]{1,0:T(8,128)(2,1)S(1)} collective-permute-done((bf16[1680,256]{1,0:T(8,128)(2,1)}, bf16[1680,256]{1,0:T(8,128)(2,1)S(1)}, u32[]{:S(2)}, u32[]{:S(2)}) %collective-permute-start.45) | collective-permute-done | bytes 860192 | tf_op jit(solution)/shard_map/ppermute | solution.py:1043
  826.5 15.2 %collective-permute-done.47 = bf16[784,1024]{1,0:T(8,128)(2,1)} collective-permute-done((bf16[784,1024]{1,0:T(8,128)(2,1)}, bf16[784,1024]{1,0:T(8,128)(2,1)}, u32[]{:S(2)}, u32[]{:S(2)}) %collective-permute-start.47) | collective-permute-done | bytes 1605664 | tf_op jit(solution)/shard_map/ppermute | solution.py:1050
  (292 shorter events, 227.9 us)
Async XLA Ops:
  38.1 60.6 %collective-permute-start.13 = (bf16[2,784,1024]{2,1,0:T(8,128)(2,1)}, bf16[2,784,1024]{2,1,0:T(8,128)(2,1)}, u32[]{:S(2)}, u32[]{:S(2)}) collective-permute-start(bf16[2,784,1024]{2,1,0:T(8,128)(2,1)} %slice.191), channel_id=1, source_target_pairs={{1,2},{2,1},{5,6},{6,5},{9,10},{10,9},{13,14},{14,13},{17,18},{18,... | collective-permute-start | bytes 9633800 | tf_op jit(solution)/shard_map/ppermute | solution.py:1050
  55.5 43.2 %collective-permute-start.10 = (bf16[512,1024]{1,0:T(8,128)(2,1)S(1)}, bf16[512,1024]{1,0:T(8,128)(2,1)}, u32[]{:S(2)}, u32[]{:S(2)}) collective-permute-start(bf16[512,1024]{1,0:T(8,128)(2,1)S(1)} %constant_dynamic-slice_fusion.2), channel_id=1, source_target_pairs={{0,1},{1,0},{2,3},{3,2},{4,5},{5,4},{6,7},{7,6},{8,9},{9,8},{10,11... | collective-permute-start | bytes 3145736 | tf_op jit(solution)/shard_map/ppermute | solution.py:1039
  162.6 120.3 %collective-permute-start.23 = (bf16[2,784,1024]{2,1,0:T(8,128)(2,1)}, bf16[2,784,1024]{2,1,0:T(8,128)(2,1)}, u32[]{:S(2)}, u32[]{:S(2)}) collective-permute-start(bf16[2,784,1024]{2,1,0:T(8,128)(2,1)} %slice.202), channel_id=1, source_target_pairs={{1,2},{2,1},{5,6},{6,5},{9,10},{10,9},{13,14},{14,13},{17,18},{18,... | collective-permute-start | bytes 9633800 | tf_op jit(solution)/shard_map/ppermute | solution.py:1050
  168.8 50.5 %collective-permute-start.9 = (bf16[1,784,1024]{2,1,0:T(8,128)(2,1)}, bf16[1,784,1024]{2,1,0:T(8,128)(2,1)}, u32[]{:S(2)}, u32[]{:S(2)}) collective-permute-start(bf16[1,784,1024]{2,1,0:T(8,128)(2,1)} %slice.200), channel_id=1, source_target_pairs={{1,2},{2,1},{5,6},{6,5},{9,10},{10,9},{13,14},{14,13},{17,18},{18,... | collective-permute-start | bytes 4816904 | tf_op jit(solution)/shard_map/ppermute | solution.py:1050
  171.7 47.7 %collective-permute-start.8 = (bf16[784,512]{1,0:T(8,128)(2,1)}, bf16[784,512]{1,0:T(8,128)(2,1)S(1)}, u32[]{:S(2)}, u32[]{:S(2)}) collective-permute-start(bf16[784,512]{1,0:T(8,128)(2,1)} %get-tuple-element.152.o_r), channel_id=1, source_target_pairs={{0,2},{2,0},{1,3},{3,1},{4,6},{6,4},{5,7},{7,5},{8,10},{10,8},{9,1... | collective-permute-start | bytes 2408456 | tf_op jit(solution)/shard_map/ppermute | solution.py:1039
  171.7 48.2 %collective-permute-start.19 = (bf16[512,1024]{1,0:T(8,128)(2,1)}, bf16[512,1024]{1,0:T(8,128)(2,1)}, u32[]{:S(2)}, u32[]{:S(2)}) collective-permute-start(bf16[512,1024]{1,0:T(8,128)(2,1)} %collective-permute-done.10.d0), channel_id=1, source_target_pairs={{0,2},{2,0},{1,3},{3,1},{4,6},{6,4},{5,7},{7,5},{8,10},{10,8},{9,1... | collective-permute-start | bytes 3145736 | tf_op jit(solution)/shard_map/ppermute | solution.py:1039
  219.9 63.0 %collective-permute-start.22 = (bf16[784,512]{1,0:T(8,128)(2,1)}, bf16[784,512]{1,0:T(8,128)(2,1)}, u32[]{:S(2)}, u32[]{:S(2)}) collective-permute-start(bf16[784,512]{1,0:T(8,128)(2,1)} %get-tuple-element.169.o_r), channel_id=1, source_target_pairs={{0,2},{2,0},{1,3},{3,1},{4,6},{6,4},{5,7},{7,5},{8,10},{10,8},{9,1... | collective-permute-start | bytes 2408456 | tf_op jit(solution)/shard_map/ppermute | solution.py:1039
  279.4 58.4 %collective-permute-start.21 = (bf16[784,1024]{1,0:T(8,128)(2,1)}, bf16[784,1024]{1,0:T(8,128)(2,1)}, u32[]{:S(2)}, u32[]{:S(2)}) collective-permute-start(bf16[784,1024]{1,0:T(8,128)(2,1)} %get-tuple-element.165), channel_id=1, source_target_pairs={{1,2},{2,1},{5,6},{6,5},{9,10},{10,9},{13,14},{14,13},{17,18},{18,... | collective-permute-start | bytes 4816904 | tf_op jit(solution)/shard_map/ppermute | solution.py:1050
  335.6 57.8 %collective-permute-start.28 = (bf16[784,1024]{1,0:T(8,128)(2,1)}, bf16[784,1024]{1,0:T(8,128)(2,1)}, u32[]{:S(2)}, u32[]{:S(2)}) collective-permute-start(bf16[784,1024]{1,0:T(8,128)(2,1)} %get-tuple-element.191), channel_id=1, source_target_pairs={{1,2},{2,1},{5,6},{6,5},{9,10},{10,9},{13,14},{14,13},{17,18},{18,... | collective-permute-start | bytes 4816904 | tf_op jit(solution)/shard_map/ppermute | solution.py:1050
  411.7 41.4 %collective-permute-start.26 = (bf16[4,4,512,256]{3,2,1,0:T(8,128)(2,1)}, bf16[4,4,512,256]{3,2,1,0:T(8,128)(2,1)}, u32[]{:S(2)}, u32[]{:S(2)}) collective-permute-start(bf16[4,4,512,256]{3,2,1,0:T(8,128)(2,1)} %shard_map.182), channel_id=1, source_target_pairs={{0,2},{2,0},{1,3},{3,1},{4,6},{6,4},{5,7},{7,5},{8,10},{10,8},{9,1... | collective-permute-start | bytes 12582920 | tf_op jit(solution)/shard_map/ppermute | solution.py:1039
  430.5 77.2 %collective-permute-start.30 = (bf16[3,784,512]{2,1,0:T(8,128)(2,1)S(1)}, bf16[3,784,512]{2,1,0:T(8,128)(2,1)}, u32[]{:S(2)}, u32[]{:S(2)}) collective-permute-start(bf16[3,784,512]{2,1,0:T(8,128)(2,1)S(1)} %copy-done.7), channel_id=1, source_target_pairs={{0,2},{2,0},{1,3},{3,1},{4,6},{6,4},{5,7},{7,5},{8,10},{10,8},{9,1... | collective-permute-start | bytes 7225352 | tf_op jit(solution)/shard_map/ppermute | solution.py:1039
  442.0 53.6 %collective-permute-start.25 = (bf16[4,4,128,256]{3,2,1,0:T(8,128)(2,1)}, bf16[4,4,128,256]{3,2,1,0:T(8,128)(2,1)S(1)}, u32[]{:S(2)}, u32[]{:S(2)}) collective-permute-start(bf16[4,4,128,256]{3,2,1,0:T(8,128)(2,1)} %shard_map.181), channel_id=1, source_target_pairs={{0,2},{2,0},{1,3},{3,1},{4,6},{6,4},{5,7},{7,5},{8,10},{10,8},{9,1... | collective-permute-start | bytes 3145736 | tf_op jit(solution)/shard_map/ppermute | solution.py:1039
  505.1 56.2 %collective-permute-start.31 = (bf16[4608,256]{1,0:T(8,128)(2,1)}, bf16[4608,256]{1,0:T(8,128)(2,1)}, u32[]{:S(2)}, u32[]{:S(2)}) collective-permute-start(bf16[4608,256]{1,0:T(8,128)(2,1)} %bitcast.136), channel_id=1, source_target_pairs={{0,5},{1,4},{4,1},{5,0},{2,7},{3,6},{6,3},{7,2},{8,13},{9,12},{12,... | collective-permute-start | bytes 7077896 | tf_op jit(solution)/shard_map/ppermute | solution.py:1043
  505.1 109.0 %collective-permute-start.32 = (bf16[4608,256]{1,0:T(8,128)(2,1)}, bf16[4608,256]{1,0:T(8,128)(2,1)}, u32[]{:S(2)}, u32[]{:S(2)}) collective-permute-start(bf16[4608,256]{1,0:T(8,128)(2,1)} %bitcast.134), channel_id=1, source_target_pairs={{0,4},{4,0},{1,5},{5,1},{2,6},{6,2},{3,7},{7,3},{8,12},{12,8},{9,1... | collective-permute-start | bytes 7077896 | tf_op jit(solution)/shard_map/ppermute | solution.py:1039
  505.8 108.3 %collective-permute-start.33 = (bf16[4608,256]{1,0:T(8,128)(2,1)}, bf16[4608,256]{1,0:T(8,128)(2,1)}, u32[]{:S(2)}, u32[]{:S(2)}) collective-permute-start(bf16[4608,256]{1,0:T(8,128)(2,1)} %bitcast.135), channel_id=1, source_target_pairs={{0,1},{1,0},{2,3},{3,2},{4,5},{5,4},{6,7},{7,6},{8,9},{9,8},{10,11... | collective-permute-start | bytes 7077896 | tf_op jit(solution)/shard_map/ppermute | solution.py:1039
  560.4 119.1 %collective-permute-start.34 = (bf16[784,1536]{1,0:T(8,128)(2,1)}, bf16[784,1536]{1,0:T(8,128)(2,1)}, u32[]{:S(2)}, u32[]{:S(2)}) collective-permute-start(bf16[784,1536]{1,0:T(8,128)(2,1)} %get-tuple-element.233), channel_id=1, source_target_pairs={{0,2},{2,0},{1,3},{3,1},{4,6},{6,4},{5,7},{7,5},{8,10},{10,8},{9,1... | collective-permute-start | bytes 7225352 | tf_op jit(solution)/shard_map/ppermute | solution.py:1039
  623.2 56.4 %collective-permute-start.37 = (bf16[1152,256]{1,0:T(8,128)(2,1)S(1)}, bf16[1152,256]{1,0:T(8,128)(2,1)}, u32[]{:S(2)}, u32[]{:S(2)}) collective-permute-start(bf16[1152,256]{1,0:T(8,128)(2,1)S(1)} %get-tuple-element.306), channel_id=1, source_target_pairs={{0,8},{8,0},{16,24},{24,16},{1,9},{9,1},{17,25},{25,17},{2,10},{10... | collective-permute-start | bytes 1769480 | tf_op jit(solution)/shard_map/ppermute | solution.py:1039
  623.4 56.2 %collective-permute-start.38 = (bf16[1152,256]{1,0:T(8,128)(2,1)S(1)}, bf16[1152,256]{1,0:T(8,128)(2,1)}, u32[]{:S(2)}, u32[]{:S(2)}) collective-permute-start(bf16[1152,256]{1,0:T(8,128)(2,1)S(1)} %get-tuple-element.305), channel_id=1, source_target_pairs={{0,16},{8,24},{16,0},{24,8},{1,17},{9,25},{17,1},{25,9},{2,18},{10... | collective-permute-start | bytes 1769480 | tf_op jit(solution)/shard_map/ppermute | solution.py:1039
  625.7 53.9 %collective-permute-start.39 = (bf16[1152,256]{1,0:T(8,128)(2,1)S(1)}, bf16[1152,256]{1,0:T(8,128)(2,1)}, u32[]{:S(2)}, u32[]{:S(2)}) collective-permute-start(bf16[1152,256]{1,0:T(8,128)(2,1)S(1)} %get-tuple-element.304), channel_id=1, source_target_pairs={{0,24},{8,16},{16,8},{24,0},{1,25},{9,17},{17,9},{25,1},{2,26},{10... | collective-permute-start | bytes 1769480 | tf_op jit(solution)/shard_map/ppermute | solution.py:1039
  625.9 72.1 %collective-permute-start.35 = (bf16[784,1536]{1,0:T(8,128)(2,1)}, bf16[784,1536]{1,0:T(8,128)(2,1)}, u32[]{:S(2)}, u32[]{:S(2)}) collective-permute-start(bf16[784,1536]{1,0:T(8,128)(2,1)} %get-tuple-element.234), channel_id=1, source_target_pairs={{0,2},{2,0},{1,3},{3,1},{4,6},{6,4},{5,7},{7,5},{8,10},{10,8},{9,1... | collective-permute-start | bytes 7225352 | tf_op jit(solution)/shard_map/ppermute | solution.py:1039
  694.0 52.8 %collective-permute-start.41 = (bf16[784,1024]{1,0:T(8,128)(2,1)}, bf16[784,1024]{1,0:T(8,128)(2,1)S(1)}, u32[]{:S(2)}, u32[]{:S(2)}) collective-permute-start(bf16[784,1024]{1,0:T(8,128)(2,1)} %get-tuple-element.237), channel_id=1, source_target_pairs={{1,2},{2,1},{5,6},{6,5},{9,10},{10,9},{13,14},{14,13},{17,18},{18,... | collective-permute-start | bytes 4816904 | tf_op jit(solution)/shard_map/ppermute | solution.py:1050
  770.0 54.7 %collective-permute-start.46 = (bf16[784,1024]{1,0:T(8,128)(2,1)}, bf16[784,1024]{1,0:T(8,128)(2,1)}, u32[]{:S(2)}, u32[]{:S(2)}) collective-permute-start(bf16[784,1024]{1,0:T(8,128)(2,1)} %get-tuple-element.239), channel_id=1, source_target_pairs={{1,2},{2,1},{5,6},{6,5},{9,10},{10,9},{13,14},{14,13},{17,18},{18,... | collective-permute-start | bytes 4816904 | tf_op jit(solution)/shard_map/ppermute | solution.py:1050
  772.8 68.8 %collective-permute-start.47 = (bf16[784,1024]{1,0:T(8,128)(2,1)}, bf16[784,1024]{1,0:T(8,128)(2,1)}, u32[]{:S(2)}, u32[]{:S(2)}) collective-permute-start(bf16[784,1024]{1,0:T(8,128)(2,1)} %get-tuple-element.244), channel_id=1, source_target_pairs={{1,2},{2,1},{5,6},{6,5},{9,10},{10,9},{13,14},{14,13},{17,18},{18,... | collective-permute-start | bytes 4816904 | tf_op jit(solution)/shard_map/ppermute | solution.py:1050
  824.7 39.9 %collective-permute-start.52 = (f32[576,256]{1,0:T(8,128)S(1)}, f32[576,256]{1,0:T(8,128)S(1)}, u32[]{:S(2)}, u32[]{:S(2)}) collective-permute-start(f32[576,256]{1,0:T(8,128)S(1)} %pad_maximum_fusion.7), channel_id=1, source_target_pairs={{0,2},{2,0},{1,3},{3,1},{4,6},{6,4},{5,7},{7,5},{8,10},{10,8},{9,1... | collective-permute-start | bytes 1769480 | tf_op jit(solution)/shard_map/ppermute | solution.py:1039
  (65 other events, 1039.7 us)

commit v4 on v3

--- a/solution.py
+++ b/solution.py
@@ -780,6 +780,7 @@
         args + tuple(before),
         scratch=[pltpu.VMEM((rows, width), F32)] * 3
         + [pltpu.VMEM((inner, chunk), BF), pltpu.VMEM((chunk, width), BF)],
+        flops=COST,
         limit=62,
         aliases=[(1 + len(args), 7)] if before else (),
     )
@@ -911,7 +912,7 @@
     block = lambda i, ids: (0, 2 * jnp.where(i == 0, 1 - ids[3], ids[3]) + column_half(ids, rec))
     groups = [(d_out, (rows, width), lambda i, ids: (0, 0)), (active, (rows, cols), block)]
     shape = (4, chips, parts * width // (2 * chips), cols // parts)
-    return grad_call(grad_down_kernel, ids, (2,), groups, shape, rec, 0, joint)
+    return grad_call(grad_down_kernel, ids, (2,), groups, shape, rec, COST // 2, joint)
 
 
 def grad_up_part(ids, chips, d_pre, normed, rec, joint=None):
@@ -923,7 +924,7 @@
         (normed, (rows, cols), lambda i, ids: (0, column_half(ids, rec))),
         (normed, (rows, cols), lambda i, ids: (0, 2 + column_half(ids, rec))),
     ]
-    return grad_call(grad_up_kernel, ids, (chips,), groups, (4, chips, ff // (2 * chips), cols), rec, 0, joint)
+    return grad_call(grad_up_kernel, ids, (chips,), groups, (4, chips, ff // (2 * chips), cols), rec, COST // 2, joint)
 
 
 def grad_out_part(ids, chips, d_branch, mine, other, rec, joint=None):
@@ -931,7 +932,7 @@
     cols = width // 4
     half = lambda i, ids: (0, column_half(ids, rec))
     groups = [(d_branch, (rows, width), lambda i, ids: (0, 0)), (mine, (rows, cols), half), (other, (rows, cols), half)]
-    return grad_call(grad_out_kernel, ids, (1,), groups, (4, chips, width // (2 * chips), cols), rec, 0, joint)
+    return grad_call(grad_out_kernel, ids, (1,), groups, (4, chips, width // (2 * chips), cols), rec, COST // 2, joint)
 
 
 def grad_qkv_part(ids, chips, mine, other, normed, rec, joint=None):
@@ -944,9 +945,8 @@
         (normed, (rows, cols), lambda i, ids: (0, column_half(ids, rec))),
         (normed, (rows, cols), lambda i, ids: (0, 2 + column_half(ids, rec))),
     ]
-    flops = COST // 2
     return grad_call(
-        grad_qkv_kernel, ids, (3,), groups, (4, chips, 3 * width // (2 * chips), cols), rec, flops, joint, steps=3
+        grad_qkv_kernel, ids, (3,), groups, (4, chips, 3 * width // (2 * chips), cols), rec, COST // 2, joint, steps=3
     )
 
 
@@ -1075,7 +1075,7 @@
 
 def as_lines(x, cols):
     parts = []
-    for _ in range(3):
+    for _ in range(2):
         part = lax.reduce_precision(x, 8, 7)
         parts.append(part.astype(BF))
         x = x - part
@@ -1083,7 +1083,7 @@
 
 
 def from_lines(lines, shape):
-    return lines.astype(F32).reshape((3,) + shape).sum(0)
+    return lines.astype(F32).reshape((2,) + shape).sum(0)
 
 
 def send_sums(part):
@@ -1134,7 +1134,8 @@
     qkv_bias = jnp.concatenate([biases[1], jnp.zeros_like(biases[1]), biases[2]])[None]
     ids = [jnp.stack([core, swap, (count > s).astype(jnp.int32), x, y, z]).astype(jnp.int32) for s in range(slots)]
 
-    got_first = after(got_first, (rest, piece, down_piece))
+    cot_first, cot_others = after((cotangent[:1], cotangent[1:]), qkv_0)
+    got_first = after(got_first, (rest, piece, down_piece, cot_first, cot_others))
     blocks, normed, saved, ctx_mine, ctx_other = [], [], [], [], []
     for s in range(slots):
         got, slot = (got_first, 0) if s == 0 else (got_rest, s - 1)
@@ -1164,8 +1165,8 @@
     far = (far_0, far_1, far_2, far_3)
     far_down = (down_0, down_1, down_2, down_3)
 
-    first, others = swap_owner(cotangent[:1], chips), swap_owner(cotangent[1:], chips)
-    got_cot = [(first, 0)] + [(others, s - 1) for s in range(1, slots)]
+    others = swap_owner(after(cot_others, here), chips)
+    got_cot = [(swap_owner(cot_first, chips), 0)] + [(others, s - 1) for s in range(1, slots)]
     fed, got_result = [], []
     before = ()
     for s in range(slots):
@@ -1189,7 +1190,7 @@
     rows = rows_down + rows_up + rows_out
     joint = grad_down_part(ids[0], chips, d_out, active, swap_axis(sent_down, "core"), (rows, 0, []))
     joint = grad_up_part(
-        ids[0], chips, d_pre, normed2, after(swap_axis(sent_up, "core"), got_result[2]),
+        ids[0], chips, d_pre, normed2, swap_axis(sent_up, "core"),
         (rows, rows_down // rows_up, joint),
     )
     joint = grad_out_part(
@@ -1208,7 +1209,6 @@
             ids[s], d_mine[s], after(d_other[s], first), w_qkv, qkv_far, blocks[s], d_branch[s], gains
         )
         row_grads.append(row_grad)
-        got_rows.append(swap_owner(row_grad, chips))
         sums1.append(sum1)
         sums_mine.append(sum_mine[0])
         sums_other.append(sum_other[0])
@@ -1232,14 +1232,18 @@
             terms = send_chips(sums)
             gate = (gate, [sums[i] for i in range(chips)])
         if s == 2:
-            gate = complete(0, (d_here, terms))
-            gate = complete(1, gate)
+            gate = complete(0, (d_here, terms, got_result[2]))
+    got_rows.append(swap_owner(row_grads[0], chips))
     sent_qkv = grad_qkv_part(ids[0], chips, d_mine, after(d_other, gate), normed, None)
-    row_grad = complete(slots - 1, sent_qkv)
+    gate = complete(1, sent_qkv)
+    got_rows.append(swap_owner(row_grads[1], chips))
     part_qkv = grad_qkv_part(
-        ids[0], chips, d_mine, d_other, normed, after(swap_axis(sent_qkv, "core"), (row_grad, got_rows[0])),
+        ids[0], chips, d_mine, d_other, normed, after(swap_axis(sent_qkv, "core"), (gate, got_rows[0])),
         (sent_qkv.shape[2], 0, []),
     )
+    qkv_rows = part_qkv[0].shape[1]
+    qkv_terms = send_sums([part.reshape(-1, cols) for part in part_qkv])
+    complete(2, (part_qkv, got_rows[1]))
     total1 = sum(sums1)
     total_mine, total_other = sum(sums_mine), sum(sums_other)
     grad_bq = in_order(core, total_mine[:inner], total_other[:inner])
@@ -1249,12 +1253,9 @@
     )
     lines = lines + swap_axis(lines, "core")
     shape = lines.shape
-    under = as_lines(lines, cols)
-    qkv_rows = part_qkv[0].shape[1]
-    qkv_terms = send_sums([jnp.concatenate([part.reshape(-1, cols), under]) for part in part_qkv])
-
+    lines = sum(send_sums([lines] * 4))
+    got_rows.append(swap_owner(after(row_grads[2], lines), chips))
     sums = add_chips(ids[0], qkv_terms, chips, qkv_rows)
-    lines = sum(from_lines(term[chips * qkv_rows :], shape) for term in qkv_terms)
     under = as_lines(lines, cols)
     sends = [jnp.concatenate([sums[i], under]) for i in range(chips)]
     qkv_terms = send_chips(sends)

time: 881 us -> 827 us (0.939); the launches traced: 868 us -> 823 us
  waiting for transfers between devices: 88.7 us -> 53.3 us
  other arithmetic: 36 us -> 26.9 us
    ppermute x10, waiting for transfers between devices: 33.8 us -> 1.45 us  [swap_owner(): return lax.ppermute(x, AXES, pairs)]
    ppermute x2 -> x3, waiting for transfers between devices: 19.2 us -> 4.01 us  [swap_across(): return lax.ppermute(x, ('mid', 'grp'), [(0, 3), (1, 2), (2, 1), (3, 0)])]
    ppermute x41 -> x43, waiting for transfers between devices: 35.8 us -> 47.8 us  [swap_axis(): return lax.ppermute(x, axis, [(i, i ^ step) for i in range(size)])]
    ppermute x41 -> x43, starting transfers between devices: 25.6 us -> 24.5 us  [swap_axis(): return lax.ppermute(x, axis, [(i, i ^ step) for i in range(size)])]
  transfers between devices with their start and end apart: 53 -> 56, of which waited for: 12 -> 11; matrix products, arithmetic and copies ran while one was open for 8% -> 7% of each run, Pallas kernels for 67% -> 73%
where the time goes in v4:
time: 827 us; the launch traced here: 823 us
  Pallas kernels  636 us (77%)
  starting transfers between devices  59.7 us (7%)
  waiting for transfers between devices  53.3 us (6%)
  local copies, waits for them, and re-layouts  44 us (5%)
  other arithmetic  26.9 us (3%)
    pallas_call x22, Pallas kernels, call(): pl.pallas_call(kernel, grid_spec=pltpu.PrefetchScalarGridSpec(num_scalar_...  389 us
    pallas_call x3, Pallas kernels, attend_back(): pl.pallas_call(functools.partial(attend_back_kernel, nb=nb, np_=np_, rem=...  158 us
    pallas_call x3, Pallas kernels, attend(): pl.pallas_call(functools.partial(attend_kernel, nb=nb, np_=np_, rem=rem),...  89.1 us
    ppermute x43, waiting for transfers between devices, swap_axis(): return lax.ppermute(x, axis, [(i, i ^ step) for i in range(size)])  47.8 us
    ppermute x10, starting transfers between devices, swap_owner(): return lax.ppermute(x, AXES, pairs)  32.7 us
    ppermute x43, starting transfers between devices, swap_axis(): return lax.ppermute(x, axis, [(i, i ^ step) for i in range(size)])  24.5 us
  transfers between devices with their start and end apart: 56, of which 11 were waited for; matrix products, arithmetic and copies ran while one was open for 7% of the time, Pallas kernels for 73%

profile of v4, /device:TPU:9, one launch (start us, length us, event | category | flops | bytes accessed | tf_op | source)
XLA Modules:
  0.0 822.8 jit_solution(8221120490022855638)
XLA Ops:
  10.0 10.3 %collective-permute-done.2.p0.m0.o0 = bf16[128,3072]{1,0:T(8,128)(2,1)S(1)} collective-permute-done((bf16[128,3072]{1,0:T(8,128)(2,1)S(1)}, bf16[128,3072]{1,0:T(8,128)(2,1)S(1)}, u32[]{:S(2)}, u32[]{:S(2)}) %collective-permute-start.2) | collective-permute-done | bytes 786464 | tf_op jit(solution)/shard_map/ppermute | solution.py:1039
  51.9 8.9 %shard_map.169 = (bf16[784,1024]{1,0:T(8,128)(2,1)}, bf16[784,1024]{1,0:T(8,128)(2,1)}, bf16[784,1536]{1,0:T(8,128)(2,1)}) custom-call(s32[6]{0:T(128)} %stack.72.ids, bf16[3,784,1024]{2,1,0:T(8,128)(2,1)} %mine.5, bf16[1,784,1024]{2,1,0:T(8,128)(2,1)} %collective-permute-done.1.got, f32[1,1024]{1,0:T(1,128)} %bitcast.161, f32[1,1024]{1,0:T(1,128)} %bitcast.164, ...), custom_call_target="tpu_custom_call" | custom-call | tf_op jit(solution)/shard_map/pallas_call | solution.py:533
  70.2 29.6 %shard_map.171 = (bf16[784,512]{1,0:T(8,128)(2,1)}, bf16[784,512]{1,0:T(8,128)(2,1)}, f32[784,512]{1,0:T(8,128)}, f32[784,512]{1,0:T(8,128)}, bf16[12,2,1568,512...) custom-call(bf16[784,1536]{1,0:T(8,128)(2,1)} %shard_map.170.own, bf16[784,1536]{1,0:T(8,128)(2,1)} %copy-done.5), custom_call_target="tpu_custom_call" | custom-call | tf_op jit(solution)/shard_map/pallas_call | solution.py:151
  104.7 9.1 %shard_map.172 = (bf16[784,1024]{1,0:T(8,128)(2,1)}, bf16[784,1024]{1,0:T(8,128)(2,1)}, bf16[784,1536]{1,0:T(8,128)(2,1)}) custom-call(s32[6]{0:T(128)} %stack.73.ids, bf16[3,784,1024]{2,1,0:T(8,128)(2,1)} %mine.5, bf16[2,784,1024]{2,1,0:T(8,128)(2,1)} %collective-permute-done.13.got, f32[1,1024]{1,0:T(1,128)} %bitcast.162, f32[1,1024]{1,0:T(1,128)} %bitcast.165, ...), custom_call_target="tpu_custom_call" | custom-call | tf_op jit(solution)/shard_map/pallas_call | solution.py:533
  125.2 29.7 %shard_map.174 = (bf16[784,512]{1,0:T(8,128)(2,1)}, bf16[784,512]{1,0:T(8,128)(2,1)}, f32[784,512]{1,0:T(8,128)}, f32[784,512]{1,0:T(8,128)}, bf16[12,2,1568,512...) custom-call(bf16[784,1536]{1,0:T(8,128)(2,1)} %shard_map.173.own, bf16[784,1536]{1,0:T(8,128)(2,1)} %copy-done.6), custom_call_target="tpu_custom_call" | custom-call | tf_op jit(solution)/shard_map/pallas_call | solution.py:151
  155.0 9.5 %shard_map.175 = (bf16[784,1024]{1,0:T(8,128)(2,1)}, bf16[784,1024]{1,0:T(8,128)(2,1)}, bf16[784,1536]{1,0:T(8,128)(2,1)}) custom-call(s32[6]{0:T(128)} %stack.74.ids, bf16[3,784,1024]{2,1,0:T(8,128)(2,1)} %mine.5, bf16[2,784,1024]{2,1,0:T(8,128)(2,1)} %collective-permute-done.13.got, f32[1,1024]{1,0:T(1,128)} %bitcast.163, f32[1,1024]{1,0:T(1,128)} %bitcast.166, ...), custom_call_target="tpu_custom_call" | custom-call | tf_op jit(solution)/shard_map/pallas_call | solution.py:533
  178.1 29.7 %shard_map.177 = (bf16[784,512]{1,0:T(8,128)(2,1)}, bf16[784,512]{1,0:T(8,128)(2,1)}, f32[784,512]{1,0:T(8,128)}, f32[784,512]{1,0:T(8,128)}, bf16[12,2,1568,512...) custom-call(bf16[784,1536]{1,0:T(8,128)(2,1)} %shard_map.176.own, bf16[784,1536]{1,0:T(8,128)(2,1)} %copy-done.7), custom_call_target="tpu_custom_call" | custom-call | tf_op jit(solution)/shard_map/pallas_call | solution.py:151
  216.9 52.4 %shard_map.178 = (bf16[784,4096]{1,0:T(8,128)(2,1)}, bf16[784,4096]{1,0:T(8,128)(2,1)}, bf16[784,1024]{1,0:T(8,128)(2,1)}, bf16[784,1024]{1,0:T(8,128)(2,1)}, bf...) custom-call(s32[6]{0:T(128)} %stack.72.ids, ...), custom_call_target="tpu_custom_call" | custom-call | flops 49999998976 | tf_op jit(solution)/shard_map/pallas_call | solution.py:533
  272.0 52.6 %shard_map.179 = (bf16[784,4096]{1,0:T(8,128)(2,1)}, bf16[784,4096]{1,0:T(8,128)(2,1)}, bf16[784,1024]{1,0:T(8,128)(2,1)}, bf16[784,1024]{1,0:T(8,128)(2,1)}, bf...) custom-call(s32[6]{0:T(128)} %stack.73.ids, ...), custom_call_target="tpu_custom_call", output_to_operand_aliasing={{7}: (24, {})} | custom-call | flops 49999998976 | tf_op jit(solution)/shard_map/pallas_call | solution.py:533
  327.5 52.6 %shard_map.180 = (bf16[784,4096]{1,0:T(8,128)(2,1)}, bf16[784,4096]{1,0:T(8,128)(2,1)}, bf16[784,1024]{1,0:T(8,128)(2,1)}, bf16[784,1024]{1,0:T(8,128)(2,1)}, bf...) custom-call(s32[6]{0:T(128)} %stack.74.ids, ...), custom_call_target="tpu_custom_call", output_to_operand_aliasing={{7}: (24, {})} | custom-call | flops 49999998976 | tf_op jit(solution)/shard_map/pallas_call | solution.py:533
  380.1 18.3 %shard_map.183 = bf16[4,4,512,256]{3,2,1,0:T(8,128)(2,1)} custom-call(s32[6]{0:T(128)} %stack.72.ids, bf16[784,1024]{1,0:T(8,128)(2,1)} %get-tuple-element.196.refs_0_, bf16[784,1024]{1,0:T(8,128)(2,1)} %get-tuple-element.197.refs_1_, bf16[784,1024]{1,0:T(8,128)(2,1)} %get-tuple-element.198.refs_2_, bf16[784,4096]{1,0:T(8,128)(2,1)} %get-tuple-element.192.refs_3_, ...), custom_call_target="tpu_custom_call" | custom-call | flops 24999999488 | tf_op jit(solution)/shard_map/pallas_call | solution.py:533
  398.4 18.2 %shard_map.182 = bf16[4,4,512,256]{3,2,1,0:T(8,128)(2,1)} custom-call(s32[6]{0:T(128)} %stack.72.ids, bf16[784,4096]{1,0:T(8,128)(2,1)} %get-tuple-element.183.refs_0_, bf16[784,4096]{1,0:T(8,128)(2,1)} %get-tuple-element.184.refs_1_, bf16[784,4096]{1,0:T(8,128)(2,1)} %get-tuple-element.185.refs_2_, bf16[784,1024]{1,0:T(8,128)(2,1)} %get-tuple-element.186.refs_3_.refs_6_, ...), custom_call_target="tpu_custom_call" | custom-call | flops 24999999488 | tf_op jit(solution)/shard_map/pallas_call | solution.py:533
  430.6 22.0 %shard_map.184 = (bf16[4,1152,256]{2,1,0:T(8,128)(2,1)}, bf16[4,1152,256]{2,1,0:T(8,128)(2,1)}, bf16[4,1152,256]{2,1,0:T(8,128)(2,1)}, bf16[4,1152,256]{2,1,0:T(8,128)(2,1)}) custom-call(s32[6]{0:T(128)} %stack.72.ids, bf16[784,1024]{1,0:T(8,128)(2,1)} %get-tuple-element.196.refs_0_, bf16[784,1024]{1,0:T(8,128)(2,1)} %get-tuple-element.197.refs_1_, ...), custom_call_target="tpu_custom_call" | custom-call | flops 24999999488 | tf_op jit(solution)/shard_map/pallas_call | solution.py:533
  452.6 20.5 %shard_map.185 = (bf16[4,1152,256]{2,1,0:T(8,128)(2,1)}, bf16[4,1152,256]{2,1,0:T(8,128)(2,1)}, bf16[4,1152,256]{2,1,0:T(8,128)(2,1)}, bf16[4,1152,256]{2,1,0:T(8,128)(2,1)}) custom-call(s32[6]{0:T(128)} %stack.72.ids, bf16[784,4096]{1,0:T(8,128)(2,1)} %get-tuple-element.183.refs_0_, ...), custom_call_target="tpu_custom_call", output_to_operand_aliasing={{0}: (11, {}), {1}: (12, {}), {2}: (13, {}), {3}: (14, {})} | custom-call | flops 24999999488 | tf_op jit(solution)/shard_map/pallas_call | solution.py:533
  473.1 8.5 %shard_map.186 = (bf16[4,1152,256]{2,1,0:T(8,128)(2,1)}, bf16[4,1152,256]{2,1,0:T(8,128)(2,1)}, bf16[4,1152,256]{2,1,0:T(8,128)(2,1)}, bf16[4,1152,256]{2,1,0:T(8,128)(2,1)}) custom-call(s32[6]{0:T(128)} %stack.72.ids, ...), custom_call_target="tpu_custom_call", output_to_operand_aliasing={{0}: (11, {}), {1}: (12, {}), {2}: (13, {}), {3}: (14, {})} | custom-call | flops 24999999488 | tf_op jit(solution)/shard_map/pallas_call | solution.py:533
  484.2 52.7 %shard_map.187 = (bf16[784,1536]{1,0:T(8,128)(2,1)}, bf16[784,1536]{1,0:T(8,128)(2,1)}) custom-call(bf16[784,1536]{1,0:T(8,128)(2,1)} %shard_map.170.own, bf16[784,1536]{1,0:T(8,128)(2,1)} %copy-done.5, bf16[784,512]{1,0:T(8,128)(2,1)} %get-tuple-element.211.do_o, bf16[3,784,512]{2,1,0:T(8,128)(2,1)} %collective-permute-done.29.do_r, ...), custom_call_target="tpu_custom_call" | custom-call | flops 49999998976 | tf_op jit(solution)/shard_map/pallas_call | solution.py:255
  537.0 52.7 %shard_map.188 = (bf16[784,1536]{1,0:T(8,128)(2,1)}, bf16[784,1536]{1,0:T(8,128)(2,1)}) custom-call(bf16[784,1536]{1,0:T(8,128)(2,1)} %shard_map.173.own, bf16[784,1536]{1,0:T(8,128)(2,1)} %copy-done.6, bf16[784,512]{1,0:T(8,128)(2,1)} %get-tuple-element.220.do_o, bf16[3,784,512]{2,1,0:T(8,128)(2,1)} %collective-permute-done.29.do_r, ...), custom_call_target="tpu_custom_call" | custom-call | flops 49999998976 | tf_op jit(solution)/shard_map/pallas_call | solution.py:255
  601.4 52.7 %shard_map.190 = (bf16[784,1536]{1,0:T(8,128)(2,1)}, bf16[784,1536]{1,0:T(8,128)(2,1)}) custom-call(bf16[784,1536]{1,0:T(8,128)(2,1)} %shard_map.176.own, bf16[784,1536]{1,0:T(8,128)(2,1)} %copy-done.7, bf16[784,512]{1,0:T(8,128)(2,1)} %get-tuple-element.231.do_o, bf16[3,784,512]{2,1,0:T(8,128)(2,1)} %collective-permute-done.29.do_r, ...), custom_call_target="tpu_custom_call" | custom-call | flops 49999998976 | tf_op jit(solution)/shard_map/pallas_call | solution.py:255
  655.5 14.8 %shard_map.191 = (bf16[784,1024]{1,0:T(8,128)(2,1)}, f32[8,1024]{1,0:T(8,128)}, f32[8,1536]{1,0:T(8,128)}, f32[8,1536]{1,0:T(8,128)}) custom-call(s32[6]{0:T(128)} %stack.72.ids, bf16[784,1536]{1,0:T(8,128)(2,1)} %get-tuple-element.217.d_mine.refs_0_, bf16[784,1536]{1,0:T(8,128)(2,1)} %collective-permute-done.33.d_other.refs_3_, ...), custom_call_target="tpu_custom_call" | custom-call | flops 49999998976 | tf_op jit(solution)/shard_map/pallas_call | solution.py:533
  673.9 15.1 %shard_map.192 = bf16[4,4,384,256]{3,2,1,0:T(8,128)(2,1)} custom-call(s32[6]{0:T(128)} %stack.72.ids, bf16[784,1536]{1,0:T(8,128)(2,1)} %get-tuple-element.217.d_mine.refs_0_, bf16[784,1536]{1,0:T(8,128)(2,1)} %get-tuple-element.225.refs_1_.d_mine, bf16[784,1536]{1,0:T(8,128)(2,1)} %get-tuple-element.236.refs_2_.d_mine, ...), custom_call_target="tpu_custom_call" | custom-call | flops 24999999488 | tf_op jit(solution)/shard_map/pallas_call | solution.py:533
  689.1 14.4 %shard_map.193 = (bf16[784,1024]{1,0:T(8,128)(2,1)}, f32[8,1024]{1,0:T(8,128)}, f32[8,1536]{1,0:T(8,128)}, f32[8,1536]{1,0:T(8,128)}) custom-call(s32[6]{0:T(128)} %stack.73.ids, bf16[784,1536]{1,0:T(8,128)(2,1)} %get-tuple-element.225.refs_1_.d_mine, bf16[784,1536]{1,0:T(8,128)(2,1)} %collective-permute-done.34.refs_4_.d_other, ...), custom_call_target="tpu_custom_call" | custom-call | flops 49999998976 | tf_op jit(solution)/shard_map/pallas_call | solution.py:533
  705.6 16.8 %shard_map.194 = (bf16[4,384,256]{2,1,0:T(8,128)(2,1)}, bf16[4,384,256]{2,1,0:T(8,128)(2,1)}, bf16[4,384,256]{2,1,0:T(8,128)(2,1)}, bf16[4,384,256]{2,1,0:T(8,128)(2,1)}) custom-call(s32[6]{0:T(128)} %stack.72.ids, bf16[784,1536]{1,0:T(8,128)(2,1)} %get-tuple-element.217.d_mine.refs_0_, bf16[784,1536]{1,0:T(8,128)(2,1)} %get-tuple-element.225.refs_1_.d_mine, ...), custom_call_target="tpu_custom_call" | custom-call | flops 24999999488 | tf_op jit(solution)/shard_map/pallas_call | solution.py:533
  726.7 14.5 %shard_map.196 = (bf16[784,1024]{1,0:T(8,128)(2,1)}, f32[8,1024]{1,0:T(8,128)}, f32[8,1536]{1,0:T(8,128)}, f32[8,1536]{1,0:T(8,128)}) custom-call(s32[6]{0:T(128)} %stack.74.ids, bf16[784,1536]{1,0:T(8,128)(2,1)} %get-tuple-element.236.refs_2_.d_mine, bf16[784,1536]{1,0:T(8,128)(2,1)} %collective-permute-done.35.refs_5_.d_other, ...), custom_call_target="tpu_custom_call" | custom-call | flops 49999998976 | tf_op jit(solution)/shard_map/pallas_call | solution.py:533
  746.3 15.4 %collective-permute-done.47 = f32[12,1024]{1,0:T(8,128)S(1)} collective-permute-done((f32[12,1024]{1,0:T(8,128)S(1)}, f32[12,1024]{1,0:T(8,128)S(1)}, u32[]{:S(2)}, u32[]{:S(2)}) %collective-permute-start.47) | collective-permute-done | bytes 49184 | tf_op jit(solution)/shard_map/ppermute | solution.py:1039
  (299 shorter events, 198.5 us)
Async XLA Ops:
  5.9 44.2 %collective-permute-start.1 = (bf16[1,784,1024]{2,1,0:T(8,128)(2,1)}, bf16[1,784,1024]{2,1,0:T(8,128)(2,1)}, u32[]{:S(2)}, u32[]{:S(2)}) collective-permute-start(bf16[1,784,1024]{2,1,0:T(8,128)(2,1)} %slice.181), channel_id=1, source_target_pairs={{1,2},{2,1},{5,6},{6,5},{9,10},{10,9},{13,14},{14,13},{17,18},{18,... | collective-permute-start | bytes 4816904 | tf_op jit(solution)/shard_map/ppermute | solution.py:1050
  41.0 63.7 %collective-permute-start.13 = (bf16[2,784,1024]{2,1,0:T(8,128)(2,1)}, bf16[2,784,1024]{2,1,0:T(8,128)(2,1)}, u32[]{:S(2)}, u32[]{:S(2)}) collective-permute-start(bf16[2,784,1024]{2,1,0:T(8,128)(2,1)} %slice.182), channel_id=1, source_target_pairs={{1,2},{2,1},{5,6},{6,5},{9,10},{10,9},{13,14},{14,13},{17,18},{18,... | collective-permute-start | bytes 9633800 | tf_op jit(solution)/shard_map/ppermute | solution.py:1050
  61.0 43.7 %collective-permute-start.10 = (bf16[512,1024]{1,0:T(8,128)(2,1)}, bf16[512,1024]{1,0:T(8,128)(2,1)}, u32[]{:S(2)}, u32[]{:S(2)}) collective-permute-start(bf16[512,1024]{1,0:T(8,128)(2,1)} %constant_dynamic-slice_fusion.2), channel_id=1, source_target_pairs={{0,1},{1,0},{2,3},{3,2},{4,5},{5,4},{6,7},{7,6},{8,9},{9,8},{10,11... | collective-permute-start | bytes 3145736 | tf_op jit(solution)/shard_map/ppermute | solution.py:1039
  165.5 42.4 %collective-permute-start.15 = (bf16[640,1024]{1,0:T(8,128)(2,1)}, bf16[640,1024]{1,0:T(8,128)(2,1)}, u32[]{:S(2)}, u32[]{:S(2)}) collective-permute-start(bf16[640,1024]{1,0:T(8,128)(2,1)} %collective-permute-done.12.o0.u0), channel_id=1, source_target_pairs={{0,4},{4,0},{1,5},{5,1},{2,6},{6,2},{3,7},{7,3},{8,12},{12,8},{9,1... | collective-permute-start | bytes 3932168 | tf_op jit(solution)/shard_map/ppermute | solution.py:1039
  169.4 47.5 %collective-permute-start.17 = (bf16[640,1024]{1,0:T(8,128)(2,1)}, bf16[640,1024]{1,0:T(8,128)(2,1)}, u32[]{:S(2)}, u32[]{:S(2)}) collective-permute-start(bf16[640,1024]{1,0:T(8,128)(2,1)} %collective-permute-done.12.o0.u0), channel_id=1, source_target_pairs={{0,2},{2,0},{1,3},{3,1},{4,6},{6,4},{5,7},{7,5},{8,10},{10,8},{9,1... | collective-permute-start | bytes 3932168 | tf_op jit(solution)/shard_map/ppermute | solution.py:1039
  213.5 58.5 %collective-permute-start.22 = (bf16[784,512]{1,0:T(8,128)(2,1)}, bf16[784,512]{1,0:T(8,128)(2,1)}, u32[]{:S(2)}, u32[]{:S(2)}) collective-permute-start(bf16[784,512]{1,0:T(8,128)(2,1)} %get-tuple-element.174.o_r), channel_id=1, source_target_pairs={{0,2},{2,0},{1,3},{3,1},{4,6},{6,4},{5,7},{7,5},{8,10},{10,8},{9,1... | collective-permute-start | bytes 2408456 | tf_op jit(solution)/shard_map/ppermute | solution.py:1039
  214.0 58.0 %collective-permute-start.23 = (bf16[2,784,1024]{2,1,0:T(8,128)(2,1)}, bf16[2,784,1024]{2,1,0:T(8,128)(2,1)}, u32[]{:S(2)}, u32[]{:S(2)}) collective-permute-start(bf16[2,784,1024]{2,1,0:T(8,128)(2,1)} %slice.184), channel_id=1, source_target_pairs={{1,2},{2,1},{5,6},{6,5},{9,10},{10,9},{13,14},{14,13},{17,18},{18,... | collective-permute-start | bytes 9633800 | tf_op jit(solution)/shard_map/ppermute | solution.py:1050
  216.8 110.6 %collective-permute-start.24 = (bf16[784,512]{1,0:T(8,128)(2,1)}, bf16[784,512]{1,0:T(8,128)(2,1)}, u32[]{:S(2)}, u32[]{:S(2)}) collective-permute-start(bf16[784,512]{1,0:T(8,128)(2,1)} %get-tuple-element.179.o_r), channel_id=1, source_target_pairs={{0,2},{2,0},{1,3},{3,1},{4,6},{6,4},{5,7},{7,5},{8,10},{10,8},{9,1... | collective-permute-start | bytes 2408456 | tf_op jit(solution)/shard_map/ppermute | solution.py:1039
  269.3 55.4 %collective-permute-start.21 = (bf16[784,1024]{1,0:T(8,128)(2,1)}, bf16[784,1024]{1,0:T(8,128)(2,1)S(1)}, u32[]{:S(2)}, u32[]{:S(2)}) collective-permute-start(bf16[784,1024]{1,0:T(8,128)(2,1)} %get-tuple-element.170), channel_id=1, source_target_pairs={{1,2},{2,1},{5,6},{6,5},{9,10},{10,9},{13,14},{14,13},{17,18},{18,... | collective-permute-start | bytes 4816904 | tf_op jit(solution)/shard_map/ppermute | solution.py:1050
  324.6 55.5 %collective-permute-start.27 = (bf16[784,1024]{1,0:T(8,128)(2,1)}, bf16[784,1024]{1,0:T(8,128)(2,1)}, u32[]{:S(2)}, u32[]{:S(2)}) collective-permute-start(bf16[784,1024]{1,0:T(8,128)(2,1)} %get-tuple-element.195), channel_id=1, source_target_pairs={{1,2},{2,1},{5,6},{6,5},{9,10},{10,9},{13,14},{14,13},{17,18},{18,... | collective-permute-start | bytes 4816904 | tf_op jit(solution)/shard_map/ppermute | solution.py:1050
  424.9 48.2 %collective-permute-start.25 = (bf16[4,4,128,256]{3,2,1,0:T(8,128)(2,1)}, bf16[4,4,128,256]{3,2,1,0:T(8,128)(2,1)}, u32[]{:S(2)}, u32[]{:S(2)}) collective-permute-start(bf16[4,4,128,256]{3,2,1,0:T(8,128)(2,1)} %shard_map.181), channel_id=1, source_target_pairs={{0,2},{2,0},{1,3},{3,1},{4,6},{6,4},{5,7},{7,5},{8,10},{10,8},{9,1... | collective-permute-start | bytes 3145736 | tf_op jit(solution)/shard_map/ppermute | solution.py:1039
  424.9 59.3 %collective-permute-start.29 = (bf16[3,784,512]{2,1,0:T(8,128)(2,1)S(1)}, bf16[3,784,512]{2,1,0:T(8,128)(2,1)}, u32[]{:S(2)}, u32[]{:S(2)}) collective-permute-start(bf16[3,784,512]{2,1,0:T(8,128)(2,1)S(1)} %copy-done.39), channel_id=1, source_target_pairs={{0,2},{2,0},{1,3},{3,1},{4,6},{6,4},{5,7},{7,5},{8,10},{10,8},{9,1... | collective-permute-start | bytes 7225352 | tf_op jit(solution)/shard_map/ppermute | solution.py:1039
  425.4 228.7 %collective-permute-start.39 = (bf16[784,1024]{1,0:T(8,128)(2,1)}, bf16[784,1024]{1,0:T(8,128)(2,1)}, u32[]{:S(2)}, u32[]{:S(2)}) collective-permute-start(bf16[784,1024]{1,0:T(8,128)(2,1)} %get-tuple-element.240), channel_id=1, source_target_pairs={{1,2},{2,1},{5,6},{6,5},{9,10},{10,9},{13,14},{14,13},{17,18},{18,... | collective-permute-start | bytes 4816904 | tf_op jit(solution)/shard_map/ppermute | solution.py:1050
  481.6 55.4 %collective-permute-start.30 = (bf16[4608,256]{1,0:T(8,128)(2,1)}, bf16[4608,256]{1,0:T(8,128)(2,1)}, u32[]{:S(2)}, u32[]{:S(2)}) collective-permute-start(bf16[4608,256]{1,0:T(8,128)(2,1)} %bitcast.196), channel_id=1, source_target_pairs={{0,5},{1,4},{4,1},{5,0},{2,7},{3,6},{6,3},{7,2},{8,13},{9,12},{12,... | collective-permute-start | bytes 7077896 | tf_op jit(solution)/shard_map/ppermute | solution.py:1043
  481.6 108.1 %collective-permute-start.31 = (bf16[4608,256]{1,0:T(8,128)(2,1)}, bf16[4608,256]{1,0:T(8,128)(2,1)}, u32[]{:S(2)}, u32[]{:S(2)}) collective-permute-start(bf16[4608,256]{1,0:T(8,128)(2,1)} %bitcast.194), channel_id=1, source_target_pairs={{0,4},{4,0},{1,5},{5,1},{2,6},{6,2},{3,7},{7,3},{8,12},{12,8},{9,1... | collective-permute-start | bytes 7077896 | tf_op jit(solution)/shard_map/ppermute | solution.py:1039
  482.3 107.3 %collective-permute-start.32 = (bf16[4608,256]{1,0:T(8,128)(2,1)}, bf16[4608,256]{1,0:T(8,128)(2,1)}, u32[]{:S(2)}, u32[]{:S(2)}) collective-permute-start(bf16[4608,256]{1,0:T(8,128)(2,1)} %bitcast.195), channel_id=1, source_target_pairs={{0,1},{1,0},{2,3},{3,2},{4,5},{5,4},{6,7},{7,6},{8,9},{9,8},{10,11... | collective-permute-start | bytes 7077896 | tf_op jit(solution)/shard_map/ppermute | solution.py:1039
  536.9 118.5 %collective-permute-start.33 = (bf16[784,1536]{1,0:T(8,128)(2,1)}, bf16[784,1536]{1,0:T(8,128)(2,1)}, u32[]{:S(2)}, u32[]{:S(2)}) collective-permute-start(bf16[784,1536]{1,0:T(8,128)(2,1)} %get-tuple-element.237), channel_id=1, source_target_pairs={{0,2},{2,0},{1,3},{3,1},{4,6},{6,4},{5,7},{7,5},{8,10},{10,8},{9,1... | collective-permute-start | bytes 7225352 | tf_op jit(solution)/shard_map/ppermute | solution.py:1039
  598.8 56.8 %collective-permute-start.36 = (bf16[1152,256]{1,0:T(8,128)(2,1)S(1)}, bf16[1152,256]{1,0:T(8,128)(2,1)}, u32[]{:S(2)}, u32[]{:S(2)}) collective-permute-start(bf16[1152,256]{1,0:T(8,128)(2,1)S(1)} %get-tuple-element.312), channel_id=1, source_target_pairs={{0,8},{8,0},{16,24},{24,16},{1,9},{9,1},{17,25},{25,17},{2,10},{10... | collective-permute-start | bytes 1769480 | tf_op jit(solution)/shard_map/ppermute | solution.py:1039
  598.9 56.6 %collective-permute-start.37 = (bf16[1152,256]{1,0:T(8,128)(2,1)S(1)}, bf16[1152,256]{1,0:T(8,128)(2,1)}, u32[]{:S(2)}, u32[]{:S(2)}) collective-permute-start(bf16[1152,256]{1,0:T(8,128)(2,1)S(1)} %get-tuple-element.311), channel_id=1, source_target_pairs={{0,16},{8,24},{16,0},{24,8},{1,17},{9,25},{17,1},{25,9},{2,18},{10... | collective-permute-start | bytes 1769480 | tf_op jit(solution)/shard_map/ppermute | solution.py:1039
  601.3 54.3 %collective-permute-start.38 = (bf16[1152,256]{1,0:T(8,128)(2,1)S(1)}, bf16[1152,256]{1,0:T(8,128)(2,1)}, u32[]{:S(2)}, u32[]{:S(2)}) collective-permute-start(bf16[1152,256]{1,0:T(8,128)(2,1)S(1)} %get-tuple-element.310), channel_id=1, source_target_pairs={{0,24},{8,16},{16,8},{24,0},{1,25},{9,17},{17,9},{25,1},{2,26},{10... | collective-permute-start | bytes 1769480 | tf_op jit(solution)/shard_map/ppermute | solution.py:1039
  722.5 47.0 %collective-permute-start.42 = (bf16[1536,256]{1,0:T(8,128)(2,1)}, bf16[1536,256]{1,0:T(8,128)(2,1)S(1)}, u32[]{:S(2)}, u32[]{:S(2)}) collective-permute-start(bf16[1536,256]{1,0:T(8,128)(2,1)} %bitcast.199), channel_id=1, source_target_pairs={{0,4},{4,0},{1,5},{5,1},{2,6},{6,2},{3,7},{7,3},{8,12},{12,8},{9,1... | collective-permute-start | bytes 2359304 | tf_op jit(solution)/shard_map/ppermute | solution.py:1039
  722.8 46.8 %collective-permute-start.43 = (bf16[1536,256]{1,0:T(8,128)(2,1)}, bf16[1536,256]{1,0:T(8,128)(2,1)S(1)}, u32[]{:S(2)}, u32[]{:S(2)}) collective-permute-start(bf16[1536,256]{1,0:T(8,128)(2,1)} %bitcast.198), channel_id=1, source_target_pairs={{0,1},{1,0},{2,3},{3,2},{4,5},{5,4},{6,7},{7,6},{8,9},{9,8},{10,11... | collective-permute-start | bytes 2359304 | tf_op jit(solution)/shard_map/ppermute | solution.py:1039
  722.8 46.8 %collective-permute-start.44 = (bf16[1536,256]{1,0:T(8,128)(2,1)}, bf16[1536,256]{1,0:T(8,128)(2,1)S(1)}, u32[]{:S(2)}, u32[]{:S(2)}) collective-permute-start(bf16[1536,256]{1,0:T(8,128)(2,1)} %bitcast.197), channel_id=1, source_target_pairs={{0,5},{1,4},{4,1},{5,0},{2,7},{3,6},{6,3},{7,2},{8,13},{9,12},{12,... | collective-permute-start | bytes 2359304 | tf_op jit(solution)/shard_map/ppermute | solution.py:1043
  765.9 49.9 %collective-permute-start.50 = (bf16[784,1024]{1,0:T(8,128)(2,1)}, bf16[784,1024]{1,0:T(8,128)(2,1)}, u32[]{:S(2)}, u32[]{:S(2)}) collective-permute-start(bf16[784,1024]{1,0:T(8,128)(2,1)} %get-tuple-element.275), channel_id=1, source_target_pairs={{1,2},{2,1},{5,6},{6,5},{9,10},{10,9},{13,14},{14,13},{17,18},{18,... | collective-permute-start | bytes 4816904 | tf_op jit(solution)/shard_map/ppermute | solution.py:1050
  (76 other events, 986.8 us)

commit v5 on v4

--- a/solution.py
+++ b/solution.py
@@ -1274,6 +1274,7 @@
 
     outs = jnp.stack([jnp.where(swap == 1, after(got_result[s], sends), result[s]) for s in range(slots)])
     input_grad = jnp.stack([jnp.where(swap == 1, after(got_rows[s], sends), row_grads[s]) for s in range(slots)]).astype(F32)
+    qkv_terms = after(qkv_terms, input_grad)
     lines = sum(from_lines(term[qkv_rows:], shape) for term in qkv_terms)
     columns = own_half(lines[:8], x, 1)
     hidden_part = own_half(lines[8:], x).reshape(-1)

time: 827 us -> 816 us (0.987)
  transfers between devices with their start and end apart: 56 -> 56, of which waited for: 11 -> 10; matrix products, arithmetic and copies ran while one was open for 7% -> 7% of each run, Pallas kernels for 73% -> 74%
where the time goes in v5:
time: 816 us; the launch traced here: 812 us
  Pallas kernels  636 us (78%)
  starting transfers between devices  59.4 us (7%)
  waiting for transfers between devices  47.6 us (6%)
  local copies, waits for them, and re-layouts  40.1 us (5%)
  other arithmetic  25.8 us (3%)
    pallas_call x22, Pallas kernels, call(): pl.pallas_call(kernel, grid_spec=pltpu.PrefetchScalarGridSpec(num_scalar_...  388 us
    pallas_call x3, Pallas kernels, attend_back(): pl.pallas_call(functools.partial(attend_back_kernel, nb=nb, np_=np_, rem=...  158 us
    pallas_call x3, Pallas kernels, attend(): pl.pallas_call(functools.partial(attend_kernel, nb=nb, np_=np_, rem=rem),...  89.2 us
    ppermute x43, waiting for transfers between devices, swap_axis(): return lax.ppermute(x, axis, [(i, i ^ step) for i in range(size)])  41.7 us
    ppermute x10, starting transfers between devices, swap_owner(): return lax.ppermute(x, AXES, pairs)  32.7 us
    ppermute x43, starting transfers between devices, swap_axis(): return lax.ppermute(x, axis, [(i, i ^ step) for i in range(size)])  24.2 us
  transfers between devices with their start and end apart: 56, of which 10 were waited for; matrix products, arithmetic and copies ran while one was open for 7% of the time, Pallas kernels for 74%

profile of v5, /device:TPU:9, one launch (start us, length us, event | category | flops | bytes accessed | tf_op | source)
XLA Modules:
  0.0 811.7 jit_solution(13844292383240329712)
XLA Ops:
  10.0 10.3 %collective-permute-done.2.p0.m0.o0 = bf16[128,3072]{1,0:T(8,128)(2,1)S(1)} collective-permute-done((bf16[128,3072]{1,0:T(8,128)(2,1)S(1)}, bf16[128,3072]{1,0:T(8,128)(2,1)S(1)}, u32[]{:S(2)}, u32[]{:S(2)}) %collective-permute-start.2) | collective-permute-done | bytes 786464 | tf_op jit(solution)/shard_map/ppermute | solution.py:1039
  52.0 8.9 %shard_map.169 = (bf16[784,1024]{1,0:T(8,128)(2,1)}, bf16[784,1024]{1,0:T(8,128)(2,1)}, bf16[784,1536]{1,0:T(8,128)(2,1)}) custom-call(s32[6]{0:T(128)} %stack.72.ids, bf16[3,784,1024]{2,1,0:T(8,128)(2,1)} %mine.5, bf16[1,784,1024]{2,1,0:T(8,128)(2,1)} %collective-permute-done.1.got, f32[1,1024]{1,0:T(1,128)} %bitcast.159, f32[1,1024]{1,0:T(1,128)} %bitcast.162, ...), custom_call_target="tpu_custom_call" | custom-call | tf_op jit(solution)/shard_map/pallas_call | solution.py:533
  70.4 29.6 %shard_map.171 = (bf16[784,512]{1,0:T(8,128)(2,1)}, bf16[784,512]{1,0:T(8,128)(2,1)}, f32[784,512]{1,0:T(8,128)}, f32[784,512]{1,0:T(8,128)}, bf16[12,2,1568,512...) custom-call(bf16[784,1536]{1,0:T(8,128)(2,1)} %shard_map.170.own, bf16[784,1536]{1,0:T(8,128)(2,1)} %copy-done.5), custom_call_target="tpu_custom_call" | custom-call | tf_op jit(solution)/shard_map/pallas_call | solution.py:151
  104.8 9.1 %shard_map.172 = (bf16[784,1024]{1,0:T(8,128)(2,1)}, bf16[784,1024]{1,0:T(8,128)(2,1)}, bf16[784,1536]{1,0:T(8,128)(2,1)}) custom-call(s32[6]{0:T(128)} %stack.73.ids, bf16[3,784,1024]{2,1,0:T(8,128)(2,1)} %mine.5, bf16[2,784,1024]{2,1,0:T(8,128)(2,1)} %collective-permute-done.13.got, f32[1,1024]{1,0:T(1,128)} %bitcast.160, f32[1,1024]{1,0:T(1,128)} %bitcast.163, ...), custom_call_target="tpu_custom_call" | custom-call | tf_op jit(solution)/shard_map/pallas_call | solution.py:533
  125.4 29.8 %shard_map.174 = (bf16[784,512]{1,0:T(8,128)(2,1)}, bf16[784,512]{1,0:T(8,128)(2,1)}, f32[784,512]{1,0:T(8,128)}, f32[784,512]{1,0:T(8,128)}, bf16[12,2,1568,512...) custom-call(bf16[784,1536]{1,0:T(8,128)(2,1)} %shard_map.173.own, bf16[784,1536]{1,0:T(8,128)(2,1)} %copy-done.6), custom_call_target="tpu_custom_call" | custom-call | tf_op jit(solution)/shard_map/pallas_call | solution.py:151
  155.2 9.5 %shard_map.175 = (bf16[784,1024]{1,0:T(8,128)(2,1)}, bf16[784,1024]{1,0:T(8,128)(2,1)}, bf16[784,1536]{1,0:T(8,128)(2,1)}) custom-call(s32[6]{0:T(128)} %stack.74.ids, bf16[3,784,1024]{2,1,0:T(8,128)(2,1)} %mine.5, bf16[2,784,1024]{2,1,0:T(8,128)(2,1)} %collective-permute-done.13.got, f32[1,1024]{1,0:T(1,128)} %bitcast.161, f32[1,1024]{1,0:T(1,128)} %bitcast.164, ...), custom_call_target="tpu_custom_call" | custom-call | tf_op jit(solution)/shard_map/pallas_call | solution.py:533
  178.2 29.8 %shard_map.177 = (bf16[784,512]{1,0:T(8,128)(2,1)}, bf16[784,512]{1,0:T(8,128)(2,1)}, f32[784,512]{1,0:T(8,128)}, f32[784,512]{1,0:T(8,128)}, bf16[12,2,1568,512...) custom-call(bf16[784,1536]{1,0:T(8,128)(2,1)} %shard_map.176.own, bf16[784,1536]{1,0:T(8,128)(2,1)} %copy-done.7), custom_call_target="tpu_custom_call" | custom-call | tf_op jit(solution)/shard_map/pallas_call | solution.py:151
  217.2 52.3 %shard_map.178 = (bf16[784,4096]{1,0:T(8,128)(2,1)}, bf16[784,4096]{1,0:T(8,128)(2,1)}, bf16[784,1024]{1,0:T(8,128)(2,1)}, bf16[784,1024]{1,0:T(8,128)(2,1)}, bf...) custom-call(s32[6]{0:T(128)} %stack.72.ids, ...), custom_call_target="tpu_custom_call" | custom-call | flops 49999998976 | tf_op jit(solution)/shard_map/pallas_call | solution.py:533
  272.2 52.5 %shard_map.179 = (bf16[784,4096]{1,0:T(8,128)(2,1)}, bf16[784,4096]{1,0:T(8,128)(2,1)}, bf16[784,1024]{1,0:T(8,128)(2,1)}, bf16[784,1024]{1,0:T(8,128)(2,1)}, bf...) custom-call(s32[6]{0:T(128)} %stack.73.ids, ...), custom_call_target="tpu_custom_call", output_to_operand_aliasing={{7}: (24, {})} | custom-call | flops 49999998976 | tf_op jit(solution)/shard_map/pallas_call | solution.py:533
  327.7 52.6 %shard_map.180 = (bf16[784,4096]{1,0:T(8,128)(2,1)}, bf16[784,4096]{1,0:T(8,128)(2,1)}, bf16[784,1024]{1,0:T(8,128)(2,1)}, bf16[784,1024]{1,0:T(8,128)(2,1)}, bf...) custom-call(s32[6]{0:T(128)} %stack.74.ids, ...), custom_call_target="tpu_custom_call", output_to_operand_aliasing={{7}: (24, {})} | custom-call | flops 49999998976 | tf_op jit(solution)/shard_map/pallas_call | solution.py:533
  380.3 18.3 %shard_map.183 = bf16[4,4,512,256]{3,2,1,0:T(8,128)(2,1)} custom-call(s32[6]{0:T(128)} %stack.72.ids, bf16[784,1024]{1,0:T(8,128)(2,1)} %get-tuple-element.200.refs_0_, bf16[784,1024]{1,0:T(8,128)(2,1)} %get-tuple-element.201.refs_1_, bf16[784,1024]{1,0:T(8,128)(2,1)} %get-tuple-element.202.refs_2_, bf16[784,4096]{1,0:T(8,128)(2,1)} %get-tuple-element.196.refs_3_, ...), custom_call_target="tpu_custom_call" | custom-call | flops 24999999488 | tf_op jit(solution)/shard_map/pallas_call | solution.py:533
  398.6 18.2 %shard_map.182 = bf16[4,4,512,256]{3,2,1,0:T(8,128)(2,1)} custom-call(s32[6]{0:T(128)} %stack.72.ids, bf16[784,4096]{1,0:T(8,128)(2,1)} %get-tuple-element.187.refs_0_, bf16[784,4096]{1,0:T(8,128)(2,1)} %get-tuple-element.188.refs_1_, bf16[784,4096]{1,0:T(8,128)(2,1)} %get-tuple-element.189.refs_2_, bf16[784,1024]{1,0:T(8,128)(2,1)} %get-tuple-element.190.refs_3_.refs_6_, ...), custom_call_target="tpu_custom_call" | custom-call | flops 24999999488 | tf_op jit(solution)/shard_map/pallas_call | solution.py:533
  430.6 22.0 %shard_map.184 = (bf16[4,1152,256]{2,1,0:T(8,128)(2,1)}, bf16[4,1152,256]{2,1,0:T(8,128)(2,1)}, bf16[4,1152,256]{2,1,0:T(8,128)(2,1)}, bf16[4,1152,256]{2,1,0:T(8,128)(2,1)}) custom-call(s32[6]{0:T(128)} %stack.72.ids, bf16[784,1024]{1,0:T(8,128)(2,1)} %get-tuple-element.200.refs_0_, bf16[784,1024]{1,0:T(8,128)(2,1)} %get-tuple-element.201.refs_1_, ...), custom_call_target="tpu_custom_call" | custom-call | flops 24999999488 | tf_op jit(solution)/shard_map/pallas_call | solution.py:533
  452.6 20.5 %shard_map.185 = (bf16[4,1152,256]{2,1,0:T(8,128)(2,1)}, bf16[4,1152,256]{2,1,0:T(8,128)(2,1)}, bf16[4,1152,256]{2,1,0:T(8,128)(2,1)}, bf16[4,1152,256]{2,1,0:T(8,128)(2,1)}) custom-call(s32[6]{0:T(128)} %stack.72.ids, bf16[784,4096]{1,0:T(8,128)(2,1)} %get-tuple-element.187.refs_0_, ...), custom_call_target="tpu_custom_call", output_to_operand_aliasing={{0}: (11, {}), {1}: (12, {}), {2}: (13, {}), {3}: (14, {})} | custom-call | flops 24999999488 | tf_op jit(solution)/shard_map/pallas_call | solution.py:533
  473.1 8.5 %shard_map.186 = (bf16[4,1152,256]{2,1,0:T(8,128)(2,1)}, bf16[4,1152,256]{2,1,0:T(8,128)(2,1)}, bf16[4,1152,256]{2,1,0:T(8,128)(2,1)}, bf16[4,1152,256]{2,1,0:T(8,128)(2,1)}) custom-call(s32[6]{0:T(128)} %stack.72.ids, ...), custom_call_target="tpu_custom_call", output_to_operand_aliasing={{0}: (11, {}), {1}: (12, {}), {2}: (13, {}), {3}: (14, {})} | custom-call | flops 24999999488 | tf_op jit(solution)/shard_map/pallas_call | solution.py:533
  484.2 52.6 %shard_map.187 = (bf16[784,1536]{1,0:T(8,128)(2,1)}, bf16[784,1536]{1,0:T(8,128)(2,1)}) custom-call(bf16[784,1536]{1,0:T(8,128)(2,1)} %shard_map.170.own, bf16[784,1536]{1,0:T(8,128)(2,1)} %copy-done.5, bf16[784,512]{1,0:T(8,128)(2,1)} %get-tuple-element.215.do_o, bf16[3,784,512]{2,1,0:T(8,128)(2,1)} %collective-permute-done.29.do_r, ...), custom_call_target="tpu_custom_call" | custom-call | flops 49999998976 | tf_op jit(solution)/shard_map/pallas_call | solution.py:255
  537.0 52.8 %shard_map.188 = (bf16[784,1536]{1,0:T(8,128)(2,1)}, bf16[784,1536]{1,0:T(8,128)(2,1)}) custom-call(bf16[784,1536]{1,0:T(8,128)(2,1)} %shard_map.173.own, bf16[784,1536]{1,0:T(8,128)(2,1)} %copy-done.6, bf16[784,512]{1,0:T(8,128)(2,1)} %get-tuple-element.224.do_o, bf16[3,784,512]{2,1,0:T(8,128)(2,1)} %collective-permute-done.29.do_r, ...), custom_call_target="tpu_custom_call" | custom-call | flops 49999998976 | tf_op jit(solution)/shard_map/pallas_call | solution.py:255
  601.6 52.8 %shard_map.190 = (bf16[784,1536]{1,0:T(8,128)(2,1)}, bf16[784,1536]{1,0:T(8,128)(2,1)}) custom-call(bf16[784,1536]{1,0:T(8,128)(2,1)} %shard_map.176.own, bf16[784,1536]{1,0:T(8,128)(2,1)} %copy-done.7, bf16[784,512]{1,0:T(8,128)(2,1)} %get-tuple-element.235.do_o, bf16[3,784,512]{2,1,0:T(8,128)(2,1)} %collective-permute-done.29.do_r, ...), custom_call_target="tpu_custom_call" | custom-call | flops 49999998976 | tf_op jit(solution)/shard_map/pallas_call | solution.py:255
  655.6 14.8 %shard_map.191 = (bf16[784,1024]{1,0:T(8,128)(2,1)}, f32[8,1024]{1,0:T(8,128)}, f32[8,1536]{1,0:T(8,128)}, f32[8,1536]{1,0:T(8,128)}) custom-call(s32[6]{0:T(128)} %stack.72.ids, bf16[784,1536]{1,0:T(8,128)(2,1)} %get-tuple-element.221.d_mine.refs_0_, bf16[784,1536]{1,0:T(8,128)(2,1)} %collective-permute-done.33.d_other.refs_3_, ...), custom_call_target="tpu_custom_call" | custom-call | flops 49999998976 | tf_op jit(solution)/shard_map/pallas_call | solution.py:533
  674.1 15.1 %shard_map.192 = bf16[4,4,384,256]{3,2,1,0:T(8,128)(2,1)} custom-call(s32[6]{0:T(128)} %stack.72.ids, bf16[784,1536]{1,0:T(8,128)(2,1)} %get-tuple-element.221.d_mine.refs_0_, bf16[784,1536]{1,0:T(8,128)(2,1)} %get-tuple-element.229.refs_1_.d_mine, bf16[784,1536]{1,0:T(8,128)(2,1)} %get-tuple-element.240.refs_2_.d_mine, ...), custom_call_target="tpu_custom_call" | custom-call | flops 24999999488 | tf_op jit(solution)/shard_map/pallas_call | solution.py:533
  689.3 14.3 %shard_map.193 = (bf16[784,1024]{1,0:T(8,128)(2,1)}, f32[8,1024]{1,0:T(8,128)}, f32[8,1536]{1,0:T(8,128)}, f32[8,1536]{1,0:T(8,128)}) custom-call(s32[6]{0:T(128)} %stack.73.ids, bf16[784,1536]{1,0:T(8,128)(2,1)} %get-tuple-element.229.refs_1_.d_mine, bf16[784,1536]{1,0:T(8,128)(2,1)} %collective-permute-done.34.refs_4_.d_other, ...), custom_call_target="tpu_custom_call" | custom-call | flops 49999998976 | tf_op jit(solution)/shard_map/pallas_call | solution.py:533
  705.7 16.8 %shard_map.194 = (bf16[4,384,256]{2,1,0:T(8,128)(2,1)}, bf16[4,384,256]{2,1,0:T(8,128)(2,1)}, bf16[4,384,256]{2,1,0:T(8,128)(2,1)}, bf16[4,384,256]{2,1,0:T(8,128)(2,1)}) custom-call(s32[6]{0:T(128)} %stack.72.ids, bf16[784,1536]{1,0:T(8,128)(2,1)} %get-tuple-element.221.d_mine.refs_0_, bf16[784,1536]{1,0:T(8,128)(2,1)} %get-tuple-element.229.refs_1_.d_mine, ...), custom_call_target="tpu_custom_call" | custom-call | flops 24999999488 | tf_op jit(solution)/shard_map/pallas_call | solution.py:533
  727.1 14.5 %shard_map.196 = (bf16[784,1024]{1,0:T(8,128)(2,1)}, f32[8,1024]{1,0:T(8,128)}, f32[8,1536]{1,0:T(8,128)}, f32[8,1536]{1,0:T(8,128)}) custom-call(s32[6]{0:T(128)} %stack.74.ids, bf16[784,1536]{1,0:T(8,128)(2,1)} %get-tuple-element.240.refs_2_.d_mine, bf16[784,1536]{1,0:T(8,128)(2,1)} %collective-permute-done.35.refs_5_.d_other, ...), custom_call_target="tpu_custom_call" | custom-call | flops 49999998976 | tf_op jit(solution)/shard_map/pallas_call | solution.py:533
  746.4 15.3 %collective-permute-done.47 = f32[12,1024]{1,0:T(8,128)S(1)} collective-permute-done((f32[12,1024]{1,0:T(8,128)S(1)}, f32[12,1024]{1,0:T(8,128)S(1)}, u32[]{:S(2)}, u32[]{:S(2)}) %collective-permute-start.47) | collective-permute-done | bytes 49184 | tf_op jit(solution)/shard_map/ppermute | solution.py:1039
  (283 shorter events, 187.6 us)
Async XLA Ops:
  5.9 44.3 %collective-permute-start.1 = (bf16[1,784,1024]{2,1,0:T(8,128)(2,1)}, bf16[1,784,1024]{2,1,0:T(8,128)(2,1)}, u32[]{:S(2)}, u32[]{:S(2)}) collective-permute-start(bf16[1,784,1024]{2,1,0:T(8,128)(2,1)} %slice.187), channel_id=1, source_target_pairs={{1,2},{2,1},{5,6},{6,5},{9,10},{10,9},{13,14},{14,13},{17,18},{18,... | collective-permute-start | bytes 4816904 | tf_op jit(solution)/shard_map/ppermute | solution.py:1050
  41.1 63.7 %collective-permute-start.13 = (bf16[2,784,1024]{2,1,0:T(8,128)(2,1)}, bf16[2,784,1024]{2,1,0:T(8,128)(2,1)}, u32[]{:S(2)}, u32[]{:S(2)}) collective-permute-start(bf16[2,784,1024]{2,1,0:T(8,128)(2,1)} %slice.188), channel_id=1, source_target_pairs={{1,2},{2,1},{5,6},{6,5},{9,10},{10,9},{13,14},{14,13},{17,18},{18,... | collective-permute-start | bytes 9633800 | tf_op jit(solution)/shard_map/ppermute | solution.py:1050
  61.1 43.7 %collective-permute-start.10 = (bf16[512,1024]{1,0:T(8,128)(2,1)}, bf16[512,1024]{1,0:T(8,128)(2,1)}, u32[]{:S(2)}, u32[]{:S(2)}) collective-permute-start(bf16[512,1024]{1,0:T(8,128)(2,1)} %constant_dynamic-slice_fusion.2), channel_id=1, source_target_pairs={{0,1},{1,0},{2,3},{3,2},{4,5},{5,4},{6,7},{7,6},{8,9},{9,8},{10,11... | collective-permute-start | bytes 3145736 | tf_op jit(solution)/shard_map/ppermute | solution.py:1039
  165.6 42.4 %collective-permute-start.15 = (bf16[640,1024]{1,0:T(8,128)(2,1)}, bf16[640,1024]{1,0:T(8,128)(2,1)}, u32[]{:S(2)}, u32[]{:S(2)}) collective-permute-start(bf16[640,1024]{1,0:T(8,128)(2,1)} %collective-permute-done.12.o0.u0), channel_id=1, source_target_pairs={{0,4},{4,0},{1,5},{5,1},{2,6},{6,2},{3,7},{7,3},{8,12},{12,8},{9,1... | collective-permute-start | bytes 3932168 | tf_op jit(solution)/shard_map/ppermute | solution.py:1039
  166.9 42.2 %collective-permute-start.9 = (bf16[1,784,1024]{2,1,0:T(8,128)(2,1)S(1)}, bf16[1,784,1024]{2,1,0:T(8,128)(2,1)}, u32[]{:S(2)}, u32[]{:S(2)}) collective-permute-start(bf16[1,784,1024]{2,1,0:T(8,128)(2,1)S(1)} %copy-done.15), channel_id=1, source_target_pairs={{1,2},{2,1},{5,6},{6,5},{9,10},{10,9},{13,14},{14,13},{17,18},{18,... | collective-permute-start | bytes 4816904 | tf_op jit(solution)/shard_map/ppermute | solution.py:1050
  169.6 47.5 %collective-permute-start.17 = (bf16[640,1024]{1,0:T(8,128)(2,1)}, bf16[640,1024]{1,0:T(8,128)(2,1)}, u32[]{:S(2)}, u32[]{:S(2)}) collective-permute-start(bf16[640,1024]{1,0:T(8,128)(2,1)} %collective-permute-done.12.o0.u0), channel_id=1, source_target_pairs={{0,2},{2,0},{1,3},{3,1},{4,6},{6,4},{5,7},{7,5},{8,10},{10,8},{9,1... | collective-permute-start | bytes 3932168 | tf_op jit(solution)/shard_map/ppermute | solution.py:1039
  213.7 58.5 %collective-permute-start.22 = (bf16[784,512]{1,0:T(8,128)(2,1)}, bf16[784,512]{1,0:T(8,128)(2,1)}, u32[]{:S(2)}, u32[]{:S(2)}) collective-permute-start(bf16[784,512]{1,0:T(8,128)(2,1)} %get-tuple-element.178.o_r), channel_id=1, source_target_pairs={{0,2},{2,0},{1,3},{3,1},{4,6},{6,4},{5,7},{7,5},{8,10},{10,8},{9,1... | collective-permute-start | bytes 2408456 | tf_op jit(solution)/shard_map/ppermute | solution.py:1039
  214.2 58.0 %collective-permute-start.23 = (bf16[2,784,1024]{2,1,0:T(8,128)(2,1)}, bf16[2,784,1024]{2,1,0:T(8,128)(2,1)}, u32[]{:S(2)}, u32[]{:S(2)}) collective-permute-start(bf16[2,784,1024]{2,1,0:T(8,128)(2,1)} %slice.190), channel_id=1, source_target_pairs={{1,2},{2,1},{5,6},{6,5},{9,10},{10,9},{13,14},{14,13},{17,18},{18,... | collective-permute-start | bytes 9633800 | tf_op jit(solution)/shard_map/ppermute | solution.py:1050
  217.0 110.6 %collective-permute-start.24 = (bf16[784,512]{1,0:T(8,128)(2,1)}, bf16[784,512]{1,0:T(8,128)(2,1)}, u32[]{:S(2)}, u32[]{:S(2)}) collective-permute-start(bf16[784,512]{1,0:T(8,128)(2,1)} %get-tuple-element.183.o_r), channel_id=1, source_target_pairs={{0,2},{2,0},{1,3},{3,1},{4,6},{6,4},{5,7},{7,5},{8,10},{10,8},{9,1... | collective-permute-start | bytes 2408456 | tf_op jit(solution)/shard_map/ppermute | solution.py:1039
  269.5 55.3 %collective-permute-start.21 = (bf16[784,1024]{1,0:T(8,128)(2,1)}, bf16[784,1024]{1,0:T(8,128)(2,1)S(1)}, u32[]{:S(2)}, u32[]{:S(2)}) collective-permute-start(bf16[784,1024]{1,0:T(8,128)(2,1)} %get-tuple-element.174), channel_id=1, source_target_pairs={{1,2},{2,1},{5,6},{6,5},{9,10},{10,9},{13,14},{14,13},{17,18},{18,... | collective-permute-start | bytes 4816904 | tf_op jit(solution)/shard_map/ppermute | solution.py:1050
  324.8 55.5 %collective-permute-start.27 = (bf16[784,1024]{1,0:T(8,128)(2,1)}, bf16[784,1024]{1,0:T(8,128)(2,1)}, u32[]{:S(2)}, u32[]{:S(2)}) collective-permute-start(bf16[784,1024]{1,0:T(8,128)(2,1)} %get-tuple-element.199), channel_id=1, source_target_pairs={{1,2},{2,1},{5,6},{6,5},{9,10},{10,9},{13,14},{14,13},{17,18},{18,... | collective-permute-start | bytes 4816904 | tf_op jit(solution)/shard_map/ppermute | solution.py:1050
  425.1 48.0 %collective-permute-start.25 = (bf16[4,4,128,256]{3,2,1,0:T(8,128)(2,1)}, bf16[4,4,128,256]{3,2,1,0:T(8,128)(2,1)}, u32[]{:S(2)}, u32[]{:S(2)}) collective-permute-start(bf16[4,4,128,256]{3,2,1,0:T(8,128)(2,1)} %shard_map.181), channel_id=1, source_target_pairs={{0,2},{2,0},{1,3},{3,1},{4,6},{6,4},{5,7},{7,5},{8,10},{10,8},{9,1... | collective-permute-start | bytes 3145736 | tf_op jit(solution)/shard_map/ppermute | solution.py:1039
  425.1 59.1 %collective-permute-start.29 = (bf16[3,784,512]{2,1,0:T(8,128)(2,1)S(1)}, bf16[3,784,512]{2,1,0:T(8,128)(2,1)}, u32[]{:S(2)}, u32[]{:S(2)}) collective-permute-start(bf16[3,784,512]{2,1,0:T(8,128)(2,1)S(1)} %copy-done.30), channel_id=1, source_target_pairs={{0,2},{2,0},{1,3},{3,1},{4,6},{6,4},{5,7},{7,5},{8,10},{10,8},{9,1... | collective-permute-start | bytes 7225352 | tf_op jit(solution)/shard_map/ppermute | solution.py:1039
  425.6 228.8 %collective-permute-start.39 = (bf16[784,1024]{1,0:T(8,128)(2,1)}, bf16[784,1024]{1,0:T(8,128)(2,1)}, u32[]{:S(2)}, u32[]{:S(2)}) collective-permute-start(bf16[784,1024]{1,0:T(8,128)(2,1)} %get-tuple-element.244), channel_id=1, source_target_pairs={{1,2},{2,1},{5,6},{6,5},{9,10},{10,9},{13,14},{14,13},{17,18},{18,... | collective-permute-start | bytes 4816904 | tf_op jit(solution)/shard_map/ppermute | solution.py:1050
  481.6 55.4 %collective-permute-start.30 = (bf16[4608,256]{1,0:T(8,128)(2,1)}, bf16[4608,256]{1,0:T(8,128)(2,1)}, u32[]{:S(2)}, u32[]{:S(2)}) collective-permute-start(bf16[4608,256]{1,0:T(8,128)(2,1)} %bitcast.194), channel_id=1, source_target_pairs={{0,5},{1,4},{4,1},{5,0},{2,7},{3,6},{6,3},{7,2},{8,13},{9,12},{12,... | collective-permute-start | bytes 7077896 | tf_op jit(solution)/shard_map/ppermute | solution.py:1043
  481.6 108.3 %collective-permute-start.31 = (bf16[4608,256]{1,0:T(8,128)(2,1)}, bf16[4608,256]{1,0:T(8,128)(2,1)}, u32[]{:S(2)}, u32[]{:S(2)}) collective-permute-start(bf16[4608,256]{1,0:T(8,128)(2,1)} %bitcast.192), channel_id=1, source_target_pairs={{0,4},{4,0},{1,5},{5,1},{2,6},{6,2},{3,7},{7,3},{8,12},{12,8},{9,1... | collective-permute-start | bytes 7077896 | tf_op jit(solution)/shard_map/ppermute | solution.py:1039
  482.3 107.5 %collective-permute-start.32 = (bf16[4608,256]{1,0:T(8,128)(2,1)}, bf16[4608,256]{1,0:T(8,128)(2,1)}, u32[]{:S(2)}, u32[]{:S(2)}) collective-permute-start(bf16[4608,256]{1,0:T(8,128)(2,1)} %bitcast.193), channel_id=1, source_target_pairs={{0,1},{1,0},{2,3},{3,2},{4,5},{5,4},{6,7},{7,6},{8,9},{9,8},{10,11... | collective-permute-start | bytes 7077896 | tf_op jit(solution)/shard_map/ppermute | solution.py:1039
  536.9 118.7 %collective-permute-start.33 = (bf16[784,1536]{1,0:T(8,128)(2,1)}, bf16[784,1536]{1,0:T(8,128)(2,1)}, u32[]{:S(2)}, u32[]{:S(2)}) collective-permute-start(bf16[784,1536]{1,0:T(8,128)(2,1)} %get-tuple-element.241), channel_id=1, source_target_pairs={{0,2},{2,0},{1,3},{3,1},{4,6},{6,4},{5,7},{7,5},{8,10},{10,8},{9,1... | collective-permute-start | bytes 7225352 | tf_op jit(solution)/shard_map/ppermute | solution.py:1039
  598.9 56.7 %collective-permute-start.36 = (bf16[1152,256]{1,0:T(8,128)(2,1)S(1)}, bf16[1152,256]{1,0:T(8,128)(2,1)}, u32[]{:S(2)}, u32[]{:S(2)}) collective-permute-start(bf16[1152,256]{1,0:T(8,128)(2,1)S(1)} %get-tuple-element.320), channel_id=1, source_target_pairs={{0,8},{8,0},{16,24},{24,16},{1,9},{9,1},{17,25},{25,17},{2,10},{10... | collective-permute-start | bytes 1769480 | tf_op jit(solution)/shard_map/ppermute | solution.py:1039
  599.1 56.5 %collective-permute-start.37 = (bf16[1152,256]{1,0:T(8,128)(2,1)S(1)}, bf16[1152,256]{1,0:T(8,128)(2,1)}, u32[]{:S(2)}, u32[]{:S(2)}) collective-permute-start(bf16[1152,256]{1,0:T(8,128)(2,1)S(1)} %get-tuple-element.319), channel_id=1, source_target_pairs={{0,16},{8,24},{16,0},{24,8},{1,17},{9,25},{17,1},{25,9},{2,18},{10... | collective-permute-start | bytes 1769480 | tf_op jit(solution)/shard_map/ppermute | solution.py:1039
  601.4 54.2 %collective-permute-start.38 = (bf16[1152,256]{1,0:T(8,128)(2,1)S(1)}, bf16[1152,256]{1,0:T(8,128)(2,1)}, u32[]{:S(2)}, u32[]{:S(2)}) collective-permute-start(bf16[1152,256]{1,0:T(8,128)(2,1)S(1)} %get-tuple-element.318), channel_id=1, source_target_pairs={{0,24},{8,16},{16,8},{24,0},{1,25},{9,17},{17,9},{25,1},{2,26},{10... | collective-permute-start | bytes 1769480 | tf_op jit(solution)/shard_map/ppermute | solution.py:1039
  722.5 46.9 %collective-permute-start.42 = (bf16[1536,256]{1,0:T(8,128)(2,1)}, bf16[1536,256]{1,0:T(8,128)(2,1)}, u32[]{:S(2)}, u32[]{:S(2)}) collective-permute-start(bf16[1536,256]{1,0:T(8,128)(2,1)} %bitcast.197), channel_id=1, source_target_pairs={{0,4},{4,0},{1,5},{5,1},{2,6},{6,2},{3,7},{7,3},{8,12},{12,8},{9,1... | collective-permute-start | bytes 2359304 | tf_op jit(solution)/shard_map/ppermute | solution.py:1039
  722.8 46.7 %collective-permute-start.43 = (bf16[1536,256]{1,0:T(8,128)(2,1)}, bf16[1536,256]{1,0:T(8,128)(2,1)}, u32[]{:S(2)}, u32[]{:S(2)}) collective-permute-start(bf16[1536,256]{1,0:T(8,128)(2,1)} %bitcast.196), channel_id=1, source_target_pairs={{0,1},{1,0},{2,3},{3,2},{4,5},{5,4},{6,7},{7,6},{8,9},{9,8},{10,11... | collective-permute-start | bytes 2359304 | tf_op jit(solution)/shard_map/ppermute | solution.py:1039
  722.8 46.7 %collective-permute-start.44 = (bf16[1536,256]{1,0:T(8,128)(2,1)}, bf16[1536,256]{1,0:T(8,128)(2,1)}, u32[]{:S(2)}, u32[]{:S(2)}) collective-permute-start(bf16[1536,256]{1,0:T(8,128)(2,1)} %bitcast.195), channel_id=1, source_target_pairs={{0,5},{1,4},{4,1},{5,0},{2,7},{3,6},{6,3},{7,2},{8,13},{9,12},{12,... | collective-permute-start | bytes 2359304 | tf_op jit(solution)/shard_map/ppermute | solution.py:1043
  (67 other events, 916.3 us)

commit v6 on v5

--- a/solution.py
+++ b/solution.py
@@ -20,7 +20,7 @@
 BQ = 512
 TK = 224
 COST = 5 * 10**10
-LIMIT = 70.0
+LIMIT = 56.0
 
 
 def dot(a, b, dims):

time: 816 us -> 849 us (1.040)
  starting transfers between devices: 59.4 us -> 93.8 us
    ppermute x43, starting transfers between devices: 24.2 us -> 47.5 us  [swap_axis(): return lax.ppermute(x, axis, [(i, i ^ step) for i in range(size)])]
    ppermute x3, starting transfers between devices: 2.46 us -> 14.2 us  [swap_across(): return lax.ppermute(x, ('mid', 'grp'), [(0, 3), (1, 2), (2, 1), (3, 0)])]
  transfers between devices with their start and end apart: 56 -> 56, of which waited for: 10 -> 10; matrix products, arithmetic and copies ran while one was open for 7% -> 6% of each run, Pallas kernels for 74% -> 71%
where the time goes in v6:
time: 849 us; the launch traced here: 843 us
  Pallas kernels  636 us (75%)
  starting transfers between devices  93.8 us (11%)
  waiting for transfers between devices  45 us (5%)
  local copies, waits for them, and re-layouts  40.1 us (5%)
  other arithmetic  25.5 us (3%)
    pallas_call x22, Pallas kernels, call(): pl.pallas_call(kernel, grid_spec=pltpu.PrefetchScalarGridSpec(num_scalar_...  388 us
    pallas_call x3, Pallas kernels, attend_back(): pl.pallas_call(functools.partial(attend_back_kernel, nb=nb, np_=np_, rem=...  158 us
    pallas_call x3, Pallas kernels, attend(): pl.pallas_call(functools.partial(attend_kernel, nb=nb, np_=np_, rem=rem),...  89.2 us
    ppermute x43, starting transfers between devices, swap_axis(): return lax.ppermute(x, axis, [(i, i ^ step) for i in range(size)])  47.5 us
    ppermute x43, waiting for transfers between devices, swap_axis(): return lax.ppermute(x, axis, [(i, i ^ step) for i in range(size)])  40.3 us
    ppermute x10, starting transfers between devices, swap_owner(): return lax.ppermute(x, AXES, pairs)  32.1 us
  transfers between devices with their start and end apart: 56, of which 10 were waited for; matrix products, arithmetic and copies ran while one was open for 6% of the time, Pallas kernels for 71%

profile of v6, /device:TPU:9, one launch (start us, length us, event | category | flops | bytes accessed | tf_op | source)
XLA Modules:
  0.0 843.3 jit_solution(277420600367826024)
XLA Ops:
  10.0 10.3 %collective-permute-done.2.p0.m0.o0 = bf16[128,3072]{1,0:T(8,128)(2,1)S(1)} collective-permute-done((bf16[128,3072]{1,0:T(8,128)(2,1)S(1)}, bf16[128,3072]{1,0:T(8,128)(2,1)S(1)}, u32[]{:S(2)}, u32[]{:S(2)}) %collective-permute-start.2) | collective-permute-done | bytes 786464 | tf_op jit(solution)/shard_map/ppermute | solution.py:1039
  70.4 29.6 %shard_map.171 = (bf16[784,512]{1,0:T(8,128)(2,1)}, bf16[784,512]{1,0:T(8,128)(2,1)}, f32[784,512]{1,0:T(8,128)}, f32[784,512]{1,0:T(8,128)}, bf16[12,2,1568,512...) custom-call(bf16[784,1536]{1,0:T(8,128)(2,1)} %shard_map.170.own, bf16[784,1536]{1,0:T(8,128)(2,1)} %copy-done.5), custom_call_target="tpu_custom_call" | custom-call | tf_op jit(solution)/shard_map/pallas_call | solution.py:151
  104.8 9.1 %shard_map.172 = (bf16[784,1024]{1,0:T(8,128)(2,1)}, bf16[784,1024]{1,0:T(8,128)(2,1)}, bf16[784,1536]{1,0:T(8,128)(2,1)}) custom-call(s32[6]{0:T(128)} %stack.73.ids, bf16[3,784,1024]{2,1,0:T(8,128)(2,1)} %mine.5, bf16[2,784,1024]{2,1,0:T(8,128)(2,1)} %collective-permute-done.13.got, f32[1,1024]{1,0:T(1,128)} %bitcast.160, f32[1,1024]{1,0:T(1,128)} %bitcast.163, ...), custom_call_target="tpu_custom_call" | custom-call | tf_op jit(solution)/shard_map/pallas_call | solution.py:533
  125.4 29.8 %shard_map.174 = (bf16[784,512]{1,0:T(8,128)(2,1)}, bf16[784,512]{1,0:T(8,128)(2,1)}, f32[784,512]{1,0:T(8,128)}, f32[784,512]{1,0:T(8,128)}, bf16[12,2,1568,512...) custom-call(bf16[784,1536]{1,0:T(8,128)(2,1)} %shard_map.173.own, bf16[784,1536]{1,0:T(8,128)(2,1)} %copy-done.6), custom_call_target="tpu_custom_call" | custom-call | tf_op jit(solution)/shard_map/pallas_call | solution.py:151
  155.2 9.5 %shard_map.175 = (bf16[784,1024]{1,0:T(8,128)(2,1)}, bf16[784,1024]{1,0:T(8,128)(2,1)}, bf16[784,1536]{1,0:T(8,128)(2,1)}) custom-call(s32[6]{0:T(128)} %stack.74.ids, bf16[3,784,1024]{2,1,0:T(8,128)(2,1)} %mine.5, bf16[2,784,1024]{2,1,0:T(8,128)(2,1)} %collective-permute-done.13.got, f32[1,1024]{1,0:T(1,128)} %bitcast.161, f32[1,1024]{1,0:T(1,128)} %bitcast.164, ...), custom_call_target="tpu_custom_call" | custom-call | tf_op jit(solution)/shard_map/pallas_call | solution.py:533
  178.2 29.8 %shard_map.177 = (bf16[784,512]{1,0:T(8,128)(2,1)}, bf16[784,512]{1,0:T(8,128)(2,1)}, f32[784,512]{1,0:T(8,128)}, f32[784,512]{1,0:T(8,128)}, bf16[12,2,1568,512...) custom-call(bf16[784,1536]{1,0:T(8,128)(2,1)} %shard_map.176.own, bf16[784,1536]{1,0:T(8,128)(2,1)} %copy-done.7), custom_call_target="tpu_custom_call" | custom-call | tf_op jit(solution)/shard_map/pallas_call | solution.py:151
  217.2 52.3 %shard_map.178 = (bf16[784,4096]{1,0:T(8,128)(2,1)}, bf16[784,4096]{1,0:T(8,128)(2,1)}, bf16[784,1024]{1,0:T(8,128)(2,1)}, bf16[784,1024]{1,0:T(8,128)(2,1)}, bf...) custom-call(s32[6]{0:T(128)} %stack.72.ids, ...), custom_call_target="tpu_custom_call" | custom-call | flops 49999998976 | tf_op jit(solution)/shard_map/pallas_call | solution.py:533
  272.2 52.5 %shard_map.179 = (bf16[784,4096]{1,0:T(8,128)(2,1)}, bf16[784,4096]{1,0:T(8,128)(2,1)}, bf16[784,1024]{1,0:T(8,128)(2,1)}, bf16[784,1024]{1,0:T(8,128)(2,1)}, bf...) custom-call(s32[6]{0:T(128)} %stack.73.ids, ...), custom_call_target="tpu_custom_call", output_to_operand_aliasing={{7}: (24, {})} | custom-call | flops 49999998976 | tf_op jit(solution)/shard_map/pallas_call | solution.py:533
  327.7 52.6 %shard_map.180 = (bf16[784,4096]{1,0:T(8,128)(2,1)}, bf16[784,4096]{1,0:T(8,128)(2,1)}, bf16[784,1024]{1,0:T(8,128)(2,1)}, bf16[784,1024]{1,0:T(8,128)(2,1)}, bf...) custom-call(s32[6]{0:T(128)} %stack.74.ids, ...), custom_call_target="tpu_custom_call", output_to_operand_aliasing={{7}: (24, {})} | custom-call | flops 49999998976 | tf_op jit(solution)/shard_map/pallas_call | solution.py:533
  380.3 18.3 %shard_map.183 = bf16[4,4,512,256]{3,2,1,0:T(8,128)(2,1)} custom-call(s32[6]{0:T(128)} %stack.72.ids, bf16[784,1024]{1,0:T(8,128)(2,1)} %get-tuple-element.200.refs_0_, bf16[784,1024]{1,0:T(8,128)(2,1)} %get-tuple-element.201.refs_1_, bf16[784,1024]{1,0:T(8,128)(2,1)} %get-tuple-element.202.refs_2_, bf16[784,4096]{1,0:T(8,128)(2,1)} %get-tuple-element.196.refs_3_, ...), custom_call_target="tpu_custom_call" | custom-call | flops 24999999488 | tf_op jit(solution)/shard_map/pallas_call | solution.py:533
  398.6 18.2 %shard_map.182 = bf16[4,4,512,256]{3,2,1,0:T(8,128)(2,1)} custom-call(s32[6]{0:T(128)} %stack.72.ids, bf16[784,4096]{1,0:T(8,128)(2,1)} %get-tuple-element.187.refs_0_, bf16[784,4096]{1,0:T(8,128)(2,1)} %get-tuple-element.188.refs_1_, bf16[784,4096]{1,0:T(8,128)(2,1)} %get-tuple-element.189.refs_2_, bf16[784,1024]{1,0:T(8,128)(2,1)} %get-tuple-element.190.refs_3_.refs_6_, ...), custom_call_target="tpu_custom_call" | custom-call | flops 24999999488 | tf_op jit(solution)/shard_map/pallas_call | solution.py:533
  430.6 22.0 %shard_map.184 = (bf16[4,1152,256]{2,1,0:T(8,128)(2,1)}, bf16[4,1152,256]{2,1,0:T(8,128)(2,1)}, bf16[4,1152,256]{2,1,0:T(8,128)(2,1)}, bf16[4,1152,256]{2,1,0:T(8,128)(2,1)}) custom-call(s32[6]{0:T(128)} %stack.72.ids, bf16[784,1024]{1,0:T(8,128)(2,1)} %get-tuple-element.200.refs_0_, bf16[784,1024]{1,0:T(8,128)(2,1)} %get-tuple-element.201.refs_1_, ...), custom_call_target="tpu_custom_call" | custom-call | flops 24999999488 | tf_op jit(solution)/shard_map/pallas_call | solution.py:533
  452.6 20.5 %shard_map.185 = (bf16[4,1152,256]{2,1,0:T(8,128)(2,1)}, bf16[4,1152,256]{2,1,0:T(8,128)(2,1)}, bf16[4,1152,256]{2,1,0:T(8,128)(2,1)}, bf16[4,1152,256]{2,1,0:T(8,128)(2,1)}) custom-call(s32[6]{0:T(128)} %stack.72.ids, bf16[784,4096]{1,0:T(8,128)(2,1)} %get-tuple-element.187.refs_0_, ...), custom_call_target="tpu_custom_call", output_to_operand_aliasing={{0}: (11, {}), {1}: (12, {}), {2}: (13, {}), {3}: (14, {})} | custom-call | flops 24999999488 | tf_op jit(solution)/shard_map/pallas_call | solution.py:533
  481.6 12.7 %collective-permute-start.30 = (bf16[4608,256]{1,0:T(8,128)(2,1)}, bf16[4608,256]{1,0:T(8,128)(2,1)}, u32[]{:S(2)}, u32[]{:S(2)}) collective-permute-start(bf16[4608,256]{1,0:T(8,128)(2,1)} %bitcast.194), channel_id=1, source_target_pairs={{0,5},{1,4},{4,1},{5,0},{2,7},{3,6},{6,3},{7,2},{8,13},{9,12},{12,... | collective-permute-start | bytes 7077896 | tf_op jit(solution)/shard_map/ppermute | solution.py:1043
  496.2 52.6 %shard_map.187 = (bf16[784,1536]{1,0:T(8,128)(2,1)}, bf16[784,1536]{1,0:T(8,128)(2,1)}) custom-call(bf16[784,1536]{1,0:T(8,128)(2,1)} %shard_map.170.own, bf16[784,1536]{1,0:T(8,128)(2,1)} %copy-done.5, bf16[784,512]{1,0:T(8,128)(2,1)} %get-tuple-element.215.do_o, bf16[3,784,512]{2,1,0:T(8,128)(2,1)} %collective-permute-done.29.do_r, ...), custom_call_target="tpu_custom_call" | custom-call | flops 49999998976 | tf_op jit(solution)/shard_map/pallas_call | solution.py:255
  549.1 52.8 %shard_map.188 = (bf16[784,1536]{1,0:T(8,128)(2,1)}, bf16[784,1536]{1,0:T(8,128)(2,1)}) custom-call(bf16[784,1536]{1,0:T(8,128)(2,1)} %shard_map.173.own, bf16[784,1536]{1,0:T(8,128)(2,1)} %copy-done.6, bf16[784,512]{1,0:T(8,128)(2,1)} %get-tuple-element.224.do_o, bf16[3,784,512]{2,1,0:T(8,128)(2,1)} %collective-permute-done.29.do_r, ...), custom_call_target="tpu_custom_call" | custom-call | flops 49999998976 | tf_op jit(solution)/shard_map/pallas_call | solution.py:255
  611.0 19.4 %collective-permute-start.36 = (bf16[1152,256]{1,0:T(8,128)(2,1)S(1)}, bf16[1152,256]{1,0:T(8,128)(2,1)}, u32[]{:S(2)}, u32[]{:S(2)}) collective-permute-start(bf16[1152,256]{1,0:T(8,128)(2,1)S(1)} %get-tuple-element.320), channel_id=1, source_target_pairs={{0,8},{8,0},{16,24},{24,16},{1,9},{9,1},{17,25},{25,17},{2,10},{10... | collective-permute-start | bytes 1769480 | tf_op jit(solution)/shard_map/ppermute | solution.py:1039
  633.1 52.7 %shard_map.190 = (bf16[784,1536]{1,0:T(8,128)(2,1)}, bf16[784,1536]{1,0:T(8,128)(2,1)}) custom-call(bf16[784,1536]{1,0:T(8,128)(2,1)} %shard_map.176.own, bf16[784,1536]{1,0:T(8,128)(2,1)} %copy-done.7, bf16[784,512]{1,0:T(8,128)(2,1)} %get-tuple-element.235.do_o, bf16[3,784,512]{2,1,0:T(8,128)(2,1)} %collective-permute-done.29.do_r, ...), custom_call_target="tpu_custom_call" | custom-call | flops 49999998976 | tf_op jit(solution)/shard_map/pallas_call | solution.py:255
  686.5 14.8 %shard_map.191 = (bf16[784,1024]{1,0:T(8,128)(2,1)}, f32[8,1024]{1,0:T(8,128)}, f32[8,1536]{1,0:T(8,128)}, f32[8,1536]{1,0:T(8,128)}) custom-call(s32[6]{0:T(128)} %stack.72.ids, bf16[784,1536]{1,0:T(8,128)(2,1)} %get-tuple-element.221.d_mine.refs_0_, bf16[784,1536]{1,0:T(8,128)(2,1)} %collective-permute-done.33.d_other.refs_3_, ...), custom_call_target="tpu_custom_call" | custom-call | flops 49999998976 | tf_op jit(solution)/shard_map/pallas_call | solution.py:533
  704.7 15.1 %shard_map.192 = bf16[4,4,384,256]{3,2,1,0:T(8,128)(2,1)} custom-call(s32[6]{0:T(128)} %stack.72.ids, bf16[784,1536]{1,0:T(8,128)(2,1)} %get-tuple-element.221.d_mine.refs_0_, bf16[784,1536]{1,0:T(8,128)(2,1)} %get-tuple-element.229.refs_1_.d_mine, bf16[784,1536]{1,0:T(8,128)(2,1)} %get-tuple-element.240.refs_2_.d_mine, ...), custom_call_target="tpu_custom_call" | custom-call | flops 24999999488 | tf_op jit(solution)/shard_map/pallas_call | solution.py:533
  719.8 14.3 %shard_map.193 = (bf16[784,1024]{1,0:T(8,128)(2,1)}, f32[8,1024]{1,0:T(8,128)}, f32[8,1536]{1,0:T(8,128)}, f32[8,1536]{1,0:T(8,128)}) custom-call(s32[6]{0:T(128)} %stack.73.ids, bf16[784,1536]{1,0:T(8,128)(2,1)} %get-tuple-element.229.refs_1_.d_mine, bf16[784,1536]{1,0:T(8,128)(2,1)} %collective-permute-done.34.refs_4_.d_other, ...), custom_call_target="tpu_custom_call" | custom-call | flops 49999998976 | tf_op jit(solution)/shard_map/pallas_call | solution.py:533
  736.6 16.8 %shard_map.194 = (bf16[4,384,256]{2,1,0:T(8,128)(2,1)}, bf16[4,384,256]{2,1,0:T(8,128)(2,1)}, bf16[4,384,256]{2,1,0:T(8,128)(2,1)}, bf16[4,384,256]{2,1,0:T(8,128)(2,1)}) custom-call(s32[6]{0:T(128)} %stack.72.ids, bf16[784,1536]{1,0:T(8,128)(2,1)} %get-tuple-element.221.d_mine.refs_0_, bf16[784,1536]{1,0:T(8,128)(2,1)} %get-tuple-element.229.refs_1_.d_mine, ...), custom_call_target="tpu_custom_call" | custom-call | flops 24999999488 | tf_op jit(solution)/shard_map/pallas_call | solution.py:533
  757.1 14.5 %shard_map.196 = (bf16[784,1024]{1,0:T(8,128)(2,1)}, f32[8,1024]{1,0:T(8,128)}, f32[8,1536]{1,0:T(8,128)}, f32[8,1536]{1,0:T(8,128)}) custom-call(s32[6]{0:T(128)} %stack.74.ids, bf16[784,1536]{1,0:T(8,128)(2,1)} %get-tuple-element.240.refs_2_.d_mine, bf16[784,1536]{1,0:T(8,128)(2,1)} %collective-permute-done.35.refs_5_.d_other, ...), custom_call_target="tpu_custom_call" | custom-call | flops 49999998976 | tf_op jit(solution)/shard_map/pallas_call | solution.py:533
  778.5 15.0 %collective-permute-done.47 = f32[12,1024]{1,0:T(8,128)S(1)} collective-permute-done((f32[12,1024]{1,0:T(8,128)S(1)}, f32[12,1024]{1,0:T(8,128)S(1)}, u32[]{:S(2)}, u32[]{:S(2)}) %collective-permute-start.47) | collective-permute-done | bytes 49184 | tf_op jit(solution)/shard_map/ppermute | solution.py:1039
  (283 shorter events, 204.7 us)
Async XLA Ops:
  5.9 44.3 %collective-permute-start.1 = (bf16[1,784,1024]{2,1,0:T(8,128)(2,1)}, bf16[1,784,1024]{2,1,0:T(8,128)(2,1)}, u32[]{:S(2)}, u32[]{:S(2)}) collective-permute-start(bf16[1,784,1024]{2,1,0:T(8,128)(2,1)} %slice.187), channel_id=1, source_target_pairs={{1,2},{2,1},{5,6},{6,5},{9,10},{10,9},{13,14},{14,13},{17,18},{18,... | collective-permute-start | bytes 4816904 | tf_op jit(solution)/shard_map/ppermute | solution.py:1050
  41.1 63.7 %collective-permute-start.13 = (bf16[2,784,1024]{2,1,0:T(8,128)(2,1)}, bf16[2,784,1024]{2,1,0:T(8,128)(2,1)}, u32[]{:S(2)}, u32[]{:S(2)}) collective-permute-start(bf16[2,784,1024]{2,1,0:T(8,128)(2,1)} %slice.188), channel_id=1, source_target_pairs={{1,2},{2,1},{5,6},{6,5},{9,10},{10,9},{13,14},{14,13},{17,18},{18,... | collective-permute-start | bytes 9633800 | tf_op jit(solution)/shard_map/ppermute | solution.py:1050
  61.1 43.7 %collective-permute-start.10 = (bf16[512,1024]{1,0:T(8,128)(2,1)}, bf16[512,1024]{1,0:T(8,128)(2,1)}, u32[]{:S(2)}, u32[]{:S(2)}) collective-permute-start(bf16[512,1024]{1,0:T(8,128)(2,1)} %constant_dynamic-slice_fusion.2), channel_id=1, source_target_pairs={{0,1},{1,0},{2,3},{3,2},{4,5},{5,4},{6,7},{7,6},{8,9},{9,8},{10,11... | collective-permute-start | bytes 3145736 | tf_op jit(solution)/shard_map/ppermute | solution.py:1039
  165.6 42.4 %collective-permute-start.15 = (bf16[640,1024]{1,0:T(8,128)(2,1)}, bf16[640,1024]{1,0:T(8,128)(2,1)}, u32[]{:S(2)}, u32[]{:S(2)}) collective-permute-start(bf16[640,1024]{1,0:T(8,128)(2,1)} %collective-permute-done.12.o0.u0), channel_id=1, source_target_pairs={{0,4},{4,0},{1,5},{5,1},{2,6},{6,2},{3,7},{7,3},{8,12},{12,8},{9,1... | collective-permute-start | bytes 3932168 | tf_op jit(solution)/shard_map/ppermute | solution.py:1039
  166.9 42.2 %collective-permute-start.9 = (bf16[1,784,1024]{2,1,0:T(8,128)(2,1)S(1)}, bf16[1,784,1024]{2,1,0:T(8,128)(2,1)}, u32[]{:S(2)}, u32[]{:S(2)}) collective-permute-start(bf16[1,784,1024]{2,1,0:T(8,128)(2,1)S(1)} %copy-done.15), channel_id=1, source_target_pairs={{1,2},{2,1},{5,6},{6,5},{9,10},{10,9},{13,14},{14,13},{17,18},{18,... | collective-permute-start | bytes 4816904 | tf_op jit(solution)/shard_map/ppermute | solution.py:1050
  169.6 47.5 %collective-permute-start.17 = (bf16[640,1024]{1,0:T(8,128)(2,1)}, bf16[640,1024]{1,0:T(8,128)(2,1)}, u32[]{:S(2)}, u32[]{:S(2)}) collective-permute-start(bf16[640,1024]{1,0:T(8,128)(2,1)} %collective-permute-done.12.o0.u0), channel_id=1, source_target_pairs={{0,2},{2,0},{1,3},{3,1},{4,6},{6,4},{5,7},{7,5},{8,10},{10,8},{9,1... | collective-permute-start | bytes 3932168 | tf_op jit(solution)/shard_map/ppermute | solution.py:1039
  213.7 58.5 %collective-permute-start.22 = (bf16[784,512]{1,0:T(8,128)(2,1)}, bf16[784,512]{1,0:T(8,128)(2,1)}, u32[]{:S(2)}, u32[]{:S(2)}) collective-permute-start(bf16[784,512]{1,0:T(8,128)(2,1)} %get-tuple-element.178.o_r), channel_id=1, source_target_pairs={{0,2},{2,0},{1,3},{3,1},{4,6},{6,4},{5,7},{7,5},{8,10},{10,8},{9,1... | collective-permute-start | bytes 2408456 | tf_op jit(solution)/shard_map/ppermute | solution.py:1039
  214.2 58.0 %collective-permute-start.23 = (bf16[2,784,1024]{2,1,0:T(8,128)(2,1)}, bf16[2,784,1024]{2,1,0:T(8,128)(2,1)}, u32[]{:S(2)}, u32[]{:S(2)}) collective-permute-start(bf16[2,784,1024]{2,1,0:T(8,128)(2,1)} %slice.190), channel_id=1, source_target_pairs={{1,2},{2,1},{5,6},{6,5},{9,10},{10,9},{13,14},{14,13},{17,18},{18,... | collective-permute-start | bytes 9633800 | tf_op jit(solution)/shard_map/ppermute | solution.py:1050
  217.0 110.6 %collective-permute-start.24 = (bf16[784,512]{1,0:T(8,128)(2,1)}, bf16[784,512]{1,0:T(8,128)(2,1)}, u32[]{:S(2)}, u32[]{:S(2)}) collective-permute-start(bf16[784,512]{1,0:T(8,128)(2,1)} %get-tuple-element.183.o_r), channel_id=1, source_target_pairs={{0,2},{2,0},{1,3},{3,1},{4,6},{6,4},{5,7},{7,5},{8,10},{10,8},{9,1... | collective-permute-start | bytes 2408456 | tf_op jit(solution)/shard_map/ppermute | solution.py:1039
  269.5 55.3 %collective-permute-start.21 = (bf16[784,1024]{1,0:T(8,128)(2,1)}, bf16[784,1024]{1,0:T(8,128)(2,1)S(1)}, u32[]{:S(2)}, u32[]{:S(2)}) collective-permute-start(bf16[784,1024]{1,0:T(8,128)(2,1)} %get-tuple-element.174), channel_id=1, source_target_pairs={{1,2},{2,1},{5,6},{6,5},{9,10},{10,9},{13,14},{14,13},{17,18},{18,... | collective-permute-start | bytes 4816904 | tf_op jit(solution)/shard_map/ppermute | solution.py:1050
  324.8 55.5 %collective-permute-start.27 = (bf16[784,1024]{1,0:T(8,128)(2,1)}, bf16[784,1024]{1,0:T(8,128)(2,1)}, u32[]{:S(2)}, u32[]{:S(2)}) collective-permute-start(bf16[784,1024]{1,0:T(8,128)(2,1)} %get-tuple-element.199), channel_id=1, source_target_pairs={{1,2},{2,1},{5,6},{6,5},{9,10},{10,9},{13,14},{14,13},{17,18},{18,... | collective-permute-start | bytes 4816904 | tf_op jit(solution)/shard_map/ppermute | solution.py:1050
  425.1 48.0 %collective-permute-start.25 = (bf16[4,4,128,256]{3,2,1,0:T(8,128)(2,1)}, bf16[4,4,128,256]{3,2,1,0:T(8,128)(2,1)}, u32[]{:S(2)}, u32[]{:S(2)}) collective-permute-start(bf16[4,4,128,256]{3,2,1,0:T(8,128)(2,1)} %shard_map.181), channel_id=1, source_target_pairs={{0,2},{2,0},{1,3},{3,1},{4,6},{6,4},{5,7},{7,5},{8,10},{10,8},{9,1... | collective-permute-start | bytes 3145736 | tf_op jit(solution)/shard_map/ppermute | solution.py:1039
  425.1 71.1 %collective-permute-start.29 = (bf16[3,784,512]{2,1,0:T(8,128)(2,1)S(1)}, bf16[3,784,512]{2,1,0:T(8,128)(2,1)}, u32[]{:S(2)}, u32[]{:S(2)}) collective-permute-start(bf16[3,784,512]{2,1,0:T(8,128)(2,1)S(1)} %copy-done.30), channel_id=1, source_target_pairs={{0,2},{2,0},{1,3},{3,1},{4,6},{6,4},{5,7},{7,5},{8,10},{10,8},{9,1... | collective-permute-start | bytes 7225352 | tf_op jit(solution)/shard_map/ppermute | solution.py:1039
  425.6 260.2 %collective-permute-start.39 = (bf16[784,1024]{1,0:T(8,128)(2,1)}, bf16[784,1024]{1,0:T(8,128)(2,1)}, u32[]{:S(2)}, u32[]{:S(2)}) collective-permute-start(bf16[784,1024]{1,0:T(8,128)(2,1)} %get-tuple-element.244), channel_id=1, source_target_pairs={{1,2},{2,1},{5,6},{6,5},{9,10},{10,9},{13,14},{14,13},{17,18},{18,... | collective-permute-start | bytes 4816904 | tf_op jit(solution)/shard_map/ppermute | solution.py:1050
  481.6 67.5 %collective-permute-start.30 = (bf16[4608,256]{1,0:T(8,128)(2,1)}, bf16[4608,256]{1,0:T(8,128)(2,1)}, u32[]{:S(2)}, u32[]{:S(2)}) collective-permute-start(bf16[4608,256]{1,0:T(8,128)(2,1)} %bitcast.194), channel_id=1, source_target_pairs={{0,5},{1,4},{4,1},{5,0},{2,7},{3,6},{6,3},{7,2},{8,13},{9,12},{12,... | collective-permute-start | bytes 7077896 | tf_op jit(solution)/shard_map/ppermute | solution.py:1043
  494.3 107.6 %collective-permute-start.31 = (bf16[4608,256]{1,0:T(8,128)(2,1)}, bf16[4608,256]{1,0:T(8,128)(2,1)}, u32[]{:S(2)}, u32[]{:S(2)}) collective-permute-start(bf16[4608,256]{1,0:T(8,128)(2,1)} %bitcast.192), channel_id=1, source_target_pairs={{0,4},{4,0},{1,5},{5,1},{2,6},{6,2},{3,7},{7,3},{8,12},{12,8},{9,1... | collective-permute-start | bytes 7077896 | tf_op jit(solution)/shard_map/ppermute | solution.py:1039
  495.1 106.9 %collective-permute-start.32 = (bf16[4608,256]{1,0:T(8,128)(2,1)}, bf16[4608,256]{1,0:T(8,128)(2,1)}, u32[]{:S(2)}, u32[]{:S(2)}) collective-permute-start(bf16[4608,256]{1,0:T(8,128)(2,1)} %bitcast.193), channel_id=1, source_target_pairs={{0,1},{1,0},{2,3},{3,2},{4,5},{5,4},{6,7},{7,6},{8,9},{9,8},{10,11... | collective-permute-start | bytes 7077896 | tf_op jit(solution)/shard_map/ppermute | solution.py:1039
  548.8 137.6 %collective-permute-start.33 = (bf16[784,1536]{1,0:T(8,128)(2,1)}, bf16[784,1536]{1,0:T(8,128)(2,1)}, u32[]{:S(2)}, u32[]{:S(2)}) collective-permute-start(bf16[784,1536]{1,0:T(8,128)(2,1)} %get-tuple-element.241), channel_id=1, source_target_pairs={{0,2},{2,0},{1,3},{3,1},{4,6},{6,4},{5,7},{7,5},{8,10},{10,8},{9,1... | collective-permute-start | bytes 7225352 | tf_op jit(solution)/shard_map/ppermute | solution.py:1039
  611.0 75.5 %collective-permute-start.36 = (bf16[1152,256]{1,0:T(8,128)(2,1)S(1)}, bf16[1152,256]{1,0:T(8,128)(2,1)}, u32[]{:S(2)}, u32[]{:S(2)}) collective-permute-start(bf16[1152,256]{1,0:T(8,128)(2,1)S(1)} %get-tuple-element.320), channel_id=1, source_target_pairs={{0,8},{8,0},{16,24},{24,16},{1,9},{9,1},{17,25},{25,17},{2,10},{10... | collective-permute-start | bytes 1769480 | tf_op jit(solution)/shard_map/ppermute | solution.py:1039
  630.4 56.1 %collective-permute-start.37 = (bf16[1152,256]{1,0:T(8,128)(2,1)S(1)}, bf16[1152,256]{1,0:T(8,128)(2,1)}, u32[]{:S(2)}, u32[]{:S(2)}) collective-permute-start(bf16[1152,256]{1,0:T(8,128)(2,1)S(1)} %get-tuple-element.319), channel_id=1, source_target_pairs={{0,16},{8,24},{16,0},{24,8},{1,17},{9,25},{17,1},{25,9},{2,18},{10... | collective-permute-start | bytes 1769480 | tf_op jit(solution)/shard_map/ppermute | solution.py:1039
  632.8 53.7 %collective-permute-start.38 = (bf16[1152,256]{1,0:T(8,128)(2,1)S(1)}, bf16[1152,256]{1,0:T(8,128)(2,1)}, u32[]{:S(2)}, u32[]{:S(2)}) collective-permute-start(bf16[1152,256]{1,0:T(8,128)(2,1)S(1)} %get-tuple-element.318), channel_id=1, source_target_pairs={{0,24},{8,16},{16,8},{24,0},{1,25},{9,17},{17,9},{25,1},{2,26},{10... | collective-permute-start | bytes 1769480 | tf_op jit(solution)/shard_map/ppermute | solution.py:1039
  753.4 47.2 %collective-permute-start.42 = (bf16[1536,256]{1,0:T(8,128)(2,1)}, bf16[1536,256]{1,0:T(8,128)(2,1)}, u32[]{:S(2)}, u32[]{:S(2)}) collective-permute-start(bf16[1536,256]{1,0:T(8,128)(2,1)} %bitcast.197), channel_id=1, source_target_pairs={{0,4},{4,0},{1,5},{5,1},{2,6},{6,2},{3,7},{7,3},{8,12},{12,8},{9,1... | collective-permute-start | bytes 2359304 | tf_op jit(solution)/shard_map/ppermute | solution.py:1039
  754.9 45.8 %collective-permute-start.43 = (bf16[1536,256]{1,0:T(8,128)(2,1)}, bf16[1536,256]{1,0:T(8,128)(2,1)}, u32[]{:S(2)}, u32[]{:S(2)}) collective-permute-start(bf16[1536,256]{1,0:T(8,128)(2,1)} %bitcast.196), channel_id=1, source_target_pairs={{0,1},{1,0},{2,3},{3,2},{4,5},{5,4},{6,7},{7,6},{8,9},{9,8},{10,11... | collective-permute-start | bytes 2359304 | tf_op jit(solution)/shard_map/ppermute | solution.py:1039
  754.9 45.8 %collective-permute-start.44 = (bf16[1536,256]{1,0:T(8,128)(2,1)}, bf16[1536,256]{1,0:T(8,128)(2,1)}, u32[]{:S(2)}, u32[]{:S(2)}) collective-permute-start(bf16[1536,256]{1,0:T(8,128)(2,1)} %bitcast.195), channel_id=1, source_target_pairs={{0,5},{1,4},{4,1},{5,0},{2,7},{3,6},{6,3},{7,2},{8,13},{9,12},{12,... | collective-permute-start | bytes 2359304 | tf_op jit(solution)/shard_map/ppermute | solution.py:1043
  (67 other events, 918.9 us)
